TPU v7x, 32 devices: a whole 2x2x4 slice. The times are simulated.
32 devices in a mesh: head: 4 (over x, core), seq: 8 (over z, y).
Axes of the slice: x: 2, y: 2, z: 4, core: 2. Of those that a mesh axis runs over, the one named last changes fastest.
Arguments:
- tokens: bfloat16 [8192, 1536], P(('seq', 'head')), may hold values from -6 to 6
- cotangent: bfloat16 [8192, 1536], P(('seq', 'head')), may hold values from -6 to 6
- attn_gain: float32 [1536], P(('head', 'seq')), may hold values from 0.5 to 1.5
- ffn_gain: float32 [1536], P(('head', 'seq')), may hold values from 0.5 to 1.5
- qkv_stack: float32 [256, 96, 112], P(('head', 'seq')), may hold values from -0.15625 to 0.15625
- out_stack: float32 [256, 96, 96], P(('head', 'seq')), may hold values from -1.25 to 1.25
- gateup_stack: float32 [1536, 96, 96], P(('head', 'seq')), may hold values from -0.15625 to 0.15625
- down_stack: float32 [768, 96, 96], P(('head', 'seq')), may hold values from -0.09375 to 0.09375
- qkv_left: float32 [256, 96, 96], P(('head', 'seq')), as said below
- qkv_right: float32 [256, 112, 112], P(('head', 'seq')), as said below
- out_left: float32 [256, 96, 96], P(('head', 'seq')), as said below
- out_right: float32 [256, 96, 96], P(('head', 'seq')), as said below
- gateup_left: float32 [1536, 96, 96], P(('head', 'seq')), as said below
- gateup_right: float32 [1536, 96, 96], P(('head', 'seq')), as said below
- down_left: float32 [768, 96, 96], P(('head', 'seq')), as said below
- down_right: float32 [768, 96, 96], P(('head', 'seq')), as said below
- qkv_left_root: float32 [256, 96, 96], P(('head', 'seq')), as said below
- qkv_right_root: float32 [256, 112, 112], P(('head', 'seq')), as said below
- out_left_root: float32 [256, 96, 96], P(('head', 'seq')), as said below
- out_right_root: float32 [256, 96, 96], P(('head', 'seq')), as said below
- gateup_left_root: float32 [1536, 96, 96], P(('head', 'seq')), as said below
- gateup_right_root: float32 [1536, 96, 96], P(('head', 'seq')), as said below
- down_left_root: float32 [768, 96, 96], P(('head', 'seq')), as said below
- down_right_root: float32 [768, 96, 96], P(('head', 'seq')), as said below
- sequence_ids: int32 [8192], replicated, may hold values from 0 to 2, as said below
- token_order: int32 [8192], P('seq'), may hold values from 0 to 1023, as said below
Outputs:
- block_out: bfloat16 [8192, 1536], P(('seq', 'head'))
- input_grad: float32 [8192, 1536], P(('seq', 'head'))
- attn_gain_grad: float32 [1536], P(('head', 'seq'))
- ffn_gain_grad: float32 [1536], P(('head', 'seq'))
- qkv_left_new: float32 [256, 96, 96], P(('head', 'seq'))
- qkv_right_new: float32 [256, 112, 112], P(('head', 'seq'))
- qkv_weight_new: float32 [256, 96, 112], P(('head', 'seq'))
- out_left_new: float32 [256, 96, 96], P(('head', 'seq'))
- out_right_new: float32 [256, 96, 96], P(('head', 'seq'))
- out_weight_new: float32 [256, 96, 96], P(('head', 'seq'))
- gateup_left_new: float32 [1536, 96, 96], P(('head', 'seq'))
- gateup_right_new: float32 [1536, 96, 96], P(('head', 'seq'))
- gateup_weight_new: float32 [1536, 96, 96], P(('head', 'seq'))
- down_left_new: float32 [768, 96, 96], P(('head', 'seq'))
- down_right_new: float32 [768, 96, 96], P(('head', 'seq'))
- down_weight_new: float32 [768, 96, 96], P(('head', 'seq'))
Inputs may be any that keep to these rules, and one draw needn't show every extreme that they name: `token_order`: each aligned block of 1024 entries is a permutation of 0 to 1023. `sequence_ids`: never falls along the stream, starts at 0 and rises by one at each change; a value's run is at most 4096 positions long, one run exactly that long; apart from the first, no run begins at a multiple of 1024. `qkv_left`: symmetric blocks. `qkv_right`: symmetric blocks. `out_left`: symmetric blocks. `out_right`: symmetric blocks. `gateup_left`: symmetric blocks. `gateup_right`: symmetric blocks. `down_left`: symmetric blocks. `down_right`: symmetric blocks. `qkv_left_root`: symmetric blocks. `qkv_right_root`: symmetric blocks. `out_left_root`: symmetric blocks. `out_right_root`: symmetric blocks. `gateup_left_root`: symmetric blocks. `gateup_right_root`: symmetric blocks. `down_left_root`: symmetric blocks. `down_right_root`: symmetric blocks.
All inputs are finite; a program needn't handle non-finite values.
Results may differ from a plain program's by a relative error of at most 0.017.
Values may be sent and summed in bfloat16 or wider, within the bound.
A program may use at most 256 MiB of HBM per device.

v0:
```python
import jax
import jax.numpy as jnp
from jax import lax
from jax.sharding import PartitionSpec as P

D = 1536
HEAD_DIM = 128
FF = 4608
WINDOW = 1024
GRID = 16
QW = 1536
QKV = 1792
BLK = 96
BQ = 112
BH = 96
NU = 48


norm_eps = 1e-06
stat_eps = 1e-06
neg_fill = -1e30


def passed_along(block, axis, distance):
    devices = range(lax.axis_size(axis))
    route = [(i - distance, i) for i in devices if i - distance in devices]
    return lax.ppermute(block, axis, route)


def shortened(value):
    return jax.tree.map(lambda a: a.astype(jnp.bfloat16) if a.dtype == jnp.float32 else a, value)


def rms_norm(values, gain):
    return values * lax.rsqrt(jnp.mean(values * values, axis=-1, keepdims=True) + norm_eps) * gain


def gelu_product(gate, upper):
    return jax.nn.gelu(gate, approximate=True) * upper


def precondition(weight, grad, left, right, left_root, right_root, rate):
    highest = lax.Precision.HIGHEST
    mean_square = jnp.mean(grad * grad, axis=(1, 2), keepdims=True) + stat_eps
    left_new = 0.5 * left + 0.5 * jnp.einsum("bij,bkj->bik", grad, grad, precision=highest) / (
        grad.shape[2] * mean_square
    )
    right_new = 0.5 * right + 0.5 * jnp.einsum("bji,bjk->bik", grad, grad, precision=highest) / (
        grad.shape[1] * mean_square
    )
    step = jnp.einsum("bij,bjk->bik", left_root, grad, precision=highest)
    step = jnp.einsum("bij,bjk->bik", step, right_root, precision=highest)
    return (left_new, right_new, weight - rate * step * lax.rsqrt(mean_square))


def fetch_weights(qkv_stack, out_stack, attn_gain, ffn_gain, gateup_stack, down_stack, unit_blocks):
    qkv_low, out_low, gain_first, gain_second = (
        lax.all_gather(qkv_stack.astype(jnp.bfloat16), ("head", "seq"), axis=0, tiled=True),
        lax.all_gather(out_stack.astype(jnp.bfloat16), ("head", "seq"), axis=0, tiled=True),
        lax.all_gather(attn_gain.astype(jnp.bfloat16), ("head", "seq"), axis=0, tiled=True),
        lax.all_gather(ffn_gain.astype(jnp.bfloat16), ("head", "seq"), axis=0, tiled=True),
    )
    gateup_low, down_low = (
        lax.all_gather(gateup_stack.astype(jnp.bfloat16), "seq", axis=0, tiled=True),
        lax.all_gather(down_stack.astype(jnp.bfloat16), "seq", axis=0, tiled=True),
    )
    return (
        qkv_low.reshape(GRID, GRID, BLK, BQ),
        out_low.reshape(GRID, GRID, BH, BLK),
        gain_first.astype(jnp.float32),
        gain_second.astype(jnp.float32),
        gateup_low.reshape(unit_blocks, 2, GRID, BLK, BLK),
        down_low.reshape(unit_blocks, GRID, BLK, BLK),
    )


def on_device(
    tokens,
    cotangent,
    attn_gain,
    ffn_gain,
    qkv_stack,
    out_stack,
    gateup_stack,
    down_stack,
    qkv_left,
    qkv_right,
    out_left,
    out_right,
    gateup_left,
    gateup_right,
    down_left,
    down_right,
    qkv_left_root,
    qkv_right_root,
    out_left_root,
    out_right_root,
    gateup_left_root,
    gateup_right_root,
    down_left_root,
    down_right_root,
    sequence_ids,
    token_order,
):
    row_count = tokens.shape[0]
    head_count = lax.axis_size("head")
    group = row_count * head_count
    unit_blocks = NU // head_count
    seq_index = lax.axis_index("seq")
    scale = HEAD_DIM ** (-0.5)
    query_block = min(512, group)
    key_span = WINDOW + query_block
    starts = jnp.arange(group // query_block, dtype=jnp.int32) * query_block
    qkv_grid, out_grid, gain_one, gain_two, gateup_grid, down_grid = fetch_weights(
        qkv_stack, out_stack, attn_gain, ffn_gain, gateup_stack, down_stack, unit_blocks
    )
    tokens_float = tokens.astype(jnp.float32)
    normed_one, norm_one_pull = jax.vjp(rms_norm, tokens_float, gain_one)
    normed_one_low = normed_one.astype(jnp.bfloat16)
    normed_one_grid = normed_one_low.reshape(row_count, GRID, BLK)
    projected = jnp.einsum(
        "tri,rcij->tcj", normed_one_grid, qkv_grid, preferred_element_type=jnp.float32
    )
    projected_low = projected.reshape(row_count, QKV).astype(jnp.bfloat16)
    kv_tiled = jnp.tile(projected_low[:, QW:], (1, head_count))
    query_group, kv_group = (
        lax.all_to_all(projected_low[:, :QW], "head", split_axis=1, concat_axis=0, tiled=True),
        lax.all_to_all(kv_tiled, "head", split_axis=1, concat_axis=0, tiled=True),
    )
    query_stream = jnp.take(query_group, token_order, axis=0)
    kv_stream = jnp.take(kv_group, token_order, axis=0)
    kv_before = passed_along(kv_stream, "seq", 1)
    kv_both = jnp.concatenate([kv_before, kv_stream], axis=0)
    ids_own = lax.dynamic_slice_in_dim(sequence_ids, seq_index * group, group, 0)
    ids_before = lax.dynamic_slice_in_dim(
        sequence_ids, jnp.maximum(seq_index - 1, 0) * group, group, 0
    )
    ids_before = jnp.where(seq_index > 0, ids_before, -1)
    key_ids = jnp.concatenate([ids_before, ids_own])
    local_heads = query_group.shape[1] // HEAD_DIM
    query_offsets = jnp.arange(query_block, dtype=jnp.int32)
    key_offsets = jnp.arange(key_span, dtype=jnp.int32)
    distance = query_offsets[:, None] + WINDOW - key_offsets[None, :]
    nearby = (distance >= 0) & (distance < WINDOW)

    def block_keys(start):
        key_start = start + group - WINDOW
        kv_rows = lax.dynamic_slice_in_dim(kv_both, key_start, key_span, 0)
        query_ids = lax.dynamic_slice_in_dim(ids_own, start, query_block, 0)
        span_ids = lax.dynamic_slice_in_dim(key_ids, key_start, key_span, 0)
        allowed = nearby & (query_ids[:, None] == span_ids[None, :])
        return (key_start, kv_rows[:, :HEAD_DIM], kv_rows[:, HEAD_DIM:], allowed)

    def head_scores(query_head, keys_rows, allowed):
        scores = (
            jnp.einsum("qd,kd->qk", query_head, keys_rows, preferred_element_type=jnp.float32)
            * scale
        )
        return jnp.where(allowed, scores, neg_fill)

    def attention_block(start):
        key_start, keys_rows, values_rows, allowed = block_keys(start)
        query_rows = lax.dynamic_slice_in_dim(query_stream, start, query_block, 0)
        mixed_parts = []
        lse_parts = []
        for head in range(local_heads):
            scores = head_scores(
                query_rows[:, head * HEAD_DIM : (head + 1) * HEAD_DIM], keys_rows, allowed
            )
            top = jnp.max(scores, axis=-1, keepdims=True)
            expo = jnp.exp(scores - top)
            total = jnp.sum(expo, axis=-1, keepdims=True)
            probs_low = (expo / total).astype(jnp.bfloat16)
            mixed_parts.append(
                jnp.dot(probs_low, values_rows, preferred_element_type=jnp.float32).astype(
                    jnp.bfloat16
                )
            )
            lse_parts.append(top[:, 0] + jnp.log(total[:, 0]))
        return (jnp.concatenate(mixed_parts, axis=1), jnp.stack(lse_parts, axis=1))

    mixed_blocks, lse_blocks = lax.map(attention_block, starts)
    mixed_stream = mixed_blocks.reshape(group, local_heads * HEAD_DIM)
    lse_stream = lse_blocks.reshape(group, local_heads)
    inverse = jnp.zeros((group,), jnp.int32).at[token_order].set(jnp.arange(group, dtype=jnp.int32))
    attended = lax.all_to_all(
        shortened(jnp.take(mixed_stream, inverse, axis=0)),
        "head",
        split_axis=0,
        concat_axis=1,
        tiled=True,
    )
    attended_grid = attended.reshape(row_count, GRID, BH)
    attn_proj = jnp.einsum(
        "tri,rcij->tcj", attended_grid, out_grid, preferred_element_type=jnp.float32
    ).reshape(row_count, D)
    resid = tokens_float + attn_proj
    normed_two, norm_two_pull = jax.vjp(rms_norm, resid, gain_two)
    normed_group, grad_group = (
        lax.all_gather(normed_two.astype(jnp.bfloat16), "head", axis=0, tiled=True),
        lax.all_gather(cotangent, "head", axis=0, tiled=True),
    )
    rows_here = normed_group.shape[0]
    normed_grid = normed_group.reshape(rows_here, GRID, BLK)
    gate_up = jnp.einsum(
        "tri,ukrij->tukj", normed_grid, gateup_grid, preferred_element_type=jnp.float32
    )
    hidden, act_pull = jax.vjp(gelu_product, gate_up[:, :, 0], gate_up[:, :, 1])
    hidden_low = hidden.astype(jnp.bfloat16)
    down_part = jnp.einsum(
        "tui,ucij->tcj", hidden_low, down_grid, preferred_element_type=jnp.float32
    ).reshape(rows_here, D)
    ffn_out = lax.psum_scatter(
        down_part.astype(jnp.bfloat16), "head", scatter_dimension=0, tiled=True
    ).astype(jnp.float32)
    block_out = (resid + ffn_out).astype(jnp.bfloat16)
    qkv_grid, out_grid, gain_one, gain_two, gateup_grid, down_grid = fetch_weights(
        qkv_stack, out_stack, attn_gain, ffn_gain, gateup_stack, down_stack, unit_blocks
    )
    grad_grid = grad_group.reshape(rows_here, GRID, BLK)
    hidden_grad = jnp.einsum(
        "tcj,ucij->tui", grad_grid, down_grid, preferred_element_type=jnp.float32
    )
    gate_grad, up_grad = act_pull(hidden_grad)
    gate_up_grad = jnp.stack([gate_grad, up_grad], axis=2).astype(jnp.bfloat16)
    down_wgrad = jnp.einsum(
        "tui,tcj->ucij", hidden_low, grad_grid, preferred_element_type=jnp.float32
    ).reshape(unit_blocks * GRID, BLK, BLK)
    gateup_wgrad = jnp.einsum(
        "tri,tukj->ukrij", normed_grid, gate_up_grad, preferred_element_type=jnp.float32
    ).reshape(unit_blocks * 2 * GRID, BLK, BLK)
    normed_part = jnp.einsum(
        "tukj,ukrij->tri", gate_up_grad, gateup_grid, preferred_element_type=jnp.float32
    ).reshape(rows_here, D)
    gateup_grad_own, down_grad_own = (
        lax.psum_scatter(gateup_wgrad, "seq", scatter_dimension=0, tiled=True),
        lax.psum_scatter(down_wgrad, "seq", scatter_dimension=0, tiled=True),
    )
    normed_two_grad = lax.psum_scatter(
        normed_part.astype(jnp.bfloat16), "head", scatter_dimension=0, tiled=True
    ).astype(jnp.float32)
    resid_part, gain_two_grad = norm_two_pull(normed_two_grad)
    resid_grad = cotangent.astype(jnp.float32) + resid_part
    proj_grid = resid_grad.astype(jnp.bfloat16).reshape(row_count, GRID, BLK)
    out_wgrad = jnp.einsum(
        "tri,tcj->rcij", attended_grid, proj_grid, preferred_element_type=jnp.float32
    ).reshape(GRID * GRID, BH, BLK)
    attended_grad = (
        jnp.einsum("tcj,rcij->tri", proj_grid, out_grid, preferred_element_type=jnp.float32)
        .reshape(row_count, QW)
        .astype(jnp.bfloat16)
    )
    mixed_grad_group = lax.all_to_all(
        attended_grad, "head", split_axis=1, concat_axis=0, tiled=True
    )
    mixed_grad_stream = jnp.take(mixed_grad_group, token_order, axis=0)

    def attention_back(carry, start):
        key_start, keys_rows, values_rows, allowed = block_keys(start)
        query_rows = lax.dynamic_slice_in_dim(query_stream, start, query_block, 0)
        grad_rows = lax.dynamic_slice_in_dim(mixed_grad_stream, start, query_block, 0)
        lse_rows = lax.dynamic_slice_in_dim(lse_stream, start, query_block, 0)
        key_total = jnp.zeros((key_span, HEAD_DIM), jnp.float32)
        value_total = jnp.zeros((key_span, HEAD_DIM), jnp.float32)
        query_parts = []
        for head in range(local_heads):
            query_head = query_rows[:, head * HEAD_DIM : (head + 1) * HEAD_DIM]
            grad_head = grad_rows[:, head * HEAD_DIM : (head + 1) * HEAD_DIM]
            probs = jnp.exp(
                head_scores(query_head, keys_rows, allowed) - lse_rows[:, head : head + 1]
            )
            prob_grad = jnp.einsum(
                "qd,kd->qk", grad_head, values_rows, preferred_element_type=jnp.float32
            )
            delta = jnp.sum(probs * prob_grad, axis=-1, keepdims=True)
            score_grad = (probs * (prob_grad - delta)).astype(jnp.bfloat16)
            query_parts.append(
                jnp.dot(score_grad, keys_rows, preferred_element_type=jnp.float32) * scale
            )
            key_total = (
                key_total
                + jnp.einsum(
                    "qk,qd->kd", score_grad, query_head, preferred_element_type=jnp.float32
                )
                * scale
            )
            value_total = value_total + jnp.einsum(
                "qk,qd->kd",
                probs.astype(jnp.bfloat16),
                grad_head,
                preferred_element_type=jnp.float32,
            )
        block_total = jnp.concatenate([key_total, value_total], axis=1)
        current = lax.dynamic_slice_in_dim(carry, key_start, key_span, 0)
        carry = lax.dynamic_update_slice_in_dim(carry, current + block_total, key_start, 0)
        return (carry, jnp.concatenate(query_parts, axis=1))

    kv_grad_both, query_blocks = lax.scan(
        attention_back, jnp.zeros((2 * group, 2 * HEAD_DIM), jnp.float32), starts
    )
    kv_grad_later = passed_along(kv_grad_both[:group].astype(jnp.bfloat16), "seq", -1).astype(
        jnp.float32
    )
    kv_grad_stream = kv_grad_both[group:] + kv_grad_later
    query_grad_stream = query_blocks.reshape(group, local_heads * HEAD_DIM).astype(jnp.bfloat16)
    query_grad = lax.all_to_all(
        jnp.take(query_grad_stream, inverse, axis=0),
        "head",
        split_axis=0,
        concat_axis=1,
        tiled=True,
    )
    kv_grad = lax.psum_scatter(
        jnp.take(kv_grad_stream, inverse, axis=0).astype(jnp.bfloat16),
        "head",
        scatter_dimension=0,
        tiled=True,
    )
    qkv_grad = jnp.concatenate([query_grad, kv_grad], axis=1)
    qkv_grad_grid = qkv_grad.reshape(row_count, GRID, BQ)
    qkv_wgrad = jnp.einsum(
        "tri,tcj->rcij", normed_one_grid, qkv_grad_grid, preferred_element_type=jnp.float32
    ).reshape(GRID * GRID, BLK, BQ)
    normed_one_grad = jnp.einsum(
        "tcj,rcij->tri", qkv_grad_grid, qkv_grid, preferred_element_type=jnp.float32
    ).reshape(row_count, D)
    tokens_part, gain_one_grad = norm_one_pull(normed_one_grad)
    input_grad = resid_grad + tokens_part
    qkv_grad_own, out_grad_own, attn_gain_grad, ffn_gain_grad = (
        lax.psum_scatter(qkv_wgrad, ("head", "seq"), scatter_dimension=0, tiled=True),
        lax.psum_scatter(out_wgrad, ("head", "seq"), scatter_dimension=0, tiled=True),
        lax.psum_scatter(gain_one_grad, ("head", "seq"), scatter_dimension=0, tiled=True),
        lax.psum_scatter(gain_two_grad, ("head", "seq"), scatter_dimension=0, tiled=True),
    )
    qkv_rate = 0.5 * D ** (-0.5)
    out_rate = 0.5 * (QW // 64) ** (-0.5)
    gateup_rate = 0.5 * D ** (-0.5)
    down_rate = 0.5 * FF ** (-0.5)
    qkv_new = precondition(
        qkv_stack, qkv_grad_own, qkv_left, qkv_right, qkv_left_root, qkv_right_root, qkv_rate
    )
    out_new = precondition(
        out_stack, out_grad_own, out_left, out_right, out_left_root, out_right_root, out_rate
    )
    gateup_new = precondition(
        gateup_stack,
        gateup_grad_own,
        gateup_left,
        gateup_right,
        gateup_left_root,
        gateup_right_root,
        gateup_rate,
    )
    down_new = precondition(
        down_stack, down_grad_own, down_left, down_right, down_left_root, down_right_root, down_rate
    )
    return (
        block_out,
        input_grad,
        attn_gain_grad,
        ffn_gain_grad,
        qkv_new[0],
        qkv_new[1],
        qkv_new[2],
        out_new[0],
        out_new[1],
        out_new[2],
        gateup_new[0],
        gateup_new[1],
        gateup_new[2],
        down_new[0],
        down_new[1],
        down_new[2],
    )


def solution(mesh):
    placed = (
        P(("seq", "head"), None),
        P(("seq", "head"), None),
        P(("head", "seq")),
        P(("head", "seq")),
        P(("head", "seq"), None, None),
        P(("head", "seq"), None, None),
        P(("head", "seq"), None, None),
        P(("head", "seq"), None, None),
        P(("head", "seq"), None, None),
        P(("head", "seq"), None, None),
        P(("head", "seq"), None, None),
        P(("head", "seq"), None, None),
        P(("head", "seq"), None, None),
        P(("head", "seq"), None, None),
        P(("head", "seq"), None, None),
        P(("head", "seq"), None, None),
        P(("head", "seq"), None, None),
        P(("head", "seq"), None, None),
        P(("head", "seq"), None, None),
        P(("head", "seq"), None, None),
        P(("head", "seq"), None, None),
        P(("head", "seq"), None, None),
        P(("head", "seq"), None, None),
        P(("head", "seq"), None, None),
        P(),
        P("seq"),
    )
    return jax.shard_map(
        on_device,
        mesh=mesh,
        in_specs=placed,
        out_specs=(
            P(("seq", "head"), None),
            P(("seq", "head"), None),
            P(("head", "seq")),
            P(("head", "seq")),
            P(("head", "seq"), None, None),
            P(("head", "seq"), None, None),
            P(("head", "seq"), None, None),
            P(("head", "seq"), None, None),
            P(("head", "seq"), None, None),
            P(("head", "seq"), None, None),
            P(("head", "seq"), None, None),
            P(("head", "seq"), None, None),
            P(("head", "seq"), None, None),
            P(("head", "seq"), None, None),
            P(("head", "seq"), None, None),
            P(("head", "seq"), None, None),
        ),
        check_vma=False,
    )
```

profile of v0, /device:TPU:0, one launch (start us, length us, event | category | flops | bytes accessed | tf_op | source)
XLA Modules:
  0.0 1614.6 jit_solution(9798757608393534103)
XLA Ops:
  15.3 42.6 %all-reduce.5 = (bf16[1536]{0:T(1024)(128)(2,1)S(1)}, bf16[1536]{0:T(1024)(128)(2,1)S(1)}) all-reduce(bf16[1536]{0:T(1024)(128)(2,1)S(1)} %dynamic-update-slice, bf16[1536]{0:T(1024)(128)(2,1)S(1)} %dynamic-update-slice.1), channel_id=1, replica_groups=mesh['head'=4,'seq'=8] {'head','seq'}, use_global_device_ids=true, to_apply=%add | all-reduce | flops 3072 | bytes 12288
  63.3 4.3 scatter_custom_fusion
  67.7 16.3 %all-gather.7.cloned.1.call-done = bf16[256,96,112]{2,1,0:T(8,128)(2,1)} async-done(((bf16[8,96,112]{2,1,0:T(8,128)(2,1)}), bf16[256,96,112]{2,1,0:T(8,128)(2,1)}) %all-gather.7.cloned.1.call-update) | async-done | bytes 5505040 | tf_op jit(solution)/shard_map/all_gather | solution.py:58
  83.9 8.0 copy.205
  92.0 11.9 dot_general.298
  103.8 4.2 fusion.118
  109.8 3.5 all-to-all-start.1
  115.4 9.5 all-to-all-done.1
  125.8 3.5 all-to-all-start
  129.9 5.7 gather_fusion
  137.6 4.3 collective-permute-start
  145.2 5.0 gather_fusion.2
  152.4 4.9 collective-permute-done
  158.6 44.7 %while.34 = (s32[]{:T(128)}, bf16[2,512,384]{2,1,0:T(8,128)(2,1)}, f32[2,512,3]{1,2,0:T(4,128)}, s32[2]{0:T(128)}, s32[1024]{0:T(1024)}, /*index=5*/s32[2048]{0:...) while((s32[]{:T(128)}, bf16[2,512,384]{2,1,0:T(8,128)(2,1)}, ...), condition=%wide.region_8.10_spmd.clone, body=%wide.region_1.9_spmd.clone.sunk | while | flops 1242367488 | bytes 33933628 | solution.py:182
  203.3 6.1 gather_fusion.3
  213.9 4.2 all-to-all-start.2
  218.5 8.1 copy.202
  226.6 11.2 dot_general.301
  237.8 4.3 multiply_reduce_fusion.4
  249.5 4.7 copy.117
  254.2 27.0 %all-gather.11.cloned.1.call-done = bf16[1024,1536]{1,0:T(8,128)(2,1)} async-done(((bf16[256,1536]{1,0:T(8,128)(2,1)}), bf16[1024,1536]{1,0:T(8,128)(2,1)}) %all-gather.11.cloned.1.call-update) | async-done | bytes 3145744 | tf_op jit(solution)/shard_map/all_gather | solution.py:200
  281.2 4.7 copy.114
  285.8 136.0 %all-gather.13.cloned.1.call-done = bf16[384,96,96]{2,1,0:T(8,128)(2,1)} async-done(((bf16[48,96,96]{2,1,0:T(8,128)(2,1)}), bf16[384,96,96]{2,1,0:T(8,128)(2,1)}) %all-gather.13.cloned.1.call-update) | async-done | bytes 7077904 | tf_op jit(solution)/shard_map/all_gather | solution.py:64
  421.9 13.3 convolution_bitcast_fusion.2
  435.1 67.5 %all-gather.15.cloned.1.call-done = bf16[192,96,96]{2,1,0:T(8,128)(2,1)} async-done(((bf16[24,96,96]{2,1,0:T(8,128)(2,1)}), bf16[192,96,96]{2,1,0:T(8,128)(2,1)}) %all-gather.15.cloned.1.call-update) | async-done | bytes 3538960 | tf_op jit(solution)/shard_map/all_gather | solution.py:65
  502.6 11.5 fusion.128
  516.3 11.9 bitcast_convert_fusion
  528.2 9.7 copy.121
  537.9 11.3 dot_general.312
  549.2 15.3 reduce-scatter.10.cloned.1.call-done
  572.4 4.0 fusion.119
  577.4 4.2 all-to-all-start.3
  581.6 11.7 all-to-all-done.3
  593.3 6.1 gather_fusion.4
  603.1 85.3 %while.35 = (s32[]{:T(128)}, f32[2048,256]{1,0:T(8,128)}, bf16[2,512,384]{1,2,0:T(8,128)(2,1)}, s32[2]{0:T(128)}, s32[1024]{0:T(1024)}, /*index=5*/s32[2048]{0:T...) while((s32[]{:T(128)}, f32[2048,256]{1,0:T(8,128)}, ...), condition=%wide.region_18.20_spmd.clone, body=%wide.region_14.19_spmd.clone.sunk | while | flops 3058629120 | bytes 114938480 | solution.py:298
  640.5 5.5 dynamic_update_slice.53
  683.2 5.0 dynamic_update_slice.53
  690.9 6.4 copy.116
  697.3 8.7 dot_general.305
  707.4 3.9 gather_fusion.1
  712.4 11.5 bitcast_convert_fusion.1
  724.0 11.6 fusion.122
  735.5 9.7 copy.140
  746.6 7.3 convolution_bitcast_fusion
  753.9 12.7 copy.131
  768.1 5.0 gather_fusion.5
  774.5 14.8 all_to_all.89
  794.8 5.8 convolution_bitcast_fusion.1
  800.5 11.0 copy.130
  811.6 15.6 fusion.106
  828.4 6.7 fusion.134
  835.1 44.3 %all-reduce.4 = (f32[1536]{0:T(1024)S(1)}, f32[1536]{0:T(1024)S(1)}) all-reduce(f32[1536]{0:T(1024)S(1)} %get-tuple-element.467, f32[1536]{0:T(1024)S(1)} %copy-done.39), channel_id=5, replica_groups=mesh['head'=4,'seq'=8] {'head','seq'}, use_global_device_ids=true, to_apply=%region_22.24.clone | all-reduce | flops 3072 | bytes 24576
  880.6 4.8 fusion.138
  885.4 59.6 %reduce-scatter.20.cloned.1.call-done = f32[24,96,96]{1,2,0:T(8,128)} async-done(((f32[192,96,96]{1,2,0:T(8,128)}), f32[24,96,96]{1,2,0:T(8,128)}) %reduce-scatter.20.cloned.1.call-update) | async-done | bytes 884752 | tf_op jit(solution)/shard_map/reduce_scatter | solution.py:237
  946.7 4.2 fusion.179
  953.3 3.6 fusion.143
  957.0 3.3 fusion.145
  960.2 146.4 %reduce-scatter.16.cloned.1.call-done = f32[8,96,96]{2,1,0:T(8,128)} async-done(((f32[256,96,96]{2,1,0:T(8,128)}), f32[8,96,96]{2,1,0:T(8,128)}) %reduce-scatter.16.cloned.1.call-update) | async-done | bytes 294928 | tf_op jit(solution)/shard_map/reduce_scatter | solution.py:331
  1113.9 153.0 %reduce-scatter.14.cloned.1.call-done = f32[8,96,112]{2,1,0:T(8,128)} async-done(((f32[256,96,112]{2,1,0:T(8,128)}), f32[8,96,112]{2,1,0:T(8,128)}) %reduce-scatter.14.cloned.1.call-update) | async-done | bytes 344080 | tf_op jit(solution)/shard_map/reduce_scatter | solution.py:330
  1276.0 307.7 %reduce-scatter.18.cloned.1.call-done = f32[48,96,96]{1,2,0:T(8,128)} async-done(((f32[384,96,96]{1,2,0:T(8,128)}), f32[48,96,96]{1,2,0:T(8,128)}) %reduce-scatter.18.cloned.1.call-update) | async-done | bytes 1769488 | tf_op jit(solution)/shard_map/reduce_scatter | solution.py:236
  1586.1 5.0 fusion.178
  1591.2 4.0 multiply_subtract_fusion
  1595.2 6.7 divide_add_fusion
  1601.9 5.7 divide_add_fusion.1
  (340 shorter events, 200.2 us)
Async XLA Ops:
  7.2 1578.9 %copy-start = (f32[48,96,96]{2,1,0:T(8,128)S(1)}, f32[48,96,96]{2,1,0:T(8,128)}, u32[]{:S(2)}) copy-start(f32[48,96,96]{2,1,0:T(8,128)} %param.52) | copy-start | bytes 5308420
  7.2 51.3 %copy-start.6 = (bf16[256,1536]{1,0:T(8,128)(2,1)S(1)}, bf16[256,1536]{1,0:T(8,128)(2,1)}, u32[]{:S(2)}) copy-start(bf16[256,1536]{1,0:T(8,128)(2,1)} %param.32) | copy-start | bytes 2359300
  7.2 50.7 %copy-start.42 = (s32[1024]{0:T(1024)S(1)}, s32[1024]{0:T(1024)}, u32[]{:S(2)}) copy-start(s32[1024]{0:T(1024)} %param.57) | copy-start | bytes 12292
  7.2 76.7 %all-gather.7.cloned.1.call-start = ((), (), s32[]{:S(2)}) async-start(), calls=%async_computation.12 | async-start | bytes 6488064 | tf_op jit(solution)/shard_map/all_gather | solution.py:58
  9.1 209.3 %all-gather.9.cloned.1.call-start = ((), (), s32[]{:S(2)}) async-start(), calls=%async_computation.13 | async-start | bytes 6488064 | tf_op jit(solution)/shard_map/all_gather | solution.py:59
  10.9 238.6 %all-gather.17.cloned.1.call-start = ((), (), s32[]{:S(2)}) async-start(), calls=%async_computation.18 | async-start | bytes 3932160 | tf_op jit(solution)/shard_map/all_gather | solution.py:201
  14.4 77.6 %copy-start.51 = (f32[256]{0:T(256)}, f32[256]{0:T(256)S(1)}, u32[]{:S(2)}) copy-start(f32[256]{0:T(256)S(1)} %fusion.159) | copy-start | bytes 3076
  58.5 86.7 %copy-start.31 = (s32[1024]{0:T(1024)}, s32[1024]{0:T(1024)S(1)}, u32[]{:S(2)}) copy-start(s32[1024]{0:T(1024)S(1)} %get-tuple-element.537) | copy-start | bytes 12292
  61.3 42.6 %copy-start.9 = (bf16[256,1536]{0,1:T(8,128)(2,1)}, bf16[256,1536]{0,1:T(8,128)(2,1)S(1)}, u32[]{:S(2)}) copy-start(bf16[256,1536]{0,1:T(8,128)(2,1)S(1)} %copy.108) | copy-start | bytes 2359300
  109.8 15.2 all-to-all-start.1
  113.2 37.0 %copy-start.45 = (pred[1024]{0:T(1024)(128)(4,1)}, pred[1024]{0:T(1024)(128)(4,1)S(1)}, u32[]{:S(2)}) copy-start(pred[1024]{0:T(1024)(128)(4,1)S(1)} %compare_and_fusion.1) | copy-start | bytes 3076
  113.3 96.2 %copy-start.43 = (pred[1024]{0:T(1024)(128)(4,1)}, pred[1024]{0:T(1024)(128)(4,1)S(1)}, u32[]{:S(2)}) copy-start(pred[1024]{0:T(1024)(128)(4,1)S(1)} %compare_and_fusion) | copy-start | bytes 3076
  125.8 19.5 %all-to-all-start = ((bf16[256,4,384]{2,0,1:T(8,128)(2,1)}), bf16[256,4,384]{2,0,1:T(8,128)(2,1)S(1)}, u32[]{:S(2)}, u32[]{:S(2)}) async-start(bf16[256,4,384]{2,0,1:T(8,128)(2,1)} %bitcast.316), calls=%async_computation | async-start | bytes 1572864 | tf_op jit(solution)/shard_map/all_to_all | solution.py:127
  137.6 19.7 %collective-permute-start = (bf16[1024,256]{1,0:T(8,128)(2,1)}, bf16[1024,256]{1,0:T(8,128)(2,1)}, u32[]{:S(2)}, u32[]{:S(2)}) collective-permute-start(bf16[1024,256]{1,0:T(8,128)(2,1)} %broadcast_select_fusion.4), channel_id=1, source_target_pairs={{0,1},{1,2},{2,3},{3,4},{4,5},{5,6},{6,7},{8,9},{9,10},{10,11},{11... | collective-permute-start | bytes 1572872 | tf_op jit(solution)/shard_map/ppermute | solution.py:27
  142.5 60.8 %copy-start.33 = (s32[1024]{0:T(1024)}, s32[1024]{0:T(1024)S(1)}, u32[]{:S(2)}) copy-start(s32[1024]{0:T(1024)S(1)} %fusion.156) | copy-start | bytes 12292
  213.9 23.8 %all-to-all-start.2 = ((bf16[4,256,384]{1,2,0:T(8,128)(2,1)}), bf16[4,256,384]{1,2,0:T(8,128)(2,1)}, u32[]{:S(2)}, u32[]{:S(2)}) async-start(bf16[4,256,384]{1,2,0:T(8,128)(2,1)} %copy.112), calls=%async_computation.2 | async-start | bytes 1572864 | tf_op jit(solution)/shard_map/all_to_all | solution.py:186
  218.1 63.0 %all-gather.11.cloned.1.call-start = ((), (), s32[]{:S(2)}) async-start(), calls=%async_computation.14 | async-start | bytes 3932160 | tf_op jit(solution)/shard_map/all_gather | solution.py:200
  218.4 348.9 %copy-start.27 = (f32[1536]{0:T(1024)}, f32[1536]{0:T(1024)S(1)}, u32[]{:S(2)}) copy-start(f32[1536]{0:T(1024)S(1)} %convert_element_type.202) | copy-start | bytes 18436
  242.0 325.3 %copy-start.40 = (f32[256]{0:T(256)}, f32[256]{0:T(256)S(1)}, u32[]{:S(2)}) copy-start(f32[256]{0:T(256)S(1)} %fusion.160) | copy-start | bytes 3076
  244.3 177.6 %all-gather.13.cloned.1.call-start = ((), (), s32[]{:S(2)}) async-start(), calls=%async_computation.15 | async-start | bytes 10616832 | tf_op jit(solution)/shard_map/all_gather | solution.py:64
  247.2 255.4 %all-gather.15.cloned.1.call-start = ((), (), s32[]{:S(2)}) async-start(), calls=%async_computation.16 | async-start | bytes 5308416 | tf_op jit(solution)/shard_map/all_gather | solution.py:65
  249.4 315.0 %reduce-scatter.10.cloned.1.call-start = ((), (), s32[]{:S(2)}) async-start(), calls=%async_computation.19 | async-start | bytes 3932160 | tf_op jit(solution)/shard_map/reduce_scatter | solution.py:239
  502.6 13.7 copy-start.53
  564.5 2.9 copy-start.4
  567.3 9.1 copy-start.49
  576.4 16.9 %copy-start.32 = (s32[1024]{0:T(1024)S(1)}, s32[1024]{0:T(1024)}, u32[]{:S(2)}) copy-start(s32[1024]{0:T(1024)} %copy-done.31) | copy-start | bytes 12292
  577.4 15.9 all-to-all-start.3
  581.6 210.0 %reduce-scatter.12.cloned.1.call-start = ((), (), s32[]{:S(2)}) async-start(), calls=%async_computation.20 | async-start | bytes 655360 | tf_op jit(solution)/shard_map/reduce_scatter | solution.py:313
  593.3 6.1 copy-start.46
  608.5 10.4 copy-start.37
  651.2 10.4 copy-start.37
  689.6 16.4 %collective-permute-start.1 = (bf16[1024,256]{1,0:T(8,128)(2,1)S(1)}, bf16[1024,256]{1,0:T(8,128)(2,1)S(1)}, u32[]{:S(2)}, u32[]{:S(2)}) collective-permute-start(bf16[1024,256]{1,0:T(8,128)(2,1)S(1)} %slice.231), channel_id=1, source_target_pairs={{1,0},{2,1},{3,2},{4,3},{5,4},{6,5},{7,6},{9,8},{10,9},{11,10},{12... | collective-permute-start | bytes 1572872 | tf_op jit(solution)/shard_map/ppermute | solution.py:27
  697.3 10.0 copy-start.34
  706.0 5.3 copy-start.44
  712.4 168.2 %reduce-scatter.8.cloned.1.call-start = ((), (), s32[]{:S(2)}) async-start(), calls=%async_computation.17 | async-start | bytes 3932160 | tf_op jit(solution)/shard_map/reduce_scatter | solution.py:213
  723.9 221.1 %reduce-scatter.20.cloned.1.call-start = ((), (), s32[]{:S(2)}) async-start(), calls=%async_computation.24 | async-start | bytes 10616832 | tf_op jit(solution)/shard_map/reduce_scatter | solution.py:237
  745.3 361.3 %reduce-scatter.16.cloned.1.call-start = ((), (), s32[]{:S(2)}) async-start(), calls=%async_computation.22 | async-start | bytes 12976128 | tf_op jit(solution)/shard_map/reduce_scatter | solution.py:331
  766.6 500.4 %reduce-scatter.14.cloned.1.call-start = ((), (), s32[]{:S(2)}) async-start(), calls=%async_computation.21 | async-start | bytes 12976128 | tf_op jit(solution)/shard_map/reduce_scatter | solution.py:330
  773.1 21.6 %copy-start.10 = (bf16[256,1536]{0,1:T(8,128)(2,1)S(1)}, bf16[256,1536]{0,1:T(8,128)(2,1)}, u32[]{:S(2)}) copy-start(bf16[256,1536]{0,1:T(8,128)(2,1)} %copy-done.9) | copy-start | bytes 2359300
  811.6 772.2 %reduce-scatter.18.cloned.1.call-start = ((), (), s32[]{:S(2)}) async-start(), calls=%async_computation.23 | async-start | bytes 21233664 | tf_op jit(solution)/shard_map/reduce_scatter | solution.py:236
  828.4 6.7 copy-start.39
  828.4 52.2 %copy-start.48 = (f32[256]{0:T(256)S(1)}, f32[256]{0:T(256)}, u32[]{:S(2)}) copy-start(f32[256]{0:T(256)} %copy-done.47) | copy-start | bytes 3076
  828.4 52.3 %copy-start.28 = (f32[1536]{0:T(1024)S(1)}, f32[1536]{0:T(1024)}, u32[]{:S(2)}) copy-start(f32[1536]{0:T(1024)} %copy-done.27) | copy-start | bytes 18436
  828.4 52.3 %copy-start.41 = (f32[256]{0:T(256)S(1)}, f32[256]{0:T(256)}, u32[]{:S(2)}) copy-start(f32[256]{0:T(256)} %copy-done.40) | copy-start | bytes 3076
  828.4 52.3 %copy-start.50 = (f32[256]{0:T(256)S(1)}, f32[256]{0:T(256)}, u32[]{:S(2)}) copy-start(f32[256]{0:T(256)} %copy-done.49) | copy-start | bytes 3076
  885.4 65.5 %copy-start.14 = (f32[24,96,96]{2,1,0:T(8,128)S(1)}, f32[24,96,96]{2,1,0:T(8,128)}, u32[]{:S(2)}) copy-start(f32[24,96,96]{2,1,0:T(8,128)} %param.39) | copy-start | bytes 2654212
  945.1 5.9 copy-start.23
  950.9 2.4 copy-start.15
  950.9 2.4 copy-start.56
  953.3 3.6 copy-start.57
  956.9 150.9 %copy-start.25 = (f32[8,96,96]{2,1,0:T(8,128)S(1)}, f32[8,96,96]{2,1,0:T(8,128)}, u32[]{:S(2)}) copy-start(f32[8,96,96]{2,1,0:T(8,128)} %param.50) | copy-start | bytes 884740
  956.9 152.4 %copy-start.19 = (f32[8,96,96]{2,1,0:T(8,128)S(1)}, f32[8,96,96]{2,1,0:T(8,128)}, u32[]{:S(2)}) copy-start(f32[8,96,96]{2,1,0:T(8,128)} %param.37) | copy-start | bytes 884740
  956.9 152.4 %copy-start.26 = (f32[8,96,96]{2,1,0:T(8,128)S(1)}, f32[8,96,96]{2,1,0:T(8,128)}, u32[]{:S(2)}) copy-start(f32[8,96,96]{2,1,0:T(8,128)} %param.51) | copy-start | bytes 884740
  1106.6 4.1 copy-start.21
  1106.6 4.1 copy-start.59
  1106.6 5.7 copy-start.60
  1110.7 162.3 %copy-start.20 = (f32[8,96,112]{2,1,0:T(8,128)S(1)}, f32[8,96,112]{2,1,0:T(8,128)}, u32[]{:S(2)}) copy-start(f32[8,96,112]{2,1,0:T(8,128)} %param.36) | copy-start | bytes 1032196
  1110.7 162.3 %copy-start.24 = (f32[8,112,112]{2,1,0:T(8,128)S(1)}, f32[8,112,112]{2,1,0:T(8,128)}, u32[]{:S(2)}) copy-start(f32[8,112,112]{2,1,0:T(8,128)} %param.49) | copy-start | bytes 1204228
  1267.0 7.4 copy-start.22
  1267.0 7.4 copy-start.58
  1586.1 5.0 copy-start.13
  1586.1 5.0 copy-start.18
  1591.2 4.0 copy-start.54
  1595.2 6.7 copy-start.55
  (25 other events, 32.6 us)
Sparse Core Ops, SparseCore 0:
  11.5 72.3 all-gather.6
  87.4 78.0 all-gather.8
  167.1 28.0 all-gather.16
  244.4 36.7 all-gather.10
  283.8 138.0 all-gather.12
  424.5 78.0 all-gather.14
  528.4 36.0 reduce-scatter.9
  712.5 22.8 reduce-scatter.11
  737.9 37.9 reduce-scatter.7
  779.8 165.2 reduce-scatter.19
  952.1 154.4 reduce-scatter.15
  1112.5 154.4 reduce-scatter.13
  1271.3 312.3 reduce-scatter.17
where the time goes:
time: 1630 us; the launch traced here: 1610 us
  waiting for transfers between devices  959 us (59%)
  local copies, waits for them, and re-layouts  231 us (14%)
  matrix products  210 us (13%)
  blocking collectives  102 us (6%)
  other arithmetic  62.9 us (4%)
  starting transfers between devices  21.7 us (1%)
    reduce_scatter x1, waiting for transfers between devices, on_device(): lax.psum_scatter(gateup_wgrad, 'seq', scatter_dimension=0, tiled=True)  308 us
    reduce_scatter x1, waiting for transfers between devices, on_device(): lax.psum_scatter(qkv_wgrad, ('head', 'seq'), scatter_dimension=0, tiled=T...  153 us
    reduce_scatter x1, waiting for transfers between devices, on_device(): lax.psum_scatter(out_wgrad, ('head', 'seq'), scatter_dimension=0, tiled=T...  146 us
    all_gather x1, waiting for transfers between devices, fetch_weights(): lax.all_gather(gateup_stack.astype(jnp.bfloat16), 'seq', axis=0, tiled=True)  136 us
    unnamed x2, blocking collectives  86.9 us
    all_gather x1, waiting for transfers between devices, fetch_weights(): lax.all_gather(down_stack.astype(jnp.bfloat16), 'seq', axis=0, tiled=True)  67.5 us
    reduce_scatter x1, waiting for transfers between devices, on_device(): lax.psum_scatter(down_wgrad, 'seq', scatter_dimension=0, tiled=True)  59.6 us
  transfers between devices with their start and end apart: 19, of which 13 were waited for; matrix products, arithmetic and copies ran while one was open for 21% of the time, Pallas kernels for 0%

commit v1 on v0

v1 whole, which is shorter than its diff:
```python
import functools

import jax
import jax.numpy as jnp
from jax import lax
from jax.experimental import pallas as pl
from jax.experimental.pallas import tpu as pltpu
from jax.sharding import PartitionSpec as P

D = 1536
HEAD_DIM = 128
FF = 4608
WINDOW = 1024
GRID = 16
QW = 1536
QKV = 1792
BLK = 96
BQ = 112
BH = 96
NU = 48

norm_eps = 1e-06
stat_eps = 1e-06
neg_fill = -1e30

QUERY_TILE = 256
SPAN = WINDOW + QUERY_TILE

low = jnp.bfloat16
full = jnp.float32

NT = (((1,), (1,)), ((), ()))
NN = (((1,), (0,)), ((), ()))
TN = (((0,), (0,)), ((), ()))


def mul(a, b, dims, kind=full):
    return lax.dot_general(a, b, dims, preferred_element_type=kind)


def ring_place(index, count):
    return jnp.where(index % 2 == 0, index // 2, count - 1 - index // 2)


def ring_index(place, count):
    return jnp.where(place < count // 2, 2 * place, 2 * (count - 1 - place) + 1)


def ring_routes(count):
    order = [i for i in range(0, count, 2)] + [i for i in range(count - 1, 0, -2)]
    up = [(order[i], order[(i + 1) % count]) for i in range(count)]
    return up, [(b, a) for a, b in up]


def seq_gather(shard):
    count = lax.axis_size("seq")
    rows = shard.shape[0]
    half = rows // 2
    me = lax.axis_index("seq")
    place = ring_place(me, count)
    up, down = ring_routes(count)
    out = jnp.zeros((count,) + shard.shape, shard.dtype)
    out = lax.dynamic_update_slice(out, shard[None], (me, 0, 0))
    ahead = shard
    behind = shard
    for step in range(1, count // 2):
        ahead = lax.ppermute(ahead, "seq", up)
        behind = lax.ppermute(behind, "seq", down)
        out = lax.dynamic_update_slice(
            out, ahead[None], (ring_index((place - step + count) % count, count), 0, 0)
        )
        out = lax.dynamic_update_slice(
            out, behind[None], (ring_index((place + step) % count, count), 0, 0)
        )
    ahead = lax.ppermute(ahead[:half], "seq", up)
    behind = lax.ppermute(behind[half:], "seq", down)
    far = ring_index((place + count // 2) % count, count)
    out = lax.dynamic_update_slice(out, ahead[None], (far, 0, 0))
    return lax.dynamic_update_slice(out, behind[None], (far, half, 0))


def seq_sum(parts):
    count, rows = parts.shape[:2]
    half = rows // 2
    place = ring_place(lax.axis_index("seq"), count)
    up, down = ring_routes(count)

    def part(offset):
        index = ring_index((place + offset + count) % count, count)
        return lax.dynamic_slice_in_dim(parts, index, 1, 0)[0]

    far = part(count // 2)
    ahead = lax.ppermute(far[:half], "seq", up)
    behind = lax.ppermute(far[half:], "seq", down)
    for offset in range(count // 2 - 1, 0, -1):
        local = part(offset)
        if ahead.shape[0] == rows:
            local = (local.astype(full) + ahead.astype(full)).astype(low)
        else:
            local = jnp.concatenate(
                [(local[:half].astype(full) + ahead.astype(full)).astype(low), local[half:]]
            )
        ahead = lax.ppermute(local, "seq", up)
        local = part(-offset)
        if behind.shape[0] == rows:
            local = (local.astype(full) + behind.astype(full)).astype(low)
        else:
            local = jnp.concatenate(
                [local[:half], (local[half:].astype(full) + behind.astype(full)).astype(low)]
            )
        behind = lax.ppermute(local, "seq", down)
    return part(0).astype(full) + ahead.astype(full) + behind.astype(full)


def gather_rows(stack, unit, layout):
    short = stack.astype(low)
    if stack.shape[0] % unit == 0:
        shard = layout(short)
        rows = shard.reshape(-1, shard.shape[-1])
        out = seq_gather(rows)
        return out.reshape((-1,) + shard.shape[1:])
    return layout(lax.all_gather(short, "seq", axis=0, tiled=True))


def sum_rows(rows, local, unit, back):
    count = lax.axis_size("seq")
    if local % unit == 0:
        own = seq_sum(rows.reshape(count, -1, rows.shape[-1]))
        return back(own.reshape((-1,) + rows.shape[1:]))
    return lax.psum_scatter(back(rows), "seq", scatter_dimension=0, tiled=True).astype(full)


def to_columns(stack):
    n, i, j = stack.shape
    return stack.reshape(n // 8, 8, i, j).transpose(0, 2, 1, 3).reshape(n // 8, i, 8 * j)


def from_columns(rows):
    n, i, j = rows.shape
    return rows.reshape(n, i, 8, j // 8).transpose(0, 2, 1, 3).reshape(n * 8, i, j // 8)


def to_units(stack):
    n, i, j = stack.shape
    return stack.reshape(n // 16, 16, i, j).transpose(0, 3, 1, 2).reshape(n // 16, j, 16 * i)


def from_units(rows):
    n, j, i = rows.shape
    return rows.reshape(n, j, 16, i // 16).transpose(0, 2, 3, 1).reshape(n * 16, i // 16, j)


def joined_halves(rows):
    n, i, j = rows.shape
    return rows.reshape(n // 2, 2, i, j).transpose(0, 2, 1, 3).reshape(n // 2 * i, 2 * j)


def split_halves(matrix, i):
    rows, columns = matrix.shape
    m = rows // i
    return (
        matrix.reshape(m, i, 2, columns // 2).transpose(0, 2, 1, 3).reshape(2 * m, i, columns // 2)
    )


def to_partner(value, which):
    count = lax.axis_size("head")
    return lax.ppermute(value, "head", [(i, i ^ which) for i in range(count)])


def head_gather(value):
    across = to_partner(value, 2)
    mate = to_partner(value, 1)
    return value, mate, across, to_partner(across, 1)


def head_exchange(parts):
    return (parts[0],) + tuple(to_partner(parts[j], j) for j in (2, 1, 3))


def head_sum(parts):
    across = (parts[2].astype(full) + to_partner(parts[3], 1).astype(full)).astype(low)
    across = to_partner(across, 2)
    mine = parts[0].astype(full) + to_partner(parts[1], 1).astype(full)
    return mine + across.astype(full)


def in_order(parts, axis):
    me = lax.axis_index("head")
    odd = me % 2 == 1
    lower = [jnp.where(odd, parts[1], parts[0]), jnp.where(odd, parts[0], parts[1])]
    upper = [jnp.where(odd, parts[3], parts[2]), jnp.where(odd, parts[2], parts[3])]
    second = me >= 2
    return jnp.concatenate(
        [jnp.where(second, b, a) for a, b in zip(lower, upper)]
        + [jnp.where(second, a, b) for a, b in zip(lower, upper)],
        axis=axis,
    )


def tile_bias(tile, key_ids, query_ids, bias_ref):
    start = pl.multiple_of(tile * QUERY_TILE, QUERY_TILE)
    shape = (SPAN, QUERY_TILE)
    key = lax.broadcasted_iota(jnp.int32, shape, 0)
    query = lax.broadcasted_iota(jnp.int32, shape, 1)
    same = key_ids[pl.ds(start, SPAN), :] == query_ids[...]
    allowed = same & (key > query) & (key <= query + WINDOW)
    bias_ref[...] = jnp.where(allowed, 0.0, neg_fill)


def attend_kernel(q_ref, kv_ref, kvt_ref, key_ids, query_ids, out_ref, lse_ref, bias_ref):
    tile = pl.program_id(0)
    start = pl.multiple_of(tile * QUERY_TILE, QUERY_TILE)

    @pl.when(pl.program_id(1) == 0)
    def _():
        tile_bias(tile, key_ids, query_ids, bias_ref)

    keys = kv_ref[pl.ds(start, SPAN), :HEAD_DIM]
    scores = mul(keys, q_ref[...], NT) * HEAD_DIM ** (-0.5) + bias_ref[...]
    top = jnp.max(scores, axis=0, keepdims=True)
    expo = jnp.exp(scores - top)
    total = jnp.sum(expo, axis=0, keepdims=True)
    values = kvt_ref[HEAD_DIM:, pl.ds(start, SPAN)]
    mixed = mul(values, expo.astype(low), NN) / total
    out_ref[...] = mixed.T.astype(low)
    lse_ref[0] = top + jnp.log(total)


def attend_back_kernel(
    q_ref, g_ref, kv_ref, kvt_ref, key_ids, query_ids, lse_ref, dq_ref, dkv_ref, bias_ref
):
    tile = pl.program_id(0)
    start = pl.multiple_of(tile * QUERY_TILE, QUERY_TILE)
    scale = HEAD_DIM ** (-0.5)

    @pl.when((tile == 0) & (pl.program_id(1) == 0))
    def _():
        dkv_ref[...] = jnp.zeros_like(dkv_ref)

    @pl.when(pl.program_id(1) == 0)
    def _():
        tile_bias(tile, key_ids, query_ids, bias_ref)

    here = pl.ds(start, SPAN)
    queries = q_ref[...]
    grads = g_ref[...]
    scores = mul(kv_ref[here, :HEAD_DIM], queries, NT) * scale + bias_ref[...]
    probs = jnp.exp(scores - lse_ref[0])
    prob_grad = mul(kv_ref[here, HEAD_DIM:], grads, NT)
    delta = jnp.sum(probs * prob_grad, axis=0, keepdims=True)
    score_grad = (probs * (prob_grad - delta)).astype(low)
    dq = mul(kvt_ref[:HEAD_DIM, here], score_grad, NN) * scale
    dq_ref[...] = dq.T.astype(low)
    dkv_ref[here, :HEAD_DIM] += mul(score_grad, queries, NN) * scale
    dkv_ref[here, HEAD_DIM:] += mul(probs.astype(low), grads, NN)


def attention_specs(group):
    whole = lambda *shape: pl.BlockSpec(shape, lambda t, h: (0,) * len(shape))
    head_rows = pl.BlockSpec((QUERY_TILE, HEAD_DIM), lambda t, h: (t, h))
    keys = whole(2 * group, 2 * HEAD_DIM)
    keys_turned = whole(2 * HEAD_DIM, 2 * group)
    key_ids = whole(2 * group, 1)
    query_ids = pl.BlockSpec((1, QUERY_TILE), lambda t, h: (0, t))
    lse = pl.BlockSpec((1, 1, QUERY_TILE), lambda t, h: (h, 0, t))
    return head_rows, keys, keys_turned, key_ids, query_ids, lse


attention_params = pltpu.CompilerParams(
    dimension_semantics=("arbitrary", "arbitrary"), vmem_limit_bytes=40 * 1024 * 1024
)


def attend(queries, kv, kv_turned, key_ids, query_ids):
    group, width = queries.shape
    heads = width // HEAD_DIM
    rows, keys, turned, kids, qids, lse = attention_specs(group)
    work = heads * (group // QUERY_TILE) * SPAN * QUERY_TILE
    return pl.pallas_call(
        attend_kernel,
        grid=(group // QUERY_TILE, heads),
        in_specs=[rows, keys, turned, kids, qids],
        out_specs=[rows, lse],
        out_shape=[
            jax.ShapeDtypeStruct((group, width), low),
            jax.ShapeDtypeStruct((heads, 1, group), full),
        ],
        scratch_shapes=[pltpu.VMEM((SPAN, QUERY_TILE), full)],
        compiler_params=attention_params,
        cost_estimate=pl.CostEstimate(
            flops=8 * work * HEAD_DIM, bytes_accessed=6 << 20, transcendentals=work
        ),
        name="attend",
    )(queries, kv, kv_turned, key_ids, query_ids)


def attend_back(queries, grads, kv, kv_turned, key_ids, query_ids, lse_rows):
    group, width = queries.shape
    heads = width // HEAD_DIM
    rows, keys, turned, kids, qids, lse = attention_specs(group)
    work = heads * (group // QUERY_TILE) * SPAN * QUERY_TILE
    return pl.pallas_call(
        attend_back_kernel,
        grid=(group // QUERY_TILE, heads),
        in_specs=[rows, rows, keys, turned, kids, qids, lse],
        out_specs=[rows, keys],
        out_shape=[
            jax.ShapeDtypeStruct((group, width), low),
            jax.ShapeDtypeStruct((2 * group, 2 * HEAD_DIM), full),
        ],
        scratch_shapes=[pltpu.VMEM((SPAN, QUERY_TILE), full)],
        compiler_params=attention_params,
        cost_estimate=pl.CostEstimate(
            flops=20 * work * HEAD_DIM, bytes_accessed=8 << 20, transcendentals=work
        ),
        name="attend_back",
    )(queries, grads, kv, kv_turned, key_ids, query_ids, lse_rows)


def update_kernel(rate, w_ref, g_ref, l_ref, r_ref, lr_ref, rr_ref, ln_ref, rn_ref, wn_ref):
    count, rows, columns = g_ref.shape

    def block(b, carry):
        grad = g_ref[b]
        square = jnp.sum(jnp.sum(grad * grad, axis=1, keepdims=True), axis=0, keepdims=True)
        square = square * (1.0 / (rows * columns)) + stat_eps
        short = grad.astype(low)
        turned = grad.T.astype(low)
        ln_ref[b] = 0.5 * l_ref[b] + mul(short, turned, NN) * (0.5 / (columns * square))
        rn_ref[b] = 0.5 * r_ref[b] + mul(turned, short, NN) * (0.5 / (rows * square))
        step = mul(lr_ref[b].astype(low), short, NN).astype(low)
        step = mul(step, rr_ref[b].astype(low), NN)
        wn_ref[b] = w_ref[b] - step * (rate * lax.rsqrt(square))
        return carry

    lax.fori_loop(0, count, block, 0, unroll=2 if count % 2 == 0 else 1)


def update(weight, grad, left, right, left_root, right_root, rate):
    count, rows, columns = weight.shape
    batch = next(b for b in (8, 6, 4, 3, 2, 1) if count % b == 0)
    spec = lambda i, j: pl.BlockSpec((batch, i, j), lambda b: (b, 0, 0))
    return pl.pallas_call(
        functools.partial(update_kernel, rate),
        grid=(count // batch,),
        in_specs=[
            spec(rows, columns),
            spec(rows, columns),
            spec(rows, rows),
            spec(columns, columns),
            spec(rows, rows),
            spec(columns, columns),
        ],
        out_specs=[spec(rows, rows), spec(columns, columns), spec(rows, columns)],
        out_shape=[
            jax.ShapeDtypeStruct(left.shape, full),
            jax.ShapeDtypeStruct(right.shape, full),
            jax.ShapeDtypeStruct(weight.shape, full),
        ],
        compiler_params=pltpu.CompilerParams(vmem_limit_bytes=24 * 1024 * 1024),
        cost_estimate=pl.CostEstimate(
            flops=16 * count * 256 * 256 * 128,
            bytes_accessed=36 * count * rows * 128,
            transcendentals=0,
        ),
        name="update",
    )(weight, grad, left, right, left_root, right_root)


def norm_back(values, inverse, gain, grad):
    scaled = gain * grad
    mean = jnp.mean(values * scaled, axis=-1, keepdims=True)
    return inverse * scaled - values * (inverse * inverse * inverse * mean)


def inverse_norm(values):
    return lax.rsqrt(jnp.mean(values * values, axis=-1, keepdims=True) + norm_eps)


def on_device(
    tokens,
    cotangent,
    attn_gain,
    ffn_gain,
    qkv_stack,
    out_stack,
    gateup_stack,
    down_stack,
    qkv_left,
    qkv_right,
    out_left,
    out_right,
    gateup_left,
    gateup_right,
    down_left,
    down_right,
    qkv_left_root,
    qkv_right_root,
    out_left_root,
    out_right_root,
    gateup_left_root,
    gateup_right_root,
    down_left_root,
    down_right_root,
    sequence_ids,
    token_order,
):
    row_count = tokens.shape[0]
    head_count = lax.axis_size("head")
    seq_count = lax.axis_size("seq")
    device_count = head_count * seq_count
    group = row_count * head_count
    seq_index = lax.axis_index("seq")
    head_index = lax.axis_index("head")
    chip = head_index // 2
    core = head_index % 2
    local_width = QW // head_count

    gains = jnp.concatenate([attn_gain, ffn_gain]).astype(low).astype(full)[None]
    gains = lax.all_to_all(
        jnp.broadcast_to(gains, (device_count, gains.shape[1])),
        ("head", "seq"),
        split_axis=0,
        concat_axis=0,
        tiled=True,
    )
    own_gains = attn_gain.shape[0]
    gain_one = gains[:, :own_gains].reshape(1, D)
    gain_two = gains[:, own_gains:].reshape(1, D)

    qkv_rows = joined_halves(gather_rows(qkv_stack, 8, to_columns))
    out_rows = joined_halves(gather_rows(out_stack, 8, to_columns))
    gateup_shard, down_shard, qkv_rows, out_rows = lax.optimization_barrier(
        (gateup_stack, down_stack, qkv_rows, out_rows)
    )
    gateup = gather_rows(gateup_shard, 16, to_units)
    down = gather_rows(down_shard, 8, to_columns)
    unit_count = gateup.shape[0] // 2
    gateup = gateup.reshape(2 * unit_count * BLK, D)
    down = joined_halves(down)

    tokens_float = tokens.astype(full)
    inverse_one = inverse_norm(tokens_float)
    normed_one = (tokens_float * inverse_one * gain_one).astype(low)
    normed_one_group = jnp.concatenate(head_gather(normed_one))

    def chip_columns(which):
        return jnp.concatenate(
            [
                lax.dynamic_slice_in_dim(qkv_rows, which * 2 * local_width, 2 * local_width, 1),
                qkv_rows[:, QW:],
            ],
            axis=1,
        )

    def core_columns(block, which):
        return jnp.concatenate(
            [
                lax.dynamic_slice_in_dim(block, which * local_width, local_width, 1),
                block[:, 2 * local_width :],
            ],
            axis=1,
        )

    own_block = chip_columns(chip)
    across_block = to_partner(chip_columns(1 - chip), 2)
    qkv_own = in_order(
        [
            core_columns(own_block, core),
            to_partner(core_columns(own_block, 1 - core), 1),
            core_columns(across_block, core),
            to_partner(core_columns(across_block, 1 - core), 1),
        ],
        0,
    )
    projected = mul(normed_one_group, qkv_own, NN, low)

    buffer_rows = ((token_order // row_count) ^ head_index) * row_count + token_order % row_count
    shuffle = (
        buffer_rows[:, None] == lax.broadcasted_iota(jnp.int32, (group, group), 1)
    ).astype(low)
    stream = mul(shuffle, projected, NN, low)
    query_stream = stream[:, :local_width]
    kv_stream = stream[:, local_width:]
    kv_before = lax.ppermute(kv_stream, "seq", [(i, i + 1) for i in range(seq_count - 1)])
    kv_both = jnp.concatenate([kv_before, kv_stream], axis=0)
    kv_turned = kv_both.T
    ids_own = lax.dynamic_slice_in_dim(sequence_ids, seq_index * group, group, 0)
    ids_before = lax.dynamic_slice_in_dim(
        sequence_ids, jnp.maximum(seq_index - 1, 0) * group, group, 0
    )
    ids_before = jnp.where(seq_index > 0, ids_before, -1)
    key_ids = jnp.concatenate([ids_before, ids_own])[:, None]
    query_ids = ids_own[None, :]
    mixed_stream, lse = attend(query_stream, kv_both, kv_turned, key_ids, query_ids)
    mixed_group = mul(shuffle, mixed_stream, TN, low)

    mixed_parts = head_exchange([mixed_group[i * row_count :][:row_count] for i in range(4)])
    order = (0, 2, 1, 3)
    mixed_parts = [mixed_parts[order.index(j)] for j in range(4)]
    attended = jnp.concatenate(mixed_parts, axis=1)
    out_all = jnp.concatenate(head_gather(out_rows))
    resid = tokens_float + mul(attended, out_all, NN)
    inverse_two = inverse_norm(resid)
    normed_two = (resid * inverse_two * gain_two).astype(low)
    normed_group = jnp.concatenate(head_gather(normed_two))
    grad_group = jnp.concatenate(head_gather(cotangent))

    gate_up = mul(gateup, normed_group, NT).reshape(unit_count, 2, BLK, group)
    hidden, act_pull = jax.vjp(
        lambda g, u: jax.nn.gelu(g, approximate=True) * u, gate_up[:, 0], gate_up[:, 1]
    )
    hidden = hidden.astype(low).reshape(unit_count * BLK, group)
    hidden_grad = mul(down, grad_group, NT).reshape(unit_count, BLK, group)
    gate_grad, up_grad = act_pull(hidden_grad)
    gate_up_grad = (
        jnp.stack([gate_grad, up_grad], axis=1).astype(low).reshape(2 * unit_count * BLK, group)
    )
    normed_part = mul(gate_up_grad, gateup, TN, low)
    normed_two_grad = head_sum([normed_part[i * row_count :][:row_count] for i in range(4)])
    gateup_wgrad = mul(gate_up_grad, normed_group, NN, low).reshape(2 * unit_count, BLK, D)
    down_wgrad = split_halves(mul(hidden, grad_group, NN, low), BLK)
    gateup_grad_own = sum_rows(gateup_wgrad, gateup_stack.shape[0], 16, from_units)
    down_grad_own = sum_rows(down_wgrad, down_stack.shape[0], 8, from_columns)
    ffn_part = mul(hidden, down, TN, low)
    ffn_out = head_sum([ffn_part[i * row_count :][:row_count] for i in range(4)])
    block_out = (resid + ffn_out).astype(low)

    resid_grad = cotangent.astype(full) + norm_back(resid, inverse_two, gain_two, normed_two_grad)
    gain_two_grad = jnp.sum(normed_two_grad * resid * inverse_two, axis=0)
    proj_grad = resid_grad.astype(low)
    attended_grad = mul(proj_grad, out_all, NT, low)
    grad_parts = head_exchange(
        [attended_grad[:, i * local_width : (i + 1) * local_width] for i in range(4)]
    )
    mixed_grad_group = jnp.concatenate([grad_parts[order.index(j)] for j in range(4)])
    mixed_grad_stream = mul(shuffle, mixed_grad_group, NN, low)
    proj_grad_group = jnp.concatenate(head_gather(proj_grad))
    out_wgrad = split_halves(mul(mixed_group, proj_grad_group, TN, low), BLK)
    out_grad_own = sum_rows(out_wgrad, out_stack.shape[0], 8, from_columns)

    query_grad, kv_grad = attend_back(
        query_stream, mixed_grad_stream, kv_both, kv_turned, key_ids, query_ids, lse
    )
    kv_later = lax.ppermute(
        kv_grad[:group].astype(low), "seq", [(i, i - 1) for i in range(1, seq_count)]
    )
    kv_grad = (kv_grad[group:] + kv_later.astype(full)).astype(low)
    grad_local = mul(shuffle, jnp.concatenate([query_grad, kv_grad], axis=1), TN, low)
    gathered = head_gather(grad_local)

    def own_order(value, j):
        quarters = [value[i * row_count :][:row_count] for i in range(4)]
        return jnp.concatenate([quarters[i ^ j] for i in range(4)])

    gathered = [own_order(value, j) for j, value in enumerate(gathered)]
    kv_total = sum(value[:, local_width:].astype(full) for value in gathered).astype(low)
    qkv_grad = jnp.concatenate(
        [in_order([value[:, :local_width] for value in gathered], 1), kv_total], axis=1
    )
    feature_start = head_index * local_width
    features = lax.dynamic_slice_in_dim(normed_one_group, feature_start, local_width, 1)
    qkv_wgrad = split_halves(mul(features, qkv_grad, TN, low), BLK)
    qkv_grad_own = sum_rows(qkv_wgrad, qkv_stack.shape[0], 8, from_columns)
    feature_grad = mul(qkv_grad, qkv_rows, NT, low)
    feature_parts = head_exchange([feature_grad[i * row_count :][:row_count] for i in range(4)])
    normed_one_grad = in_order([feature_parts[order.index(j)] for j in range(4)], 1).astype(full)
    input_grad = resid_grad + norm_back(tokens_float, inverse_one, gain_one, normed_one_grad)
    gain_one_grad = jnp.sum(normed_one_grad * tokens_float * inverse_one, axis=0)
    gain_grads = jnp.concatenate(
        [gain_one_grad.reshape(device_count, -1), gain_two_grad.reshape(device_count, -1)], axis=1
    )
    gain_grads = lax.all_to_all(
        gain_grads, ("head", "seq"), split_axis=0, concat_axis=0, tiled=True
    )
    gain_grads = jnp.sum(gain_grads, axis=0)

    gateup_new = update(
        gateup_stack,
        gateup_grad_own,
        gateup_left,
        gateup_right,
        gateup_left_root,
        gateup_right_root,
        0.5 * D ** (-0.5),
    )
    down_new = update(
        down_stack,
        down_grad_own,
        down_left,
        down_right,
        down_left_root,
        down_right_root,
        0.5 * FF ** (-0.5),
    )
    out_new = update(
        out_stack,
        out_grad_own,
        out_left,
        out_right,
        out_left_root,
        out_right_root,
        0.5 * (QW // 64) ** (-0.5),
    )
    qkv_new = update(
        qkv_stack,
        qkv_grad_own,
        qkv_left,
        qkv_right,
        qkv_left_root,
        qkv_right_root,
        0.5 * D ** (-0.5),
    )
    return (
        (block_out, input_grad, gain_grads[:own_gains], gain_grads[own_gains:])
        + tuple(qkv_new)
        + tuple(out_new)
        + tuple(gateup_new)
        + tuple(down_new)
    )


def solution(mesh):
    rows = P(("seq", "head"), None)
    gain = P(("head", "seq"))
    blocks = P(("head", "seq"), None, None)
    return jax.shard_map(
        on_device,
        mesh=mesh,
        in_specs=(rows, rows, gain, gain) + (blocks,) * 20 + (P(), P("seq")),
        out_specs=(rows, rows, gain, gain) + (blocks,) * 12,
        check_vma=False,
    )
```

time: 1630 us -> 642 us (0.39)
  waiting for transfers between devices: 959 us -> 182 us
  matrix products: 210 us -> 77.6 us
  blocking collectives: 102 us -> 0 us
  starting transfers between devices: 21.7 us -> 115 us
  local copies, waits for them, and re-layouts: 231 us -> 141 us
  Pallas kernels: 0 us -> 52.1 us
    reduce_scatter x7 -> x0, waiting for transfers between devices: 682 us -> none  [the longest x1 308 us: on_device(): lax.psum_scatter(gateup_wgrad, 'seq', scatter_dimension=0, tiled=True)]
    all_gather x6 -> x0, waiting for transfers between devices: 247 us -> none  [the longest x1 136 us: fetch_weights(): lax.all_gather(gateup_stack.astype(jnp.bfloat16), 'seq', axis=0, tiled=True)]
    ppermute x2 -> x102, waiting for transfers between devices: 4.89 us -> 182 us  [the longest x12 51.2 us: seq_sum(): ahead = lax.ppermute(local, 'seq', up)]
    dot_general x70 -> x15, matrix products: 210 us -> 77.6 us  [mul(): return lax.dot_general(a, b, dims, preferred_element_type=kind)]
    ppermute x2 -> x102, starting transfers between devices: 5.64 us -> 105 us  [the longest x36 19.7 us: to_partner(): return lax.ppermute(value, 'head', [(i, i ^ which) for i in range(count)])]
    unnamed x2 -> x0, blocking collectives: 86.9 us -> none
    pallas_call x0 -> x6, Pallas kernels: none -> 52.1 us  [the longest x4 20.8 us: update(): pl.pallas_call(functools.partial(update_kernel, rate), grid=(count // bat...]
    dot_general x5 -> x2, local copies, waits for them, and re-layouts: 49.4 us -> 8.81 us  [mul(): return lax.dot_general(a, b, dims, preferred_element_type=kind)]
  transfers between devices with their start and end apart: 19 -> 104, of which waited for: 13 -> 43; matrix products, arithmetic and copies ran while one was open for 21% -> 34% of each run, Pallas kernels for 0% -> 8%
where the time goes in v1:
time: 642 us; the launch traced here: 632 us
  waiting for transfers between devices  182 us (28%)
  local copies, waits for them, and re-layouts  141 us (22%)
  starting transfers between devices  115 us (18%)
  matrix products  77.6 us (12%)
  other arithmetic  60.8 us (9%)
  Pallas kernels  52.1 us (8%)
    dot_general x15, matrix products, mul(): return lax.dot_general(a, b, dims, preferred_element_type=kind)  77.6 us
    ppermute x12, waiting for transfers between devices, seq_sum(): ahead = lax.ppermute(local, 'seq', up)  51.2 us
    ppermute x36, waiting for transfers between devices, to_partner(): return lax.ppermute(value, 'head', [(i, i ^ which) for i in range(count)])  46.1 us
    unnamed x176, local copies, waits for them, and re-layouts  34.2 us
    ppermute x12, waiting for transfers between devices, seq_gather(): behind = lax.ppermute(behind, 'seq', down)  23.9 us
    pallas_call x4, Pallas kernels, update(): pl.pallas_call(functools.partial(update_kernel, rate), grid=(count // bat...  20.8 us
    ppermute x36, starting transfers between devices, to_partner(): return lax.ppermute(value, 'head', [(i, i ^ which) for i in range(count)])  19.7 us
    pallas_call x1, Pallas kernels, attend_back(): pl.pallas_call(attend_back_kernel, grid=(group // QUERY_TILE, heads), in_...  18.4 us
  transfers between devices with their start and end apart: 104, of which 43 were waited for; matrix products, arithmetic and copies ran while one was open for 34% of the time, Pallas kernels for 8%

profile of v1, /device:TPU:0, one launch (start us, length us, event | category | flops | bytes accessed | tf_op | source)
XLA Modules:
  0.0 632.2 jit_solution(5708118819460378444)
XLA Ops:
  2.7 3.0 collective-permute-start.3
  10.5 6.3 all-to-all-start
  49.3 2.9 collective-permute-done.17
  53.1 4.1 collective-permute-done.18
  68.3 2.4 copy.111
  88.4 3.5 broadcast_in_dim.148
  104.3 2.8 collective-permute-done.19
  108.8 4.0 collective-permute-done.29
  115.3 9.9 %collective-permute-done.30 = bf16[288,1536]{1,0:T(8,128)(2,1)} collective-permute-done((bf16[288,1536]{1,0:T(8,128)(2,1)S(1)}, bf16[288,1536]{1,0:T(8,128)(2,1)}, u32[]{:S(2)}, u32[]{:S(2)}) %collective-permute-start.30) | collective-permute-done | bytes 884768 | tf_op jit(solution)/shard_map/ppermute | solution.py:68
  127.9 9.9 %collective-permute-done.43 = bf16[288,768]{1,0:T(8,128)(2,1)} collective-permute-done((bf16[288,768]{1,0:T(8,128)(2,1)S(1)}, bf16[288,768]{1,0:T(8,128)(2,1)}, u32[]{:S(2)}, u32[]{:S(2)}) %collective-permute-start.43) | collective-permute-done | bytes 442400 | tf_op jit(solution)/shard_map/ppermute | solution.py:68
  143.1 4.7 copy.142
  149.7 3.0 pad_maximum_fusion
  155.8 9.7 %collective-permute-done.27 = bf16[384,1536]{1,0:T(8,128)(2,1)} collective-permute-done((bf16[384,1536]{1,0:T(8,128)(2,1)S(1)}, bf16[384,1536]{1,0:T(8,128)(2,1)}, u32[]{:S(2)}, u32[]{:S(2)}) %collective-permute-start.27) | collective-permute-done | bytes 1179680 | tf_op jit(solution)/shard_map/ppermute | solution.py:168
  167.0 2.4 constant_dynamic-update-slice_fusion.1
  172.1 2.4 broadcast_select_fusion.11
  174.5 7.3 %fusion.23 = bf16[1024,640]{1,0:T(8,128)(2,1)} fusion(s32[1024]{0:T(1024)S(1)} %fusion.117, bf16[384,640]{1,0:T(8,128)(2,1)} %broadcast_select_fusion.8, bf16[384,640]{1,0:T(8,128)(2,1)} %get-tuple-element.88, bf16[384,640]{1,0:T(8,128)(2,1)} %get-tuple-element.87, bf16[384,640]{1,0:T(8,128)(2,1)S(1)} %get-tuple-element.86, ...), kind=kOutput, calls=%fused_computation.31 | convolution fusion | flops 3376939008 | bytes 6426624 | tf_op jit(solution)/shard_map/dot_general | solution.py:38
  184.2 2.9 collective-permute-start.22
  191.7 2.6 collective-permute-done.46
  196.7 5.4 collective-permute-done.47
  202.9 4.1 copy.145
  207.0 5.6 copy.122
  212.6 2.5 copy.148
  217.3 2.6 collective-permute-start.34
  226.3 12.9 %attend.1 = (bf16[1024,384]{1,0:T(8,128)(2,1)S(1)}, f32[3,1,1024]{2,1,0:T(1,128)S(1)}) custom-call(bf16[1024,384]{1,0:T(8,128)(2,1)S(1)} %copy-done.9, bf16[2048,256]{1,0:T(8,128)(2,1)S(1)} %copy.116.kv_ref, bf16[256,2048]{1,0:T(8,128)(2,1)S(1)} %get-tuple-element.122.kvt_ref, s32[2048,1]{1,0:T(8,128)S(1)} %copy.117.key_ids, s32[1,1024]{1,0:T(1,128)S(1)} %bitcast.356), custom_call_target="tpu_custom_call" | custom-call | flops 4026531840 | bytes 6291456 | tf_op jit(solution)/shard_map/attend/pallas_call | solution.py:280
  244.9 2.9 collective-permute-done.25
  247.8 2.6 collective-permute-done.24
  250.4 3.8 multiply_reduce_fusion.2
  257.8 5.8 collective-permute-start.35
  269.3 5.3 collective-permute-done.38
  279.7 9.8 %fusion.32 = f32[12,2,96,1024]{3,2,1,0:T(8,128)S(1)} fusion(bf16[12,2,96,1536]{3,2,1,0:T(8,128)(2,1)} %bitcast.40, bf16[256,1536]{1,0:T(8,128)(2,1)S(1)} %collective-permute-done.39, bf16[256,1536]{1,0:T(8,128)(2,1)S(1)} %collective-permute-done.38, bf16[256,1536]{1,0:T(8,128)(2,1)S(1)} %collective-permute-done.37, ...), kind=kOutput, calls=%fused_computation.48 | convolution fusion | flops 7260340224 | bytes 19660800 | tf_op jit(solution)/shard_map/dot_general | solution.py:38
  291.5 10.4 %fusion.6 = (bf16[12,1,96,1024]{3,2,0,1:T(8,128)(2,1)S(1)}, bf16[12,1,96,1024]{3,2,0,1:T(8,128)(2,1)}) fusion(f32[12,2,96,1024]{3,2,1,0:T(8,128)S(1)} %fusion.32, bf16[12,96,1536]{2,1,0:T(8,128)(2,1)S(1)} %bitcast.389, bf16[1024,1536]{1,0:T(8,128)(2,1)} %constant_dynamic-update-slice_fusion.4), kind=kOutput, calls=%fused_computation.10 | convolution fusion | flops 3652190208 | bytes 20840448 | tf_op jit(solution)/shard_map/dot_general | solution.py:38
  304.5 10.0 %fusion.148 = bf16[1024,1536]{1,0:T(8,128)(2,1)S(1)} fusion(bf16[2304,1024]{1,0:T(8,128)(2,1)S(1)} %bitcast.374, bf16[2304,1536]{1,0:T(8,128)(2,1)} %bitcast.64), kind=kOutput, calls=%fused_computation.338 | convolution fusion | flops 7247757312 | bytes 14942208 | tf_op jit(solution)/shard_map/dot_general | solution.py:38
  316.3 5.0 fusion.147
  324.9 5.8 fusion.38
  330.8 3.8 collective-permute-start.94
  334.6 9.3 %fusion.34 = bf16[8,288,1536]{2,1,0:T(8,128)(2,1)S(1)} fusion(bf16[8,288,1024]{2,1,0:T(8,128)(2,1)S(1)} %bitcast.375, bf16[256,1536]{1,0:T(8,128)(2,1)} %copy-done.78, bf16[256,1536]{1,0:T(8,128)(2,1)} %copy-done.76, bf16[256,1536]{1,0:T(8,128)(2,1)} %copy-done.77, bf16[256,1536]{1,0:T(8,128)(2,1)S(1)} %multiply_convert_fusion), kind=kOutput, calls=%fused_computation.50 | convolution fusion | flops 7260340224 | bytes 14942208 | tf_op jit(solution)/shard_map/dot_general | solution.py:38
  344.1 2.5 collective-permute-start.86
  346.8 9.4 %collective-permute-done.86 = bf16[144,1536]{1,0:T(8,128)(2,1)S(1)} collective-permute-done((bf16[144,1536]{1,0:T(8,128)(2,1)S(1)}, bf16[144,1536]{1,0:T(8,128)(2,1)S(1)}, u32[]{:S(2)}, u32[]{:S(2)}) %collective-permute-start.86) | collective-permute-done | bytes 442400 | tf_op jit(solution)/shard_map/ppermute | solution.py:93
  359.9 8.4 %collective-permute-done.95 = bf16[288,768]{1,0:T(8,128)(2,1)S(1)} collective-permute-done((bf16[288,768]{1,0:T(8,128)(2,1)S(1)}, bf16[288,768]{1,0:T(8,128)(2,1)S(1)}, u32[]{:S(2)}, u32[]{:S(2)}) %collective-permute-start.95) | collective-permute-done | bytes 442400 | tf_op jit(solution)/shard_map/ppermute | solution.py:103
  376.4 21.9 %collective-permute-done.96 = bf16[288,768]{1,0:T(8,128)(2,1)S(1)} collective-permute-done((bf16[288,768]{1,0:T(8,128)(2,1)S(1)}, bf16[288,768]{1,0:T(8,128)(2,1)S(1)}, u32[]{:S(2)}, u32[]{:S(2)}) %collective-permute-start.96) | collective-permute-done | bytes 442400 | tf_op jit(solution)/shard_map/ppermute | solution.py:103
  406.8 11.2 %collective-permute-done.50 = bf16[256,1536]{1,0:T(8,128)(2,1)S(1)} collective-permute-done((bf16[256,1536]{1,0:T(8,128)(2,1)S(1)}, bf16[256,1536]{1,0:T(8,128)(2,1)S(1)}, u32[]{:S(2)}, u32[]{:S(2)}) %collective-permute-start.50) | collective-permute-done | bytes 786464 | tf_op jit(solution)/shard_map/ppermute | solution.py:168
  418.0 3.5 fusion.134
  421.4 2.6 fusion.149
  431.8 3.8 collective-permute-done.58
  438.5 18.4 %attend_back.1 = (bf16[1024,384]{1,0:T(8,128)(2,1)S(1)}, f32[2048,256]{1,0:T(8,128)S(1)}) custom-call(bf16[1024,384]{1,0:T(8,128)(2,1)S(1)} %copy-done.10, bf16[1024,384]{1,0:T(8,128)(2,1)S(1)} %fusion.21.g_ref, bf16[2048,256]{1,0:T(8,128)(2,1)S(1)} %copy-done.8, bf16[256,2048]{1,0:T(8,128)(2,1)S(1)} %get-tuple-element.122.kvt_ref, s32[2048,1]{1,0:T(8,128)S(1)} %copy-done.6, ...), custom_call_target="tpu_custom_call" | custom-call | flops 10066329600 | bytes 8388608 | tf_op jit(solution)/shard_map/attend_back/pallas_call | solution.py:303
  464.8 3.6 fusion.56
  470.8 4.4 collective-permute-done.60
  477.1 4.0 fusion.24
  481.2 3.0 reshape.280
  490.5 5.3 collective-permute-done.82
  496.7 5.7 update.7
  504.8 2.6 fusion.54
  510.7 16.1 %collective-permute-done.80 = bf16[96,768]{1,0:T(8,128)(2,1)S(1)} collective-permute-done((bf16[96,768]{1,0:T(8,128)(2,1)S(1)}, bf16[96,768]{1,0:T(8,128)(2,1)S(1)}, u32[]{:S(2)}, u32[]{:S(2)}) %collective-permute-start.80) | collective-permute-done | bytes 147488 | tf_op jit(solution)/shard_map/ppermute | solution.py:103
  531.1 2.6 collective-permute-done.84
  537.9 2.4 collective-permute-done.85
  544.1 2.4 update.5
  550.7 3.2 copy.136
  562.2 10.2 %update.6 = (f32[48,96,96]{2,1,0:T(8,128)}, f32[48,96,96]{2,1,0:T(8,128)}, f32[48,96,96]{2,1,0:T(8,128)}) custom-call(f32[48,96,96]{2,1,0:T(8,128)S(1)} %copy-done.1, f32[48,96,96]{2,1,0:T(8,128)S(1)} %bitcast.352, f32[48,96,96]{2,1,0:T(8,128)S(1)} %copy-done.13, f32[48,96,96]{2,1,0:T(8,128)S(1)} %copy-done.14, f32[48,96,96]{2,1,0:T(8,128)S(1)} %copy-done.15, ...), custom_call_target="tpu_custom_call" | custom-call | flops 6442450944 | bytes 21233664 | tf_op jit(solution)/shard_map/update/pallas_call | solution.py:344
  581.3 3.1 fusion.91
  594.0 4.7 collective-permute-done.65
  601.9 4.2 all-to-all-start.1
  608.9 4.9 collective-permute-done.69
  624.7 3.2 collective-permute-done.74
  629.3 2.5 update.4
  (523 shorter events, 268.1 us)
Async XLA Ops:
  2.7 26.5 %collective-permute-start.3 = (bf16[96,896]{1,0:T(8,128)(2,1)}, bf16[96,896]{1,0:T(8,128)(2,1)}, u32[]{:S(2)}, u32[]{:S(2)}) collective-permute-start(bf16[96,896]{1,0:T(8,128)(2,1)} %reshape_reshape.34), channel_id=1, source_target_pairs={{0,2},{2,4},{4,6},{6,7},{7,5},{5,3},{3,1},{1,0},{8,10},{10,12},{12... | collective-permute-start | bytes 516104 | tf_op jit(solution)/shard_map/ppermute | solution.py:67
  5.8 26.0 %collective-permute-start.4 = (bf16[96,896]{1,0:T(8,128)(2,1)}, bf16[96,896]{1,0:T(8,128)(2,1)S(1)}, u32[]{:S(2)}, u32[]{:S(2)}) collective-permute-start(bf16[96,896]{1,0:T(8,128)(2,1)} %reshape_reshape.34), channel_id=1, source_target_pairs={{2,0},{4,2},{6,4},{7,6},{5,7},{3,5},{1,3},{0,1},{10,8},{12,10},{14... | collective-permute-start | bytes 516104 | tf_op jit(solution)/shard_map/ppermute | solution.py:68
  7.7 17.4 %collective-permute-start.11 = (bf16[96,768]{1,0:T(8,128)(2,1)}, bf16[96,768]{1,0:T(8,128)(2,1)}, u32[]{:S(2)}, u32[]{:S(2)}) collective-permute-start(bf16[96,768]{1,0:T(8,128)(2,1)} %reshape_reshape.35), channel_id=1, source_target_pairs={{0,2},{2,4},{4,6},{6,7},{7,5},{5,3},{3,1},{1,0},{8,10},{10,12},{12... | collective-permute-start | bytes 442376 | tf_op jit(solution)/shard_map/ppermute | solution.py:67
  9.7 17.4 %collective-permute-start.12 = (bf16[96,768]{1,0:T(8,128)(2,1)}, bf16[96,768]{1,0:T(8,128)(2,1)}, u32[]{:S(2)}, u32[]{:S(2)}) collective-permute-start(bf16[96,768]{1,0:T(8,128)(2,1)} %reshape_reshape.35), channel_id=1, source_target_pairs={{2,0},{4,2},{6,4},{7,6},{5,7},{3,5},{1,3},{0,1},{10,8},{12,10},{14... | collective-permute-start | bytes 442376 | tf_op jit(solution)/shard_map/ppermute | solution.py:68
  10.5 13.3 %all-to-all-start = ((f32[32,1,96]{2,1,0:T(1,128)}), f32[32,1,96]{2,1,0:T(1,128)S(1)}, u32[]{:S(2)}, u32[]{:S(2)}) async-start(f32[32,1,96]{2,1,0:T(1,128)} %broadcast_in_dim.127), calls=%async_computation | async-start | bytes 32768 | tf_op jit(solution)/shard_map/all_to_all | solution.py:421
  16.8 77.3 %collective-permute-start.51 = (bf16[256,1536]{1,0:T(8,128)(2,1)}, bf16[256,1536]{1,0:T(8,128)(2,1)}, u32[]{:S(2)}, u32[]{:S(2)}) collective-permute-start(bf16[256,1536]{1,0:T(8,128)(2,1)} %param.27), channel_id=1, source_target_pairs={{0,8},{8,0},{16,24},{24,16},{1,9},{9,1},{17,25},{25,17},{2,10},{10... | collective-permute-start | bytes 2359304 | tf_op jit(solution)/shard_map/ppermute | solution.py:168
  25.2 72.4 %collective-permute-start.52 = (bf16[256,1536]{1,0:T(8,128)(2,1)}, bf16[256,1536]{1,0:T(8,128)(2,1)}, u32[]{:S(2)}, u32[]{:S(2)}) collective-permute-start(bf16[256,1536]{1,0:T(8,128)(2,1)} %param.27), channel_id=1, source_target_pairs={{0,16},{8,24},{16,0},{24,8},{1,17},{9,25},{17,1},{25,9},{2,18},{10... | collective-permute-start | bytes 2359304 | tf_op jit(solution)/shard_map/ppermute | solution.py:168
  27.1 88.1 %collective-permute-start.1 = (bf16[256,1536]{1,0:T(8,128)(2,1)}, bf16[256,1536]{1,0:T(8,128)(2,1)}, u32[]{:S(2)}, u32[]{:S(2)}) collective-permute-start(bf16[256,1536]{1,0:T(8,128)(2,1)} %fusion.62), channel_id=1, source_target_pairs={{0,16},{8,24},{16,0},{24,8},{1,17},{9,25},{17,1},{25,9},{2,18},{10... | collective-permute-start | bytes 2359304 | tf_op jit(solution)/shard_map/ppermute | solution.py:168
  45.6 15.0 %collective-permute-start.7 = (bf16[96,896]{1,0:T(8,128)(2,1)S(1)}, bf16[96,896]{1,0:T(8,128)(2,1)S(1)}, u32[]{:S(2)}, u32[]{:S(2)}) collective-permute-start(bf16[96,896]{1,0:T(8,128)(2,1)S(1)} %collective-permute-done.5), channel_id=1, source_target_pairs={{0,2},{2,4},{4,6},{6,7},{7,5},{5,3},{3,1},{1,0},{8,10},{10,12},{12... | collective-permute-start | bytes 516104 | tf_op jit(solution)/shard_map/ppermute | solution.py:67
  74.8 26.3 %collective-permute-start.40 = (bf16[288,768]{1,0:T(8,128)(2,1)}, bf16[288,768]{1,0:T(8,128)(2,1)}, u32[]{:S(2)}, u32[]{:S(2)}) collective-permute-start(bf16[288,768]{1,0:T(8,128)(2,1)} %reshape_reshape.37), channel_id=1, source_target_pairs={{0,2},{2,4},{4,6},{6,7},{7,5},{5,3},{3,1},{1,0},{8,10},{10,12},{12... | collective-permute-start | bytes 1327112 | tf_op jit(solution)/shard_map/ppermute | solution.py:67
  87.9 15.1 %collective-permute-start.41 = (bf16[288,768]{1,0:T(8,128)(2,1)}, bf16[288,768]{1,0:T(8,128)(2,1)S(1)}, u32[]{:S(2)}, u32[]{:S(2)}) collective-permute-start(bf16[288,768]{1,0:T(8,128)(2,1)} %reshape_reshape.37), channel_id=1, source_target_pairs={{2,0},{4,2},{6,4},{7,6},{5,7},{3,5},{1,3},{0,1},{10,8},{12,10},{14... | collective-permute-start | bytes 1327112 | tf_op jit(solution)/shard_map/ppermute | solution.py:68
  94.1 13.1 %collective-permute-start.19 = (bf16[384,1024]{1,0:T(8,128)(2,1)S(1)}, bf16[384,1024]{1,0:T(8,128)(2,1)S(1)}, u32[]{:S(2)}, u32[]{:S(2)}) collective-permute-start(bf16[384,1024]{1,0:T(8,128)(2,1)S(1)} %copy-done.65), channel_id=1, source_target_pairs={{0,16},{8,24},{16,0},{24,8},{1,17},{9,25},{17,1},{25,9},{2,18},{10... | collective-permute-start | bytes 2359304 | tf_op jit(solution)/shard_map/ppermute | solution.py:168
  97.6 15.2 %collective-permute-start.29 = (bf16[288,1536]{1,0:T(8,128)(2,1)S(1)}, bf16[288,1536]{1,0:T(8,128)(2,1)S(1)}, u32[]{:S(2)}, u32[]{:S(2)}) collective-permute-start(bf16[288,1536]{1,0:T(8,128)(2,1)S(1)} %copy-done.62), channel_id=1, source_target_pairs={{0,2},{2,4},{4,6},{6,7},{7,5},{5,3},{3,1},{1,0},{8,10},{10,12},{12... | collective-permute-start | bytes 2654216 | tf_op jit(solution)/shard_map/ppermute | solution.py:67
  101.1 46.6 %collective-permute-start = (bf16[256,1536]{1,0:T(8,128)(2,1)S(1)}, bf16[256,1536]{1,0:T(8,128)(2,1)}, u32[]{:S(2)}, u32[]{:S(2)}) collective-permute-start(bf16[256,1536]{1,0:T(8,128)(2,1)S(1)} %copy-done.51), channel_id=1, source_target_pairs={{0,8},{8,0},{16,24},{24,16},{1,9},{9,1},{17,25},{25,17},{2,10},{10... | collective-permute-start | bytes 2359304 | tf_op jit(solution)/shard_map/ppermute | solution.py:168
  103.0 22.2 %collective-permute-start.30 = (bf16[288,1536]{1,0:T(8,128)(2,1)S(1)}, bf16[288,1536]{1,0:T(8,128)(2,1)}, u32[]{:S(2)}, u32[]{:S(2)}) collective-permute-start(bf16[288,1536]{1,0:T(8,128)(2,1)S(1)} %copy-done.62), channel_id=1, source_target_pairs={{2,0},{4,2},{6,4},{7,6},{5,7},{3,5},{1,3},{0,1},{10,8},{12,10},{14... | collective-permute-start | bytes 2654216 | tf_op jit(solution)/shard_map/ppermute | solution.py:68
  107.1 45.6 %collective-permute-start.26 = (bf16[384,1536]{1,0:T(8,128)(2,1)S(1)}, bf16[384,1536]{1,0:T(8,128)(2,1)}, u32[]{:S(2)}, u32[]{:S(2)}) collective-permute-start(bf16[384,1536]{1,0:T(8,128)(2,1)S(1)} %bitcast.377), channel_id=1, source_target_pairs={{0,8},{8,0},{16,24},{24,16},{1,9},{9,1},{17,25},{25,17},{2,10},{10... | collective-permute-start | bytes 3538952 | tf_op jit(solution)/shard_map/ppermute | solution.py:168
  112.8 12.3 %collective-permute-start.42 = (bf16[288,768]{1,0:T(8,128)(2,1)}, bf16[288,768]{1,0:T(8,128)(2,1)}, u32[]{:S(2)}, u32[]{:S(2)}) collective-permute-start(bf16[288,768]{1,0:T(8,128)(2,1)} %collective-permute-done.40), channel_id=1, source_target_pairs={{0,2},{2,4},{4,6},{6,7},{7,5},{5,3},{3,1},{1,0},{8,10},{10,12},{12... | collective-permute-start | bytes 1327112 | tf_op jit(solution)/shard_map/ppermute | solution.py:67
  115.3 26.8 %collective-permute-start.53 = (bf16[256,1536]{1,0:T(8,128)(2,1)}, bf16[256,1536]{1,0:T(8,128)(2,1)S(1)}, u32[]{:S(2)}, u32[]{:S(2)}) collective-permute-start(bf16[256,1536]{1,0:T(8,128)(2,1)} %collective-permute-done.52), channel_id=1, source_target_pairs={{0,8},{8,0},{16,24},{24,16},{1,9},{9,1},{17,25},{25,17},{2,10},{10... | collective-permute-start | bytes 2359304 | tf_op jit(solution)/shard_map/ppermute | solution.py:168
  125.1 23.2 %collective-permute-start.2 = (bf16[256,1536]{1,0:T(8,128)(2,1)}, bf16[256,1536]{1,0:T(8,128)(2,1)}, u32[]{:S(2)}, u32[]{:S(2)}) collective-permute-start(bf16[256,1536]{1,0:T(8,128)(2,1)} %collective-permute-done.1), channel_id=1, source_target_pairs={{0,8},{8,0},{16,24},{24,16},{1,9},{9,1},{17,25},{25,17},{2,10},{10... | collective-permute-start | bytes 2359304 | tf_op jit(solution)/shard_map/ppermute | solution.py:168
  125.1 12.7 %collective-permute-start.43 = (bf16[288,768]{1,0:T(8,128)(2,1)S(1)}, bf16[288,768]{1,0:T(8,128)(2,1)}, u32[]{:S(2)}, u32[]{:S(2)}) collective-permute-start(bf16[288,768]{1,0:T(8,128)(2,1)S(1)} %collective-permute-done.41), channel_id=1, source_target_pairs={{2,0},{4,2},{6,4},{7,6},{5,7},{3,5},{1,3},{0,1},{10,8},{12,10},{14... | collective-permute-start | bytes 1327112 | tf_op jit(solution)/shard_map/ppermute | solution.py:68
  137.8 27.7 %collective-permute-start.27 = (bf16[384,1536]{1,0:T(8,128)(2,1)S(1)}, bf16[384,1536]{1,0:T(8,128)(2,1)}, u32[]{:S(2)}, u32[]{:S(2)}) collective-permute-start(bf16[384,1536]{1,0:T(8,128)(2,1)S(1)} %bitcast.378), channel_id=1, source_target_pairs={{0,16},{8,24},{16,0},{24,8},{1,17},{9,25},{17,1},{25,9},{2,18},{10... | collective-permute-start | bytes 3538952 | tf_op jit(solution)/shard_map/ppermute | solution.py:168
  142.1 27.3 %collective-permute-start.21 = (bf16[384,640]{1,0:T(8,128)(2,1)}, bf16[384,640]{1,0:T(8,128)(2,1)}, u32[]{:S(2)}, u32[]{:S(2)}) collective-permute-start(bf16[384,640]{1,0:T(8,128)(2,1)} %pad_maximum_fusion.12), channel_id=1, source_target_pairs={{0,8},{8,0},{16,24},{24,16},{1,9},{9,1},{17,25},{25,17},{2,10},{10... | collective-permute-start | bytes 1474568 | tf_op jit(solution)/shard_map/ppermute | solution.py:168
  147.8 22.2 %collective-permute-start.20 = (bf16[384,640]{1,0:T(8,128)(2,1)}, bf16[384,640]{1,0:T(8,128)(2,1)S(1)}, u32[]{:S(2)}, u32[]{:S(2)}) collective-permute-start(bf16[384,640]{1,0:T(8,128)(2,1)} %pad_maximum_fusion.10), channel_id=1, source_target_pairs={{0,8},{8,0},{16,24},{24,16},{1,9},{9,1},{17,25},{25,17},{2,10},{10... | collective-permute-start | bytes 1474568 | tf_op jit(solution)/shard_map/ppermute | solution.py:168
  148.3 66.9 %collective-permute-start.31 = (bf16[288,1536]{1,0:T(8,128)(2,1)}, bf16[288,1536]{1,0:T(8,128)(2,1)}, u32[]{:S(2)}, u32[]{:S(2)}) collective-permute-start(bf16[288,1536]{1,0:T(8,128)(2,1)} %copy-done.61), channel_id=1, source_target_pairs={{0,2},{2,4},{4,6},{6,7},{7,5},{5,3},{3,1},{1,0},{8,10},{10,12},{12... | collective-permute-start | bytes 2654216 | tf_op jit(solution)/shard_map/ppermute | solution.py:67
  152.8 64.5 %collective-permute-start.32 = (bf16[288,1536]{1,0:T(8,128)(2,1)}, bf16[288,1536]{1,0:T(8,128)(2,1)}, u32[]{:S(2)}, u32[]{:S(2)}) collective-permute-start(bf16[288,1536]{1,0:T(8,128)(2,1)} %collective-permute-done.30), channel_id=1, source_target_pairs={{2,0},{4,2},{6,4},{7,6},{5,7},{3,5},{1,3},{0,1},{10,8},{12,10},{14... | collective-permute-start | bytes 2654216 | tf_op jit(solution)/shard_map/ppermute | solution.py:68
  165.5 18.7 %collective-permute-start.44 = (bf16[288,768]{1,0:T(8,128)(2,1)}, bf16[288,768]{1,0:T(8,128)(2,1)S(1)}, u32[]{:S(2)}, u32[]{:S(2)}) collective-permute-start(bf16[288,768]{1,0:T(8,128)(2,1)} %collective-permute-done.42), channel_id=1, source_target_pairs={{0,2},{2,4},{4,6},{6,7},{7,5},{5,3},{3,1},{1,0},{8,10},{10,12},{12... | collective-permute-start | bytes 1327112 | tf_op jit(solution)/shard_map/ppermute | solution.py:67
  169.4 17.7 %collective-permute-start.45 = (bf16[288,768]{1,0:T(8,128)(2,1)}, bf16[288,768]{1,0:T(8,128)(2,1)}, u32[]{:S(2)}, u32[]{:S(2)}) collective-permute-start(bf16[288,768]{1,0:T(8,128)(2,1)} %collective-permute-done.43), channel_id=1, source_target_pairs={{2,0},{4,2},{6,4},{7,6},{5,7},{3,5},{1,3},{0,1},{10,8},{12,10},{14... | collective-permute-start | bytes 1327112 | tf_op jit(solution)/shard_map/ppermute | solution.py:68
  170.0 71.4 %collective-permute-start.28 = (bf16[384,1536]{1,0:T(8,128)(2,1)}, bf16[384,1536]{1,0:T(8,128)(2,1)}, u32[]{:S(2)}, u32[]{:S(2)}) collective-permute-start(bf16[384,1536]{1,0:T(8,128)(2,1)} %collective-permute-done.27), channel_id=1, source_target_pairs={{0,8},{8,0},{16,24},{24,16},{1,9},{9,1},{17,25},{25,17},{2,10},{10... | collective-permute-start | bytes 3538952 | tf_op jit(solution)/shard_map/ppermute | solution.py:168
  184.2 37.9 %collective-permute-start.22 = (bf16[1024,256]{0,1:T(8,128)(2,1)S(1)}, bf16[1024,256]{0,1:T(8,128)(2,1)S(1)}, u32[]{:S(2)}, u32[]{:S(2)}) collective-permute-start(bf16[1024,256]{0,1:T(8,128)(2,1)S(1)} %copy.143), channel_id=1, source_target_pairs={{0,1},{1,2},{2,3},{3,4},{4,5},{5,6},{6,7},{8,9},{9,10},{10,11},{11... | collective-permute-start | bytes 1572872 | tf_op jit(solution)/shard_map/ppermute | solution.py:486
  215.1 41.6 %collective-permute-start.33 = (bf16[288,1536]{1,0:T(8,128)(2,1)}, bf16[288,1536]{1,0:T(8,128)(2,1)}, u32[]{:S(2)}, u32[]{:S(2)}) collective-permute-start(bf16[288,1536]{1,0:T(8,128)(2,1)} %collective-permute-done.31), channel_id=1, source_target_pairs={{0,2},{2,4},{4,6},{6,7},{7,5},{5,3},{3,1},{1,0},{8,10},{10,12},{12... | collective-permute-start | bytes 2654216 | tf_op jit(solution)/shard_map/ppermute | solution.py:67
  217.3 46.2 %collective-permute-start.34 = (bf16[288,1536]{1,0:T(8,128)(2,1)}, bf16[288,1536]{1,0:T(8,128)(2,1)}, u32[]{:S(2)}, u32[]{:S(2)}) collective-permute-start(bf16[288,1536]{1,0:T(8,128)(2,1)} %collective-permute-done.32), channel_id=1, source_target_pairs={{2,0},{4,2},{6,4},{7,6},{5,7},{3,5},{1,3},{0,1},{10,8},{12,10},{14... | collective-permute-start | bytes 2654216 | tf_op jit(solution)/shard_map/ppermute | solution.py:68
  254.5 20.1 %collective-permute-start.38 = (bf16[256,1536]{1,0:T(8,128)(2,1)S(1)}, bf16[256,1536]{1,0:T(8,128)(2,1)S(1)}, u32[]{:S(2)}, u32[]{:S(2)}) collective-permute-start(bf16[256,1536]{1,0:T(8,128)(2,1)S(1)} %multiply_convert_fusion), channel_id=1, source_target_pairs={{0,16},{8,24},{16,0},{24,8},{1,17},{9,25},{17,1},{25,9},{2,18},{10... | collective-permute-start | bytes 2359304 | tf_op jit(solution)/shard_map/ppermute | solution.py:168
  256.7 21.9 %collective-permute-start.37 = (bf16[256,1536]{1,0:T(8,128)(2,1)S(1)}, bf16[256,1536]{1,0:T(8,128)(2,1)S(1)}, u32[]{:S(2)}, u32[]{:S(2)}) collective-permute-start(bf16[256,1536]{1,0:T(8,128)(2,1)S(1)} %multiply_convert_fusion), channel_id=1, source_target_pairs={{0,8},{8,0},{16,24},{24,16},{1,9},{9,1},{17,25},{25,17},{2,10},{10... | collective-permute-start | bytes 2359304 | tf_op jit(solution)/shard_map/ppermute | solution.py:168
  257.8 16.9 %collective-permute-start.35 = (bf16[144,1536]{1,0:T(8,128)(2,1)S(1)}, bf16[144,1536]{1,0:T(8,128)(2,1)S(1)}, u32[]{:S(2)}, u32[]{:S(2)}) collective-permute-start(bf16[144,1536]{1,0:T(8,128)(2,1)S(1)} %slice.456), channel_id=1, source_target_pairs={{0,2},{2,4},{4,6},{6,7},{7,5},{5,3},{3,1},{1,0},{8,10},{10,12},{12... | collective-permute-start | bytes 1327112 | tf_op jit(solution)/shard_map/ppermute | solution.py:75
  264.6 13.2 %collective-permute-start.36 = (bf16[144,1536]{1,0:T(8,128)(2,1)S(1)}, bf16[144,1536]{1,0:T(8,128)(2,1)S(1)}, u32[]{:S(2)}, u32[]{:S(2)}) collective-permute-start(bf16[144,1536]{1,0:T(8,128)(2,1)S(1)} %slice.457), channel_id=1, source_target_pairs={{2,0},{4,2},{6,4},{7,6},{5,7},{3,5},{1,3},{0,1},{10,8},{12,10},{14... | collective-permute-start | bytes 1327112 | tf_op jit(solution)/shard_map/ppermute | solution.py:76
  315.8 53.9 %collective-permute-start.55 = (bf16[256,1536]{1,0:T(8,128)(2,1)}, bf16[256,1536]{1,0:T(8,128)(2,1)}, u32[]{:S(2)}, u32[]{:S(2)}) collective-permute-start(bf16[256,1536]{1,0:T(8,128)(2,1)} %get-tuple-element.83), channel_id=1, source_target_pairs={{0,8},{8,0},{16,24},{24,16},{1,9},{9,1},{17,25},{25,17},{2,10},{10... | collective-permute-start | bytes 2359304 | tf_op jit(solution)/shard_map/ppermute | solution.py:168
  315.8 88.0 %collective-permute-start.54 = (bf16[256,1536]{1,0:T(8,128)(2,1)}, bf16[256,1536]{1,0:T(8,128)(2,1)S(1)}, u32[]{:S(2)}, u32[]{:S(2)}) collective-permute-start(bf16[256,1536]{1,0:T(8,128)(2,1)} %get-tuple-element.82), channel_id=1, source_target_pairs={{0,8},{8,0},{16,24},{24,16},{1,9},{9,1},{17,25},{25,17},{2,10},{10... | collective-permute-start | bytes 2359304 | tf_op jit(solution)/shard_map/ppermute | solution.py:168
  322.6 50.6 %collective-permute-start.49 = (bf16[256,1536]{1,0:T(8,128)(2,1)}, bf16[256,1536]{1,0:T(8,128)(2,1)}, u32[]{:S(2)}, u32[]{:S(2)}) collective-permute-start(bf16[256,1536]{1,0:T(8,128)(2,1)} %get-tuple-element.85), channel_id=1, source_target_pairs={{0,8},{8,0},{16,24},{24,16},{1,9},{9,1},{17,25},{25,17},{2,10},{10... | collective-permute-start | bytes 2359304 | tf_op jit(solution)/shard_map/ppermute | solution.py:168
  330.8 13.3 %collective-permute-start.94 = (bf16[144,768]{1,0:T(8,128)(2,1)S(1)}, bf16[144,768]{1,0:T(8,128)(2,1)S(1)}, u32[]{:S(2)}, u32[]{:S(2)}) collective-permute-start(bf16[144,768]{1,0:T(8,128)(2,1)S(1)} %get-tuple-element.78), channel_id=1, source_target_pairs={{0,2},{2,4},{4,6},{6,7},{7,5},{5,3},{3,1},{1,0},{8,10},{10,12},{12... | collective-permute-start | bytes 663560 | tf_op jit(solution)/shard_map/ppermute | solution.py:93
  358.6 17.7 %collective-permute-start.99 = (bf16[288,768]{1,0:T(8,128)(2,1)S(1)}, bf16[288,768]{1,0:T(8,128)(2,1)S(1)}, u32[]{:S(2)}, u32[]{:S(2)}) collective-permute-start(bf16[288,768]{1,0:T(8,128)(2,1)S(1)} %pad_maximum_fusion.17), channel_id=1, source_target_pairs={{2,0},{4,2},{6,4},{7,6},{5,7},{3,5},{1,3},{0,1},{10,8},{12,10},{14... | collective-permute-start | bytes 1327112 | tf_op jit(solution)/shard_map/ppermute | solution.py:111
  368.3 32.7 %collective-permute-start.87 = (bf16[288,1536]{1,0:T(8,128)(2,1)S(1)}, bf16[288,1536]{1,0:T(8,128)(2,1)S(1)}, u32[]{:S(2)}, u32[]{:S(2)}) collective-permute-start(bf16[288,1536]{1,0:T(8,128)(2,1)S(1)} %pad_maximum_fusion.6), channel_id=1, source_target_pairs={{0,2},{2,4},{4,6},{6,7},{7,5},{5,3},{3,1},{1,0},{8,10},{10,12},{12... | collective-permute-start | bytes 2654216 | tf_op jit(solution)/shard_map/ppermute | solution.py:103
  369.8 28.6 %collective-permute-start.96 = (bf16[288,768]{1,0:T(8,128)(2,1)S(1)}, bf16[288,768]{1,0:T(8,128)(2,1)S(1)}, u32[]{:S(2)}, u32[]{:S(2)}) collective-permute-start(bf16[288,768]{1,0:T(8,128)(2,1)S(1)} %fusion.71), channel_id=1, source_target_pairs={{0,2},{2,4},{4,6},{6,7},{7,5},{5,3},{3,1},{1,0},{8,10},{10,12},{12... | collective-permute-start | bytes 1327112 | tf_op jit(solution)/shard_map/ppermute | solution.py:103
  373.2 32.0 %collective-permute-start.56 = (bf16[256,1536]{1,0:T(8,128)(2,1)S(1)}, bf16[256,1536]{1,0:T(8,128)(2,1)S(1)}, u32[]{:S(2)}, u32[]{:S(2)}) collective-permute-start(bf16[256,1536]{1,0:T(8,128)(2,1)S(1)} %add_convert_fusion), channel_id=1, source_target_pairs={{0,16},{8,24},{16,0},{24,8},{1,17},{9,25},{17,1},{25,9},{2,18},{10... | collective-permute-start | bytes 2359304 | tf_op jit(solution)/shard_map/ppermute | solution.py:168
  376.3 30.4 %collective-permute-start.48 = (bf16[256,1536]{1,0:T(8,128)(2,1)S(1)}, bf16[256,1536]{1,0:T(8,128)(2,1)S(1)}, u32[]{:S(2)}, u32[]{:S(2)}) collective-permute-start(bf16[256,1536]{1,0:T(8,128)(2,1)S(1)} %copy-done.66), channel_id=1, source_target_pairs={{0,8},{8,0},{16,24},{24,16},{1,9},{9,1},{17,25},{25,17},{2,10},{10... | collective-permute-start | bytes 2359304 | tf_op jit(solution)/shard_map/ppermute | solution.py:168
  398.3 66.5 %collective-permute-start.91 = (bf16[288,1536]{1,0:T(8,128)(2,1)}, bf16[288,1536]{1,0:T(8,128)(2,1)}, u32[]{:S(2)}, u32[]{:S(2)}) collective-permute-start(bf16[288,1536]{1,0:T(8,128)(2,1)} %pad_maximum_fusion.7), channel_id=1, source_target_pairs={{2,0},{4,2},{6,4},{7,6},{5,7},{3,5},{1,3},{0,1},{10,8},{12,10},{14... | collective-permute-start | bytes 2654216 | tf_op jit(solution)/shard_map/ppermute | solution.py:111
  401.0 16.9 %collective-permute-start.50 = (bf16[256,1536]{1,0:T(8,128)(2,1)S(1)}, bf16[256,1536]{1,0:T(8,128)(2,1)S(1)}, u32[]{:S(2)}, u32[]{:S(2)}) collective-permute-start(bf16[256,1536]{1,0:T(8,128)(2,1)S(1)} %add_convert_fusion.2), channel_id=1, source_target_pairs={{0,16},{8,24},{16,0},{24,8},{1,17},{9,25},{17,1},{25,9},{2,18},{10... | collective-permute-start | bytes 2359304 | tf_op jit(solution)/shard_map/ppermute | solution.py:168
  403.8 23.8 %collective-permute-start.100 = (bf16[288,768]{1,0:T(8,128)(2,1)S(1)}, bf16[288,768]{1,0:T(8,128)(2,1)S(1)}, u32[]{:S(2)}, u32[]{:S(2)}) collective-permute-start(bf16[288,768]{1,0:T(8,128)(2,1)S(1)} %get-tuple-element.75), channel_id=1, source_target_pairs={{2,0},{4,2},{6,4},{7,6},{5,7},{3,5},{1,3},{0,1},{10,8},{12,10},{14... | collective-permute-start | bytes 1327112 | tf_op jit(solution)/shard_map/ppermute | solution.py:111
  405.2 53.4 %collective-permute-start.97 = (bf16[288,768]{1,0:T(8,128)(2,1)}, bf16[288,768]{1,0:T(8,128)(2,1)}, u32[]{:S(2)}, u32[]{:S(2)}) collective-permute-start(bf16[288,768]{1,0:T(8,128)(2,1)} %get-tuple-element.74), channel_id=1, source_target_pairs={{0,2},{2,4},{4,6},{6,7},{7,5},{5,3},{3,1},{1,0},{8,10},{10,12},{12... | collective-permute-start | bytes 1327112 | tf_op jit(solution)/shard_map/ppermute | solution.py:103
  431.3 33.6 %collective-permute-start.88 = (bf16[288,1536]{1,0:T(8,128)(2,1)}, bf16[288,1536]{1,0:T(8,128)(2,1)}, u32[]{:S(2)}, u32[]{:S(2)}) collective-permute-start(bf16[288,1536]{1,0:T(8,128)(2,1)} %fusion.55), channel_id=1, source_target_pairs={{0,2},{2,4},{4,6},{6,7},{7,5},{5,3},{3,1},{1,0},{8,10},{10,12},{12... | collective-permute-start | bytes 2654216 | tf_op jit(solution)/shard_map/ppermute | solution.py:103
  435.6 23.0 %collective-permute-start.101 = (bf16[288,768]{1,0:T(8,128)(2,1)}, bf16[288,768]{1,0:T(8,128)(2,1)S(1)}, u32[]{:S(2)}, u32[]{:S(2)}) collective-permute-start(bf16[288,768]{1,0:T(8,128)(2,1)} %fusion.70), channel_id=1, source_target_pairs={{2,0},{4,2},{6,4},{7,6},{5,7},{3,5},{1,3},{0,1},{10,8},{12,10},{14... | collective-permute-start | bytes 1327112 | tf_op jit(solution)/shard_map/ppermute | solution.py:111
  436.8 27.5 %collective-permute-start.76 = (bf16[256,1536]{1,0:T(8,128)(2,1)}, bf16[256,1536]{1,0:T(8,128)(2,1)}, u32[]{:S(2)}, u32[]{:S(2)}) collective-permute-start(bf16[256,1536]{1,0:T(8,128)(2,1)} %get-tuple-element.62), channel_id=1, source_target_pairs={{0,16},{8,24},{16,0},{24,8},{1,17},{9,25},{17,1},{25,9},{2,18},{10... | collective-permute-start | bytes 2359304 | tf_op jit(solution)/shard_map/ppermute | solution.py:168
  458.6 18.5 %collective-permute-start.75 = (bf16[256,1536]{1,0:T(8,128)(2,1)}, bf16[256,1536]{1,0:T(8,128)(2,1)}, u32[]{:S(2)}, u32[]{:S(2)}) collective-permute-start(bf16[256,1536]{1,0:T(8,128)(2,1)} %get-tuple-element.62), channel_id=1, source_target_pairs={{0,8},{8,0},{16,24},{24,16},{1,9},{9,1},{17,25},{25,17},{2,10},{10... | collective-permute-start | bytes 2359304 | tf_op jit(solution)/shard_map/ppermute | solution.py:168
  458.6 16.5 %collective-permute-start.60 = (bf16[1024,256]{1,0:T(8,128)(2,1)}, bf16[1024,256]{1,0:T(8,128)(2,1)}, u32[]{:S(2)}, u32[]{:S(2)}) collective-permute-start(bf16[1024,256]{1,0:T(8,128)(2,1)} %slice.565), channel_id=1, source_target_pairs={{1,0},{2,1},{3,2},{4,3},{5,4},{6,5},{7,6},{9,8},{10,9},{11,10},{12... | collective-permute-start | bytes 1572872 | tf_op jit(solution)/shard_map/ppermute | solution.py:546
  464.3 12.9 %collective-permute-start.77 = (bf16[256,1536]{1,0:T(8,128)(2,1)}, bf16[256,1536]{1,0:T(8,128)(2,1)S(1)}, u32[]{:S(2)}, u32[]{:S(2)}) collective-permute-start(bf16[256,1536]{1,0:T(8,128)(2,1)} %collective-permute-done.76), channel_id=1, source_target_pairs={{0,8},{8,0},{16,24},{24,16},{1,9},{9,1},{17,25},{25,17},{2,10},{10... | collective-permute-start | bytes 2359304 | tf_op jit(solution)/shard_map/ppermute | solution.py:168
  468.4 36.0 %collective-permute-start.92 = (bf16[288,1536]{1,0:T(8,128)(2,1)}, bf16[288,1536]{1,0:T(8,128)(2,1)}, u32[]{:S(2)}, u32[]{:S(2)}) collective-permute-start(bf16[288,1536]{1,0:T(8,128)(2,1)} %get-tuple-element.67), channel_id=1, source_target_pairs={{2,0},{4,2},{6,4},{7,6},{5,7},{3,5},{1,3},{0,1},{10,8},{12,10},{14... | collective-permute-start | bytes 2654216 | tf_op jit(solution)/shard_map/ppermute | solution.py:111
  488.5 39.9 %collective-permute-start.61 = (bf16[1024,640]{0,1:T(8,128)(2,1)S(1)}, bf16[1024,640]{0,1:T(8,128)(2,1)}, u32[]{:S(2)}, u32[]{:S(2)}) collective-permute-start(bf16[1024,640]{0,1:T(8,128)(2,1)S(1)} %fusion.20), channel_id=1, source_target_pairs={{0,16},{8,24},{16,0},{24,8},{1,17},{9,25},{17,1},{25,9},{2,18},{10... | collective-permute-start | bytes 3932168 | tf_op jit(solution)/shard_map/ppermute | solution.py:168
  502.3 44.2 %collective-permute-start.89 = (bf16[288,1536]{1,0:T(8,128)(2,1)}, bf16[288,1536]{1,0:T(8,128)(2,1)}, u32[]{:S(2)}, u32[]{:S(2)}) collective-permute-start(bf16[288,1536]{1,0:T(8,128)(2,1)} %get-tuple-element.66), channel_id=1, source_target_pairs={{0,2},{2,4},{4,6},{6,7},{7,5},{5,3},{3,1},{1,0},{8,10},{10,12},{12... | collective-permute-start | bytes 2654216 | tf_op jit(solution)/shard_map/ppermute | solution.py:103
  502.6 31.1 %collective-permute-start.63 = (bf16[1024,640]{0,1:T(8,128)(2,1)S(1)}, bf16[1024,640]{0,1:T(8,128)(2,1)S(1)}, u32[]{:S(2)}, u32[]{:S(2)}) collective-permute-start(bf16[1024,640]{0,1:T(8,128)(2,1)S(1)} %fusion.20), channel_id=1, source_target_pairs={{0,8},{8,0},{16,24},{24,16},{1,9},{9,1},{17,25},{25,17},{2,10},{10... | collective-permute-start | bytes 3932168 | tf_op jit(solution)/shard_map/ppermute | solution.py:168
  504.5 22.3 %collective-permute-start.80 = (bf16[96,768]{1,0:T(8,128)(2,1)S(1)}, bf16[96,768]{1,0:T(8,128)(2,1)S(1)}, u32[]{:S(2)}, u32[]{:S(2)}) collective-permute-start(bf16[96,768]{1,0:T(8,128)(2,1)S(1)} %fusion.107), channel_id=1, source_target_pairs={{0,2},{2,4},{4,6},{6,7},{7,5},{5,3},{3,1},{1,0},{8,10},{10,12},{12... | collective-permute-start | bytes 442376 | tf_op jit(solution)/shard_map/ppermute | solution.py:103
  509.0 37.5 %collective-permute-start.93 = (bf16[288,1536]{1,0:T(8,128)(2,1)}, bf16[288,1536]{1,0:T(8,128)(2,1)}, u32[]{:S(2)}, u32[]{:S(2)}) collective-permute-start(bf16[288,1536]{1,0:T(8,128)(2,1)} %fusion.54), channel_id=1, source_target_pairs={{2,0},{4,2},{6,4},{7,6},{5,7},{3,5},{1,3},{0,1},{10,8},{12,10},{14... | collective-permute-start | bytes 2654216 | tf_op jit(solution)/shard_map/ppermute | solution.py:111
  533.7 38.8 %collective-permute-start.62 = (bf16[1024,640]{0,1:T(8,128)(2,1)}, bf16[1024,640]{0,1:T(8,128)(2,1)}, u32[]{:S(2)}, u32[]{:S(2)}) collective-permute-start(bf16[1024,640]{0,1:T(8,128)(2,1)} %collective-permute-done.61), channel_id=1, source_target_pairs={{0,8},{8,0},{16,24},{24,16},{1,9},{9,1},{17,25},{25,17},{2,10},{10... | collective-permute-start | bytes 3932168 | tf_op jit(solution)/shard_map/ppermute | solution.py:168
  590.4 15.7 %collective-permute-start.68 = (bf16[96,896]{1,0:T(8,128)(2,1)}, bf16[96,896]{1,0:T(8,128)(2,1)S(1)}, u32[]{:S(2)}, u32[]{:S(2)}) collective-permute-start(bf16[96,896]{1,0:T(8,128)(2,1)} %pad_maximum_fusion.18), channel_id=1, source_target_pairs={{0,2},{2,4},{4,6},{6,7},{7,5},{5,3},{3,1},{1,0},{8,10},{10,12},{12... | collective-permute-start | bytes 516104 | tf_op jit(solution)/shard_map/ppermute | solution.py:103
  592.6 16.3 %collective-permute-start.72 = (bf16[96,896]{1,0:T(8,128)(2,1)}, bf16[96,896]{1,0:T(8,128)(2,1)S(1)}, u32[]{:S(2)}, u32[]{:S(2)}) collective-permute-start(bf16[96,896]{1,0:T(8,128)(2,1)} %pad_maximum_fusion.19), channel_id=1, source_target_pairs={{2,0},{4,2},{6,4},{7,6},{5,7},{3,5},{1,3},{0,1},{10,8},{12,10},{14... | collective-permute-start | bytes 516104 | tf_op jit(solution)/shard_map/ppermute | solution.py:111
  601.9 16.9 %all-to-all-start.1 = ((f32[32,1,96]{2,1,0:T(1,128)}), f32[32,1,96]{2,1,0:T(1,128)S(1)}, u32[]{:S(2)}, u32[]{:S(2)}) async-start(f32[32,1,96]{2,1,0:T(1,128)} %bitcast.65), calls=%async_computation.1 | async-start | bytes 32768 | tf_op jit(solution)/shard_map/all_to_all | solution.py:574
  (124 other events, 1294.4 us)

commit v2 on v1

--- a/solution.py
+++ b/solution.py
@@ -316,6 +316,1031 @@
         ),
         name="attend_back",
     )(queries, grads, kv, kv_turned, key_ids, query_ids, lse_rows)
+
+
+def remote(source, target, send, recv, where):
+    return pltpu.make_async_remote_copy(
+        src_ref=source,
+        dst_ref=target,
+        send_sem=send,
+        recv_sem=recv,
+        device_id=where,
+        device_id_type=pl.DeviceIdType.MESH,
+    )
+
+
+class Ring:
+    def __init__(self, count, view, send, recv):
+        me = lax.axis_index("seq")
+        odd = lax.rem(me, 2)
+        self.count = count
+        self.view = view
+        self.send = send
+        self.recv = recv
+        self.place = (1 - odd) * (me // 2) + odd * (count - 1 - me // 2)
+        self.ahead = {"seq": self.shard(1)}
+        self.behind = {"seq": self.shard(-1)}
+        self.copies = []
+
+    def shard(self, offset):
+        place = lax.rem(self.place + offset + self.count, self.count)
+        upper = place // (self.count // 2)
+        return (1 - upper) * 2 * place + upper * (2 * (self.count - 1 - place) + 1)
+
+    def pair(self, offset, step):
+        last = step == self.count // 2
+        views = [
+            self.view(self.shard(-offset), 0 if last else None),
+            self.view(self.shard(offset), 1 if last else None),
+        ]
+        return [
+            remote(view, view, self.send.at[i, step - 1], self.recv.at[i, step - 1], where)
+            for i, (view, where) in enumerate(zip(views, (self.ahead, self.behind)))
+        ]
+
+    def start(self, step):
+        for copy in self.pair(step - 1, step):
+            copy.start()
+            self.copies.append(copy)
+
+    def arrive(self, step):
+        for copy in self.pair(step, step):
+            copy.wait_recv()
+
+    def finish(self):
+        for copy in self.copies:
+            copy.wait_send()
+
+
+def forward_kernel(
+    count,
+    tokens,
+    cotangent,
+    gains,
+    qkv_shard,
+    out_shard,
+    gateup_shard,
+    down_shard,
+    order,
+    key_ids,
+    query_ids,
+    resid,
+    normed_group,
+    grad_group,
+    gateup,
+    down,
+    features,
+    qkv_rows,
+    out_rows,
+    stream,
+    kv_both,
+    kv_turned,
+    lse,
+    mixed_group,
+    shuffle,
+    tokens_group,
+    normed,
+    weights,
+    projected,
+    mixed,
+    bias,
+    part_out,
+    part_in,
+    own_sem,
+    ring_send,
+    ring_recv,
+    head_send,
+    head_recv,
+    kv_send,
+    kv_recv,
+):
+    rows = tokens.shape[0]
+    group = 4 * rows
+    width = features.shape[1]
+    heads = width // HEAD_DIM
+    head = lax.axis_index("head")
+    me = lax.axis_index("seq")
+    mate = {"head": head + 1 - 2 * lax.rem(head, 2)}
+    across = {"head": lax.rem(head + 2, 4)}
+    band = pl.multiple_of(head * width, 128)
+
+    def quarter(ref, i):
+        return ref.at[pl.ds(i * rows, rows)]
+
+    copies = []
+
+    def send(index, source, target, where):
+        copy = remote(source, target, head_send.at[index], head_recv.at[index], where)
+        copy.start()
+        copies.append(copy)
+
+    def arrived(index, target, where):
+        remote(target, target, head_send.at[index], head_recv.at[index], where).wait_recv()
+
+    def qkv_view(shard, part):
+        first = pl.multiple_of(band + (shard // 2) * BLK, 32)
+        columns = pl.ds(pl.multiple_of(lax.rem(shard, 2) * (QKV // 2), 128), QKV // 2)
+        if part is None:
+            return weights.at[pl.ds(first, BLK), columns]
+        return weights.at[pl.ds(pl.multiple_of(first + part * (BLK // 2), 16), BLK // 2), columns]
+
+    def out_view(shard, part):
+        first = pl.multiple_of((shard // 2) * BLK, 32)
+        columns = pl.ds(pl.multiple_of(lax.rem(shard, 2) * (D // 2), 128), D // 2)
+        if part is None:
+            return out_rows.at[pl.ds(first, BLK), columns]
+        return out_rows.at[pl.ds(pl.multiple_of(first + part * (BLK // 2), 16), BLK // 2), columns]
+
+    def gateup_view(shard, part):
+        size = gateup.shape[1]
+        if part is None:
+            return gateup.at[shard]
+        return gateup.at[shard, pl.ds(part * (size // 2), size // 2)]
+
+    def down_view(shard, part):
+        if part is None:
+            return down.at[shard]
+        return down.at[shard, :, pl.ds(part * (BLK // 2), BLK // 2)]
+
+    rings = [
+        Ring(count, view, ring_send.at[i], ring_recv.at[i])
+        for i, view in enumerate((qkv_view, out_view, gateup_view, down_view))
+    ]
+    qkv_ring, out_ring, gateup_ring, down_ring = rings
+
+    barrier = pltpu.get_barrier_semaphore()
+    for where in (qkv_ring.ahead, qkv_ring.behind, mate, across):
+        pl.semaphore_signal(barrier, inc=1, device_id=where, device_id_type=pl.DeviceIdType.MESH)
+
+    @pl.when(me > 0)
+    def _():
+        pl.semaphore_signal(
+            barrier, inc=1, device_id={"seq": me - 1}, device_id_type=pl.DeviceIdType.MESH
+        )
+
+    pl.semaphore_wait(barrier, 5 - me // (count - 1))
+
+    own = [
+        pltpu.make_async_copy(gateup_shard, gateup.at[me], own_sem.at[0]),
+        pltpu.make_async_copy(down_shard, down.at[me], own_sem.at[1]),
+        pltpu.make_async_copy(cotangent, quarter(grad_group, 0), own_sem.at[2]),
+        pltpu.make_async_copy(qkv_shard, qkv_view(me, None), own_sem.at[3]),
+        pltpu.make_async_copy(out_shard, out_view(me, None), own_sem.at[4]),
+    ]
+    for copy in own:
+        copy.start()
+    own[3].wait()
+    qkv_ring.start(1)
+    own[0].wait()
+    own[1].wait()
+    gateup_ring.start(1)
+    down_ring.start(1)
+
+    def band_view(which, offset):
+        shard = qkv_ring.shard(offset)
+        first = pl.multiple_of(which * width + (shard // 2) * BLK, 32)
+        columns = pl.ds(pl.multiple_of(lax.rem(shard, 2) * (QKV // 2), 128), QKV // 2)
+        return weights.at[pl.ds(first, BLK), columns]
+
+    across_head = lax.rem(head + 2, 4)
+    offsets = [[0]] + [[-i, i] for i in range(1, count // 2)] + [[count // 2]]
+
+    def pass_across(step):
+        for offset in offsets[step]:
+            part = band_view(head, offset)
+            send(17 + offset % count, part, part, across)
+
+    def pass_on(step):
+        for offset in offsets[step]:
+            part = band_view(across_head, offset)
+            arrived(17 + offset % count, part, across)
+            send(17 + count + offset % count, part, part, mate)
+
+    pass_across(0)
+    send(0, tokens, quarter(tokens_group, 2), across)
+    send(1, tokens, quarter(tokens_group, 1), mate)
+
+    def norm_rows(source, i):
+        values = source[...].astype(full)
+        normed[pl.ds(i * rows, rows), :] = (
+            values * inverse_norm(values) * gains[0:1, :]
+        ).astype(low)
+
+    norm_rows(tokens, 0)
+    qkv_ring.arrive(1)
+    qkv_ring.start(2)
+    pass_across(1)
+    at = order[...]
+    owner = at // rows
+    flip = head - 2 * (owner // 2) * (head // 2) * 2 - 2 * lax.rem(owner, 2) * lax.rem(head, 2)
+    place = (owner + flip) * rows + lax.rem(at, rows)
+    for i in range(4):
+        shuffle[pl.ds(i * rows, rows), :] = jnp.where(
+            place[i * rows : (i + 1) * rows]
+            == lax.broadcasted_iota(jnp.int32, (rows, group), 1),
+            1.0,
+            0.0,
+        ).astype(low)
+    arrived(1, quarter(tokens_group, 1), mate)
+    norm_rows(quarter(tokens_group, 1), 1)
+    for step in range(2, count // 2):
+        qkv_ring.arrive(step)
+        qkv_ring.start(step + 1)
+        pass_across(step)
+        pass_on(step - 2)
+    arrived(0, quarter(tokens_group, 2), across)
+    send(2, quarter(tokens_group, 2), quarter(tokens_group, 3), mate)
+    norm_rows(quarter(tokens_group, 2), 2)
+    qkv_ring.arrive(count // 2)
+    pass_across(count // 2)
+    part = weights.at[pl.ds(band, width)]
+    send(5, part, part, mate)
+    own[4].wait()
+    out_ring.start(1)
+    own[2].wait()
+    send(8, quarter(grad_group, 0), quarter(grad_group, 2), across)
+    send(9, quarter(grad_group, 0), quarter(grad_group, 1), mate)
+    pass_on(count // 2 - 2)
+    arrived(2, quarter(tokens_group, 3), mate)
+    norm_rows(quarter(tokens_group, 3), 3)
+    features[...] = normed[:, pl.ds(band, width)]
+    qkv_rows[...] = weights[pl.ds(band, width), :]
+    pass_on(count // 2 - 1)
+    gateup_ring.arrive(1)
+    gateup_ring.start(2)
+    down_ring.arrive(1)
+    down_ring.start(2)
+    out_ring.arrive(1)
+    out_ring.start(2)
+    pass_on(count // 2)
+    mate_head = head + 1 - 2 * lax.rem(head, 2)
+    mate_band = pl.multiple_of(mate_head * width, 128)
+    arrived(5, weights.at[pl.ds(mate_band, width)], mate)
+    for offset in range(count):
+        arrived(17 + count + offset, band_view(3 - head, offset), mate)
+
+    key_values = pl.ds(width, 2 * HEAD_DIM)
+
+    def project(columns, target):
+        def step(i, carry):
+            here = pl.ds(pl.multiple_of(i * rows, rows), rows)
+            projected[here, target] = mul(normed[here, :], weights[:, columns], NN).astype(low)
+            return carry
+
+        lax.fori_loop(0, 4, step, 0)
+
+        def turn(i, carry):
+            here = pl.ds(pl.multiple_of(i * rows, rows), rows)
+            stream[here, target] = mul(shuffle[here, :], projected[:, target], NN).astype(low)
+            return carry
+
+        lax.fori_loop(0, 4, turn, 0)
+
+    project(pl.ds(QW, 2 * HEAD_DIM), key_values)
+    kv_both[pl.ds(group, group), :] = stream[:, key_values]
+    kv_copy = remote(
+        kv_both.at[pl.ds(group, group)],
+        kv_both.at[pl.ds(0, group)],
+        kv_send,
+        kv_recv,
+        {"seq": lax.rem(me + 1, count)},
+    )
+
+    @pl.when(me < count - 1)
+    def _():
+        kv_copy.start()
+
+    @pl.when(me == 0)
+    def _():
+        kv_both[pl.ds(0, group), :] = jnp.zeros((group, 2 * HEAD_DIM), low)
+
+    out_ring.arrive(2)
+    out_ring.start(3)
+    project(pl.ds(band, width), pl.ds(0, width))
+    for i in range(4, 8):
+        kv_turned[:, i * rows : (i + 1) * rows] = kv_both[i * rows : (i + 1) * rows, :].T
+
+    @pl.when(me > 0)
+    def _():
+        kv_copy.wait_recv()
+
+    for i in range(4):
+        kv_turned[:, i * rows : (i + 1) * rows] = kv_both[i * rows : (i + 1) * rows, :].T
+    out_ring.arrive(3)
+    out_ring.start(4)
+
+    def attend_tile(tile, carry):
+        start = pl.multiple_of(tile * QUERY_TILE, QUERY_TILE)
+        here = pl.ds(start, QUERY_TILE)
+        span = pl.ds(start, SPAN)
+        shape = (SPAN, QUERY_TILE)
+        key = lax.broadcasted_iota(jnp.int32, shape, 0)
+        query = lax.broadcasted_iota(jnp.int32, shape, 1)
+        same = key_ids[span, :] == query_ids[:, here]
+        allowed = same & (key > query) & (key <= query + WINDOW)
+        bias[...] = jnp.where(allowed, 0.0, neg_fill)
+
+        def attend_head(j, carry):
+            lanes = pl.ds(pl.multiple_of(j * HEAD_DIM, HEAD_DIM), HEAD_DIM)
+            scores = mul(kv_both[span, :HEAD_DIM], stream[here, lanes], NT)
+            scores = scores * HEAD_DIM ** (-0.5) + bias[...]
+            top = jnp.max(scores, axis=0, keepdims=True)
+            expo = jnp.exp(scores - top)
+            total = jnp.sum(expo, axis=0, keepdims=True)
+            out = mul(kv_turned[HEAD_DIM:, span], expo.astype(low), NN) / total
+            mixed[here, lanes] = out.T.astype(low)
+            lse[j, :, here] = top + jnp.log(total)
+            return carry
+
+        return lax.fori_loop(0, heads, attend_head, carry)
+
+    lax.fori_loop(0, group // QUERY_TILE, attend_tile, 0)
+
+    gateup_ring.arrive(2)
+    gateup_ring.start(3)
+    down_ring.arrive(2)
+    down_ring.start(3)
+
+    def turn_back(i, carry):
+        here = pl.ds(pl.multiple_of(i * rows, rows), rows)
+        mixed_group[here, :] = mul(shuffle[:, here], mixed[...], TN).astype(low)
+        return carry
+
+    lax.fori_loop(0, 4, turn_back, 0)
+    out_ring.arrive(4)
+
+    def projection(i):
+        return mul(mixed_group[i * rows : (i + 1) * rows, :], out_rows[...], NN)
+
+    part_out[0] = projection(3).astype(low)
+    send(10, part_out.at[0], part_in.at[0], mate)
+    part_out[1] = projection(1).astype(low)
+    send(11, part_out.at[1], part_in.at[1], mate)
+    resid[...] = projection(2)
+    arrived(10, part_in.at[0], mate)
+    part_out[2] = (resid[...] + part_in[0].astype(full)).astype(low)
+    send(12, part_out.at[2], part_in.at[2], across)
+    resid[...] = projection(0) + tokens[...].astype(full)
+    arrived(11, part_in.at[1], mate)
+    resid[...] += part_in[1].astype(full)
+    arrived(8, quarter(grad_group, 2), across)
+    send(13, quarter(grad_group, 2), quarter(grad_group, 3), mate)
+    arrived(12, part_in.at[2], across)
+    resid[...] += part_in[2].astype(full)
+    values = resid[...]
+    normed_group[pl.ds(0, rows), :] = (values * inverse_norm(values) * gains[1:2, :]).astype(low)
+    send(14, quarter(normed_group, 0), quarter(normed_group, 2), across)
+    send(15, quarter(normed_group, 0), quarter(normed_group, 1), mate)
+    gateup_ring.arrive(3)
+    gateup_ring.start(4)
+    down_ring.arrive(3)
+    down_ring.start(4)
+    arrived(14, quarter(normed_group, 2), across)
+    send(16, quarter(normed_group, 2), quarter(normed_group, 3), mate)
+    arrived(9, quarter(grad_group, 1), mate)
+    arrived(13, quarter(grad_group, 3), mate)
+    arrived(15, quarter(normed_group, 1), mate)
+    arrived(16, quarter(normed_group, 3), mate)
+    gateup_ring.arrive(4)
+    down_ring.arrive(4)
+    for ring in rings:
+        ring.finish()
+    for copy in copies:
+        copy.wait_send()
+
+    @pl.when(me < count - 1)
+    def _():
+        kv_copy.wait_send()
+
+
+def forward_section(tokens, cotangent, gains, shards, order, key_ids, query_ids, count):
+    rows = tokens.shape[0]
+    group = 4 * rows
+    width = QW // 4
+    steps = count // 2
+    qkv_shard, out_shard, gateup_shard, down_shard = shards
+    vmem = pl.BlockSpec(memory_space=pltpu.VMEM)
+    hbm = pl.BlockSpec(memory_space=pl.ANY)
+    outs = [
+        ((rows, D), full, vmem),
+        ((group, D), low, vmem),
+        ((group, D), low, hbm),
+        ((count,) + gateup_shard.shape, low, hbm),
+        ((count,) + down_shard.shape, low, hbm),
+        ((group, width), low, vmem),
+        ((width, QKV), low, vmem),
+        ((width, D), low, vmem),
+        ((group, width + 2 * HEAD_DIM), low, vmem),
+        ((2 * group, 2 * HEAD_DIM), low, vmem),
+        ((2 * HEAD_DIM, 2 * group), low, vmem),
+        ((width // HEAD_DIM, 1, group), full, vmem),
+        ((group, width), low, vmem),
+        ((group, group), low, vmem),
+    ]
+    dma = pltpu.SemaphoreType.DMA
+    return pl.pallas_call(
+        functools.partial(forward_kernel, count),
+        in_specs=[vmem, hbm, vmem, hbm, hbm, hbm, hbm, vmem, vmem, vmem],
+        out_specs=[spec for _, _, spec in outs],
+        out_shape=[jax.ShapeDtypeStruct(shape, kind) for shape, kind, _ in outs],
+        scratch_shapes=[
+            pltpu.VMEM((group, D), low),
+            pltpu.VMEM((group, D), low),
+            pltpu.VMEM((D, QKV), low),
+            pltpu.VMEM((group, width + 2 * HEAD_DIM), low),
+            pltpu.VMEM((group, width), low),
+            pltpu.VMEM((SPAN, QUERY_TILE), full),
+            pltpu.VMEM((3, rows, D), low),
+            pltpu.VMEM((3, rows, D), low),
+            dma((5,)),
+            dma((4, 2, steps)),
+            dma((4, 2, steps)),
+            dma((17 + 2 * count,)),
+            dma((17 + 2 * count,)),
+            dma,
+            dma,
+        ],
+        compiler_params=pltpu.CompilerParams(
+            collective_id=0, has_side_effects=True, vmem_limit_bytes=58 * 1024 * 1024
+        ),
+        name="forward_section",
+    )(
+        tokens,
+        cotangent,
+        gains,
+        qkv_shard,
+        out_shard,
+        gateup_shard,
+        down_shard,
+        order,
+        key_ids,
+        query_ids,
+    )
+
+
+class SumRing:
+    def __init__(self, count, view, first, buffers, send, recv):
+        self.ring = Ring(count, None, None, None)
+        self.steps = count // 2
+        self.view = view
+        self.first = first
+        self.buffers = buffers
+        self.rows = buffers.shape[2]
+        self.send = send
+        self.recv = recv
+        self.copies = []
+
+    def where(self, way):
+        return self.ring.behind if way else self.ring.ahead
+
+    def half(self, way):
+        return self.buffers.at[way, 0, pl.ds(way * (self.rows // 2), self.rows // 2)]
+
+    def copy(self, way, step, source, target):
+        return remote(source, target, self.send.at[way, step], self.recv.at[way, step], self.where(way))
+
+    def start(self):
+        shard = self.ring.shard(self.steps)
+        for way in range(2):
+            copy = self.copy(way, 0, self.first(shard, way), self.half(way))
+            copy.start()
+            self.copies.append(copy)
+
+    def arrived(self, way, step):
+        target = self.buffers.at[way, step] if step else self.half(way)
+        self.copy(way, step, target, target).wait_recv()
+
+    def step(self, step):
+        block = 48
+        for way in range(2):
+            self.arrived(way, step - 1)
+            offset = self.steps - step
+            local = self.view(self.ring.shard(-offset if way else offset))
+            buffer = self.buffers.at[way, step - 1]
+
+            def add(i, carry):
+                here = pl.ds(pl.multiple_of(i * block, 16), block)
+                buffer[here, :] = (local[here, :].astype(full) + buffer[here, :].astype(full)).astype(low)
+                return carry
+
+            def keep(i, carry):
+                here = pl.ds(pl.multiple_of(i * block, 16), block)
+                buffer[here, :] = local[here, :]
+                return carry
+
+            blocks = self.rows // block
+            if step > 1:
+                lax.fori_loop(0, blocks, add, 0)
+            else:
+                lax.fori_loop(way * (blocks // 2), (way + 1) * (blocks // 2), add, 0)
+                lax.fori_loop((1 - way) * (blocks // 2), (2 - way) * (blocks // 2), keep, 0)
+            copy = self.copy(way, step, buffer, self.buffers.at[way, step])
+            copy.start()
+            self.copies.append(copy)
+
+    def finish(self, out):
+        block = 48
+        last = self.steps - 1
+        for way in range(2):
+            self.arrived(way, last)
+        local = self.view(self.ring.shard(0))
+
+        def add(i, carry):
+            here = pl.ds(pl.multiple_of(i * block, 16), block)
+            out[here, :] = (
+                local[here, :].astype(full)
+                + self.buffers[0, last, here, :].astype(full)
+                + self.buffers[1, last, here, :].astype(full)
+            )
+            return carry
+
+        lax.fori_loop(0, self.rows // block, add, 0)
+        for copy in self.copies:
+            copy.wait_send()
+
+
+class StagedSumRing(SumRing):
+    def __init__(self, count, parts, buffers, held, terms, load, send, recv):
+        size = parts.shape[1] // 2
+        first = lambda shard, part: parts.at[shard, pl.ds(part * size, size)]
+        super().__init__(count, None, first, buffers, send, recv)
+        self.parts = parts
+        self.held = held
+        self.terms = terms
+        self.load = load
+        self.last = [None, None]
+
+    def fetch(self, way, offset):
+        shard = self.ring.shard(-offset if way else offset)
+        copy = pltpu.make_async_copy(
+            self.parts.at[shard], self.terms.at[way], self.load.at[1, way]
+        )
+        copy.start()
+        return copy
+
+    def start(self):
+        super().start()
+        self.fetched = [self.fetch(way, self.steps - 1) for way in range(2)]
+
+    def take(self, way, step):
+        self.arrived(way, step)
+        if self.last[way] is not None:
+            self.last[way].wait_send()
+        source, target = self.buffers.at[way, step], self.held.at[way]
+        if step == 0:
+            half = pl.ds(way * (self.rows // 2), self.rows // 2)
+            source, target = self.half(way), self.held.at[way, half]
+        copy = pltpu.make_async_copy(source, target, self.load.at[0, way])
+        copy.start()
+        return copy
+
+    def step(self, step):
+        block = 48
+        taken = [self.take(way, step - 1) for way in range(2)]
+        for way in range(2):
+            taken[way].wait()
+            self.fetched[way].wait()
+            held, terms = self.held.at[way], self.terms.at[way]
+
+            def add(i, carry):
+                here = pl.ds(pl.multiple_of(i * block, 16), block)
+                held[here, :] = (terms[here, :].astype(full) + held[here, :].astype(full)).astype(low)
+                return carry
+
+            def keep(i, carry):
+                here = pl.ds(pl.multiple_of(i * block, 16), block)
+                held[here, :] = terms[here, :]
+                return carry
+
+            blocks = self.rows // block
+            if step > 1:
+                lax.fori_loop(0, blocks, add, 0)
+            else:
+                lax.fori_loop(way * (blocks // 2), (way + 1) * (blocks // 2), add, 0)
+                lax.fori_loop((1 - way) * (blocks // 2), (2 - way) * (blocks // 2), keep, 0)
+            self.last[way] = self.copy(way, step, held, self.buffers.at[way, step])
+            self.last[way].start()
+            if step < self.steps - 1 or way == 0:
+                self.fetched[way] = self.fetch(way, self.steps - 1 - step)
+
+    def finish(self, out):
+        block = 48
+        taken = [self.take(way, self.steps - 1) for way in range(2)]
+        for copy in taken:
+            copy.wait()
+        self.fetched[0].wait()
+
+        def add(i, carry):
+            here = pl.ds(pl.multiple_of(i * block, 16), block)
+            out[here, :] = (
+                self.terms[0, here, :].astype(full)
+                + self.held[0, here, :].astype(full)
+                + self.held[1, here, :].astype(full)
+            )
+            return carry
+
+        lax.fori_loop(0, self.rows // block, add, 0)
+        for copy in self.copies:
+            copy.wait_send()
+
+
+def backward_kernel(
+    count,
+    tokens,
+    cotangent,
+    gains,
+    resid,
+    normed_part,
+    ffn_part,
+    gateup_parts,
+    down_parts,
+    features,
+    qkv_rows,
+    out_rows,
+    stream,
+    kv_both,
+    kv_turned,
+    lse,
+    mixed_group,
+    shuffle,
+    key_ids,
+    query_ids,
+    block_out,
+    input_grad,
+    gain_grads,
+    gateup_grad,
+    down_grad,
+    qkv_grad,
+    out_grad,
+    gateup_sums,
+    down_sums,
+    gateup_held,
+    gateup_terms,
+    down_held,
+    down_terms,
+    part_quarter,
+    qkv_local,
+    out_local,
+    qkv_sums,
+    out_sums,
+    sum_out,
+    sum_in,
+    proj_group,
+    turned_grad,
+    grad_stream,
+    kv_total,
+    kv_out,
+    kv_in,
+    stream_grad,
+    kv_mate,
+    all_grad,
+    normed_grad,
+    bias,
+    load_sem,
+    part_sem,
+    ring_send,
+    ring_recv,
+    head_send,
+    head_recv,
+    kv_send,
+    kv_recv,
+):
+    rows = tokens.shape[0]
+    group = 4 * rows
+    width = features.shape[1]
+    heads = width // HEAD_DIM
+    scale = HEAD_DIM ** (-0.5)
+    query_grad = turned_grad
+    feature_grad = grad_stream
+    head = lax.axis_index("head")
+    me = lax.axis_index("seq")
+    mate_head = head + 1 - 2 * lax.rem(head, 2)
+    across_head = lax.rem(head + 2, 4)
+    mate = {"head": mate_head}
+    across = {"head": across_head}
+    corner = {"head": 3 - head}
+
+    def lanes(of):
+        return pl.ds(pl.multiple_of(of * width, 128), width)
+
+    def quarter(i):
+        return pl.ds(i * rows, rows)
+
+    copies = []
+
+    def send(index, source, target, where):
+        copy = remote(source, target, head_send.at[index], head_recv.at[index], where)
+        copy.start()
+        copies.append(copy)
+
+    def arrived(index, target, where):
+        remote(target, target, head_send.at[index], head_recv.at[index], where).wait_recv()
+
+    def shard_view(ref, columns):
+        def view(shard, part=None):
+            first = pl.multiple_of((shard // 2) * BLK, 32)
+            at = pl.ds(pl.multiple_of(lax.rem(shard, 2) * columns, 128), columns)
+            if part is None:
+                return ref.at[pl.ds(first, BLK), at]
+            return ref.at[pl.ds(pl.multiple_of(first + part * (BLK // 2), 16), BLK // 2), at]
+
+        return view
+
+    qkv_view = shard_view(qkv_local, QKV // 2)
+    out_view = shard_view(out_local, D // 2)
+    gateup_ring = StagedSumRing(
+        count,
+        gateup_parts,
+        gateup_sums,
+        gateup_held,
+        gateup_terms,
+        load_sem.at[0],
+        ring_send.at[0],
+        ring_recv.at[0],
+    )
+    down_ring = StagedSumRing(
+        count,
+        down_parts,
+        down_sums,
+        down_held,
+        down_terms,
+        load_sem.at[1],
+        ring_send.at[1],
+        ring_recv.at[1],
+    )
+    qkv_ring = SumRing(count, qkv_view, qkv_view, qkv_sums, ring_send.at[2], ring_recv.at[2])
+    out_ring = SumRing(count, out_view, out_view, out_sums, ring_send.at[3], ring_recv.at[3])
+
+    barrier = pltpu.get_barrier_semaphore()
+    for where in (gateup_ring.where(0), gateup_ring.where(1), mate, across, corner):
+        pl.semaphore_signal(barrier, inc=1, device_id=where, device_id_type=pl.DeviceIdType.MESH)
+
+    @pl.when(me < count - 1)
+    def _():
+        pl.semaphore_signal(
+            barrier, inc=1, device_id={"seq": me + 1}, device_id_type=pl.DeviceIdType.MESH
+        )
+
+    pl.semaphore_wait(barrier, 5 + (me + count - 1) // count)
+
+    def fetch(value, i):
+        copy = pltpu.make_async_copy(value.at[quarter(i)], part_quarter, part_sem)
+        copy.start()
+        copy.wait()
+        return part_quarter[...].astype(full)
+
+    def sum_first(base, slot, value):
+        send(base, value.at[quarter(3)], sum_in.at[slot], mate)
+        send(base + 1, value.at[quarter(1)], sum_in.at[slot + 1], mate)
+
+    def sum_across(base, slot, value):
+        own = fetch(value, 2)
+        arrived(base, sum_in.at[slot], mate)
+        sum_out[slot // 3] = (own + sum_in[slot].astype(full)).astype(low)
+        send(base + 2, sum_out.at[slot // 3], sum_in.at[slot + 2], across)
+
+    def sum_last(base, slot, value):
+        own = fetch(value, 0)
+        arrived(base + 1, sum_in.at[slot + 1], mate)
+        own = own + sum_in[slot + 1].astype(full)
+        arrived(base + 2, sum_in.at[slot + 2], across)
+        return own + sum_in[slot + 2].astype(full)
+
+    sum_first(0, 0, normed_part)
+    gateup_ring.start()
+    down_ring.start()
+    sum_across(0, 0, normed_part)
+    sum_first(3, 3, ffn_part)
+
+    normed_two_grad = sum_last(0, 0, normed_part)
+    values = resid[...]
+    inverse = inverse_norm(values)
+    gain_grads[1:2, :] = jnp.sum(normed_two_grad * values * inverse, axis=0, keepdims=True)
+    input_grad[...] = cotangent[...].astype(full) + norm_back(
+        values, inverse, gains[1:2, :], normed_two_grad
+    )
+    proj_group[quarter(0), :] = input_grad[...].astype(low)
+    send(6, proj_group.at[quarter(0)], proj_group.at[quarter(2)], across)
+    send(7, proj_group.at[quarter(0)], proj_group.at[quarter(1)], mate)
+    gateup_ring.step(1)
+    down_ring.step(1)
+    sum_across(3, 3, ffn_part)
+
+    def back_projection(i):
+        turned_grad[quarter(i), :] = mul(proj_group[quarter(i), :], out_rows[...], NT).astype(low)
+
+    back_projection(0)
+    arrived(7, proj_group.at[quarter(1)], mate)
+    back_projection(1)
+    arrived(6, proj_group.at[quarter(2)], across)
+    send(8, proj_group.at[quarter(2)], proj_group.at[quarter(3)], mate)
+    back_projection(2)
+    arrived(8, proj_group.at[quarter(3)], mate)
+    back_projection(3)
+
+    def turn(i, carry):
+        here = pl.ds(pl.multiple_of(i * rows, rows), rows)
+        grad_stream[here, :] = mul(shuffle[here, :], turned_grad[...], NN).astype(low)
+        return carry
+
+    lax.fori_loop(0, 4, turn, 0)
+    for i in range(3):
+        at = slice(i * (D // 3), (i + 1) * (D // 3))
+        out_local[:, at] = mul(mixed_group[...], proj_group[:, at], TN).astype(low)
+    out_ring.start()
+    gateup_ring.step(2)
+    down_ring.step(2)
+
+    kv_total[...] = jnp.zeros_like(kv_total)
+
+    def back_tile(tile, carry):
+        start = pl.multiple_of(tile * QUERY_TILE, QUERY_TILE)
+        here = pl.ds(start, QUERY_TILE)
+        span = pl.ds(start, SPAN)
+        shape = (SPAN, QUERY_TILE)
+        key = lax.broadcasted_iota(jnp.int32, shape, 0)
+        query = lax.broadcasted_iota(jnp.int32, shape, 1)
+        same = key_ids[span, :] == query_ids[:, here]
+        allowed = same & (key > query) & (key <= query + WINDOW)
+        bias[...] = jnp.where(allowed, 0.0, neg_fill)
+
+        def back_head(j, carry):
+            at = pl.ds(pl.multiple_of(j * HEAD_DIM, HEAD_DIM), HEAD_DIM)
+            queries = stream[here, at]
+            grads = grad_stream[here, at]
+            scores = mul(kv_both[span, :HEAD_DIM], queries, NT) * scale + bias[...]
+            probs = jnp.exp(scores - lse[j, :, here])
+            prob_grad = mul(kv_both[span, HEAD_DIM:], grads, NT)
+            delta = jnp.sum(probs * prob_grad, axis=0, keepdims=True)
+            score_grad = (probs * (prob_grad - delta)).astype(low)
+            turned = mul(kv_turned[:HEAD_DIM, span], score_grad, NN) * scale
+            query_grad[here, at] = turned.T.astype(low)
+            kv_total[span, :HEAD_DIM] += mul(score_grad, queries, NN) * scale
+            kv_total[span, HEAD_DIM:] += mul(probs.astype(low), grads, NN)
+            return carry
+
+        return lax.fori_loop(0, heads, back_head, carry)
+
+    lax.fori_loop(0, group // QUERY_TILE, back_tile, 0)
+    kv_out[...] = kv_total[:group, :].astype(low)
+    kv_copy = remote(kv_out, kv_in, kv_send, kv_recv, {"seq": lax.rem(me + count - 1, count)})
+
+    @pl.when(me > 0)
+    def _():
+        kv_copy.start()
+
+    def turn_back(i, carry):
+        here = pl.ds(pl.multiple_of(i * rows, rows), rows)
+        all_grad[here, lanes(head)] = mul(shuffle[:, here], query_grad[...], TN).astype(low)
+        return carry
+
+    lax.fori_loop(0, 4, turn_back, 0)
+
+    def swapped(index, ref, columns, distance, where):
+        for i in range(4):
+            send(
+                index + i,
+                ref.at[quarter(i), columns],
+                ref.at[quarter(i ^ distance), columns],
+                where,
+            )
+
+    def swapped_arrived(index, ref, columns, distance, where):
+        for i in range(4):
+            arrived(index + i, ref.at[quarter(i ^ distance), columns], where)
+
+    swapped(9, all_grad, lanes(head), 2, across)
+    swapped(13, all_grad, lanes(head), 1, mate)
+    gateup_ring.step(3)
+    down_ring.step(3)
+    out_ring.step(1)
+
+    @pl.when(me < count - 1)
+    def _():
+        kv_copy.wait_recv()
+        kv_total[pl.ds(group, group), :] += kv_in[...].astype(full)
+
+    stream_grad[...] = kv_total[pl.ds(group, group), :].astype(low)
+
+    def turn_keys(i, carry):
+        here = pl.ds(pl.multiple_of(i * rows, rows), rows)
+        kv_mate[0, here, :] = mul(shuffle[:, here], stream_grad[...], TN).astype(low)
+        return carry
+
+    lax.fori_loop(0, 4, turn_keys, 0)
+    for i in range(4):
+        send(17 + i, kv_mate.at[0, quarter(i)], kv_mate.at[1, quarter(i ^ 1)], mate)
+    for i in range(4):
+        arrived(17 + i, kv_mate.at[1, quarter(i ^ 1)], mate)
+    kv_total[pl.ds(0, group), :] = kv_mate[0].astype(full) + kv_mate[1].astype(full)
+    kv_mate[2] = kv_total[pl.ds(0, group), :].astype(low)
+    for i in range(4):
+        send(21 + i, kv_mate.at[2, quarter(i)], kv_mate.at[3, quarter(i ^ 2)], across)
+    swapped_arrived(9, all_grad, lanes(across_head), 2, across)
+    swapped(25, all_grad, lanes(across_head), 1, mate)
+    out_ring.step(2)
+    swapped_arrived(13, all_grad, lanes(mate_head), 1, mate)
+    for i in range(4):
+        arrived(21 + i, kv_mate.at[3, quarter(i ^ 2)], across)
+    all_grad[:, QW:] = (kv_total[pl.ds(0, group), :] + kv_mate[3].astype(full)).astype(low)
+    swapped_arrived(25, all_grad, lanes(3 - head), 1, mate)
+
+    for i in range(2):
+        at = slice(i * (QKV // 2), (i + 1) * (QKV // 2))
+        qkv_local[:, at] = mul(features[...], all_grad[:, at], TN).astype(low)
+    qkv_ring.start()
+    out_ring.step(3)
+    for i, where in ((2, across), (3, corner), (1, mate)):
+        feature_grad[quarter(i), :] = mul(all_grad[quarter(i), :], qkv_rows[...], NT).astype(low)
+        send(28 + i, feature_grad.at[quarter(i)], normed_grad.at[:, lanes(head)], where)
+    normed_grad[:, lanes(head)] = mul(all_grad[quarter(0), :], qkv_rows[...], NT).astype(low)
+    block_out[...] = (resid[...] + sum_last(3, 3, ffn_part)).astype(low)
+    gateup_ring.finish(gateup_grad)
+    down_ring.finish(down_grad)
+    qkv_ring.step(1)
+    for i, where, of in ((2, across, across_head), (3, corner, 3 - head), (1, mate, mate_head)):
+        arrived(28 + i, normed_grad.at[:, lanes(of)], where)
+    qkv_ring.step(2)
+    normed_one_grad = normed_grad[...].astype(full)
+    values = tokens[...].astype(full)
+    inverse = inverse_norm(values)
+    gain_grads[0:1, :] = jnp.sum(normed_one_grad * values * inverse, axis=0, keepdims=True)
+    input_grad[...] += norm_back(values, inverse, gains[0:1, :], normed_one_grad)
+    qkv_ring.step(3)
+    out_ring.finish(out_grad)
+    qkv_ring.finish(qkv_grad)
+    for copy in copies:
+        copy.wait_send()
+
+    @pl.when(me > 0)
+    def _():
+        kv_copy.wait_send()
+
+
+def backward_section(count, *values):
+    (tokens, cotangent, gains, resid, normed_part, ffn_part, gateup_parts, down_parts) = values[:8]
+    rows = tokens.shape[0]
+    group = 4 * rows
+    width = QW // 4
+    steps = count // 2
+    vmem = pl.BlockSpec(memory_space=pltpu.VMEM)
+    hbm = pl.BlockSpec(memory_space=pl.ANY)
+    shard = gateup_parts.shape[1:]
+    down_shard = down_parts.shape[1:]
+    outs = [
+        ((rows, D), low),
+        ((rows, D), full),
+        ((2, D), full),
+        (shard, full),
+        (down_shard, full),
+        ((BLK, QKV // 2), full),
+        ((BLK, D // 2), full),
+        ((2, steps) + shard, low),
+        ((2, steps) + down_shard, low),
+    ]
+    dma = pltpu.SemaphoreType.DMA
+    return pl.pallas_call(
+        functools.partial(backward_kernel, count),
+        in_specs=[vmem] * 4 + [hbm] * 4 + [vmem] * 11,
+        out_specs=[vmem] * 7 + [hbm] * 2,
+        out_shape=[jax.ShapeDtypeStruct(shape, kind) for shape, kind in outs],
+        scratch_shapes=[
+            pltpu.VMEM((2,) + shard, low),
+            pltpu.VMEM((2,) + shard, low),
+            pltpu.VMEM((2,) + down_shard, low),
+            pltpu.VMEM((2,) + down_shard, low),
+            pltpu.VMEM((rows, D), low),
+            pltpu.VMEM((width, QKV), low),
+            pltpu.VMEM((width, D), low),
+            pltpu.VMEM((2, steps, BLK, QKV // 2), low),
+            pltpu.VMEM((2, steps, BLK, D // 2), low),
+            pltpu.VMEM((2, rows, D), low),
+            pltpu.VMEM((6, rows, D), low),
+            pltpu.VMEM((group, D), low),
+            pltpu.VMEM((group, width), low),
+            pltpu.VMEM((group, width), low),
+            pltpu.VMEM((2 * group, 2 * HEAD_DIM), full),
+            pltpu.VMEM((group, 2 * HEAD_DIM), low),
+            pltpu.VMEM((group, 2 * HEAD_DIM), low),
+            pltpu.VMEM((group, 2 * HEAD_DIM), low),
+            pltpu.VMEM((4, group, 2 * HEAD_DIM), low),
+            pltpu.VMEM((group, QKV), low),
+            pltpu.VMEM((rows, D), low),
+            pltpu.VMEM((SPAN, QUERY_TILE), full),
+            dma((2, 2, 2)),
+            dma,
+            dma((4, 2, steps)),
+            dma((4, 2, steps)),
+            dma((32,)),
+            dma((32,)),
+            dma,
+            dma,
+        ],
+        compiler_params=pltpu.CompilerParams(
+            collective_id=1, has_side_effects=True, vmem_limit_bytes=60 * 1024 * 1024
+        ),
+        name="backward_section",
+    )(*values)
 
 
 def update_kernel(rate, w_ref, g_ref, l_ref, r_ref, lr_ref, rr_ref, ln_ref, rn_ref, wn_ref):
@@ -376,6 +1401,146 @@
 
 def inverse_norm(values):
     return lax.rsqrt(jnp.mean(values * values, axis=-1, keepdims=True) + norm_eps)
+
+
+def forward_steps(tokens, cotangent, gain_one, gain_two, stacks, token_order, key_ids, query_ids):
+    qkv_stack, out_stack, gateup_stack, down_stack = stacks
+    row_count = tokens.shape[0]
+    head_count = lax.axis_size("head")
+    seq_count = lax.axis_size("seq")
+    group = row_count * head_count
+    head_index = lax.axis_index("head")
+    local_width = QW // head_count
+    qkv_rows = joined_halves(gather_rows(qkv_stack, 8, to_columns))
+    out_rows = joined_halves(gather_rows(out_stack, 8, to_columns))
+    gateup = gather_rows(gateup_stack, 16, to_units)
+    down = gather_rows(down_stack, 8, to_columns)
+    tokens_float = tokens.astype(full)
+    normed_one = (tokens_float * inverse_norm(tokens_float) * gain_one).astype(low)
+    normed_one_group = jnp.concatenate(head_gather(normed_one))
+    feature_start = head_index * local_width
+    features = lax.dynamic_slice_in_dim(normed_one_group, feature_start, local_width, 1)
+    weights = in_order(head_gather(qkv_rows), 0)
+    weights = jnp.concatenate(
+        [lax.dynamic_slice_in_dim(weights, feature_start, local_width, 1), weights[:, QW:]], axis=1
+    )
+    projected = mul(normed_one_group, weights, NN, low)
+    buffer_rows = ((token_order // row_count) ^ head_index) * row_count + token_order % row_count
+    shuffle = (
+        buffer_rows[:, None] == lax.broadcasted_iota(jnp.int32, (group, group), 1)
+    ).astype(low)
+    stream = mul(shuffle, projected, NN, low)
+    kv_stream = stream[:, local_width:]
+    kv_before = lax.ppermute(kv_stream, "seq", [(i, i + 1) for i in range(seq_count - 1)])
+    kv_both = jnp.concatenate([kv_before, kv_stream], axis=0)
+    kv_turned = kv_both.T
+    mixed_stream, lse = attend(stream[:, :local_width], kv_both, kv_turned, key_ids, query_ids)
+    mixed_group = mul(shuffle, mixed_stream, TN, low)
+    part = mul(mixed_group, out_rows, NN, low)
+    resid = tokens_float + head_sum([part[i * row_count :][:row_count] for i in range(4)])
+    normed_two = (resid * inverse_norm(resid) * gain_two).astype(low)
+    normed_group = jnp.concatenate(head_gather(normed_two))
+    grad_group = jnp.concatenate(head_gather(cotangent))
+    return (
+        resid,
+        normed_group,
+        grad_group,
+        gateup,
+        down,
+        features,
+        qkv_rows,
+        out_rows,
+        stream,
+        kv_both,
+        kv_turned,
+        lse,
+        mixed_group,
+        shuffle,
+    )
+
+
+def backward_steps(
+    tokens,
+    cotangent,
+    gains,
+    resid,
+    normed_part,
+    ffn_part,
+    gateup_wgrad,
+    down_wgrad,
+    features,
+    qkv_rows,
+    out_rows,
+    stream,
+    kv_both,
+    kv_turned,
+    lse,
+    mixed_group,
+    shuffle,
+    key_ids,
+    query_ids,
+    counts,
+):
+    row_count = tokens.shape[0]
+    group = row_count * lax.axis_size("head")
+    seq_count = lax.axis_size("seq")
+    local_width = features.shape[1]
+    query_stream = stream[:, :local_width]
+    gain_one, gain_two = gains[0], gains[1]
+    tokens_float = tokens.astype(full)
+    inverse_one = inverse_norm(tokens_float)
+    inverse_two = inverse_norm(resid)
+    normed_two_grad = head_sum([normed_part[i * row_count :][:row_count] for i in range(4)])
+    gateup_grad_own = sum_rows(gateup_wgrad, counts[2], 16, from_units)
+    down_grad_own = sum_rows(down_wgrad, counts[3], 8, from_columns)
+    ffn_out = head_sum([ffn_part[i * row_count :][:row_count] for i in range(4)])
+    block_out = (resid + ffn_out).astype(low)
+
+    resid_grad = cotangent.astype(full) + norm_back(resid, inverse_two, gain_two, normed_two_grad)
+    gain_two_grad = jnp.sum(normed_two_grad * resid * inverse_two, axis=0)
+    proj_grad = resid_grad.astype(low)
+    proj_grad_group = jnp.concatenate(head_gather(proj_grad))
+    mixed_grad_group = mul(proj_grad_group, out_rows, NT, low)
+    mixed_grad_stream = mul(shuffle, mixed_grad_group, NN, low)
+    out_wgrad = split_halves(mul(mixed_group, proj_grad_group, TN, low), BLK)
+    out_grad_own = sum_rows(out_wgrad, counts[1], 8, from_columns)
+
+    query_grad, kv_grad = attend_back(
+        query_stream, mixed_grad_stream, kv_both, kv_turned, key_ids, query_ids, lse
+    )
+    kv_later = lax.ppermute(
+        kv_grad[:group].astype(low), "seq", [(i, i - 1) for i in range(1, seq_count)]
+    )
+    kv_grad = (kv_grad[group:] + kv_later.astype(full)).astype(low)
+    grad_local = mul(shuffle, jnp.concatenate([query_grad, kv_grad], axis=1), TN, low)
+    gathered = head_gather(grad_local)
+
+    def own_order(value, j):
+        quarters = [value[i * row_count :][:row_count] for i in range(4)]
+        return jnp.concatenate([quarters[i ^ j] for i in range(4)])
+
+    gathered = [own_order(value, j) for j, value in enumerate(gathered)]
+    kv_total = sum(value[:, local_width:].astype(full) for value in gathered).astype(low)
+    qkv_grad = jnp.concatenate(
+        [in_order([value[:, :local_width] for value in gathered], 1), kv_total], axis=1
+    )
+    qkv_wgrad = split_halves(mul(features, qkv_grad, TN, low), BLK)
+    qkv_grad_own = sum_rows(qkv_wgrad, counts[0], 8, from_columns)
+    feature_grad = mul(qkv_grad, qkv_rows, NT, low)
+    order = (0, 2, 1, 3)
+    feature_parts = head_exchange([feature_grad[i * row_count :][:row_count] for i in range(4)])
+    normed_one_grad = in_order([feature_parts[order.index(j)] for j in range(4)], 1).astype(full)
+    input_grad = resid_grad + norm_back(tokens_float, inverse_one, gain_one, normed_one_grad)
+    gain_one_grad = jnp.sum(normed_one_grad * tokens_float * inverse_one, axis=0)
+    return (
+        block_out,
+        input_grad,
+        jnp.stack([gain_one_grad, gain_two_grad]),
+        gateup_grad_own,
+        down_grad_own,
+        qkv_grad_own,
+        out_grad_own,
+    )
 
 
 def on_device(
@@ -412,9 +1577,6 @@
     device_count = head_count * seq_count
     group = row_count * head_count
     seq_index = lax.axis_index("seq")
-    head_index = lax.axis_index("head")
-    chip = head_index // 2
-    core = head_index % 2
     local_width = QW // head_count
 
     gains = jnp.concatenate([attn_gain, ffn_gain]).astype(low).astype(full)[None]
@@ -429,63 +1591,6 @@
     gain_one = gains[:, :own_gains].reshape(1, D)
     gain_two = gains[:, own_gains:].reshape(1, D)
 
-    qkv_rows = joined_halves(gather_rows(qkv_stack, 8, to_columns))
-    out_rows = joined_halves(gather_rows(out_stack, 8, to_columns))
-    gateup_shard, down_shard, qkv_rows, out_rows = lax.optimization_barrier(
-        (gateup_stack, down_stack, qkv_rows, out_rows)
-    )
-    gateup = gather_rows(gateup_shard, 16, to_units)
-    down = gather_rows(down_shard, 8, to_columns)
-    unit_count = gateup.shape[0] // 2
-    gateup = gateup.reshape(2 * unit_count * BLK, D)
-    down = joined_halves(down)
-
-    tokens_float = tokens.astype(full)
-    inverse_one = inverse_norm(tokens_float)
-    normed_one = (tokens_float * inverse_one * gain_one).astype(low)
-    normed_one_group = jnp.concatenate(head_gather(normed_one))
-
-    def chip_columns(which):
-        return jnp.concatenate(
-            [
-                lax.dynamic_slice_in_dim(qkv_rows, which * 2 * local_width, 2 * local_width, 1),
-                qkv_rows[:, QW:],
-            ],
-            axis=1,
-        )
-
-    def core_columns(block, which):
-        return jnp.concatenate(
-            [
-                lax.dynamic_slice_in_dim(block, which * local_width, local_width, 1),
-                block[:, 2 * local_width :],
-            ],
-            axis=1,
-        )
-
-    own_block = chip_columns(chip)
-    across_block = to_partner(chip_columns(1 - chip), 2)
-    qkv_own = in_order(
-        [
-            core_columns(own_block, core),
-            to_partner(core_columns(own_block, 1 - core), 1),
-            core_columns(across_block, core),
-            to_partner(core_columns(across_block, 1 - core), 1),
-        ],
-        0,
-    )
-    projected = mul(normed_one_group, qkv_own, NN, low)
-
-    buffer_rows = ((token_order // row_count) ^ head_index) * row_count + token_order % row_count
-    shuffle = (
-        buffer_rows[:, None] == lax.broadcasted_iota(jnp.int32, (group, group), 1)
-    ).astype(low)
-    stream = mul(shuffle, projected, NN, low)
-    query_stream = stream[:, :local_width]
-    kv_stream = stream[:, local_width:]
-    kv_before = lax.ppermute(kv_stream, "seq", [(i, i + 1) for i in range(seq_count - 1)])
-    kv_both = jnp.concatenate([kv_before, kv_stream], axis=0)
-    kv_turned = kv_both.T
     ids_own = lax.dynamic_slice_in_dim(sequence_ids, seq_index * group, group, 0)
     ids_before = lax.dynamic_slice_in_dim(
         sequence_ids, jnp.maximum(seq_index - 1, 0) * group, group, 0
@@ -493,19 +1598,45 @@
     ids_before = jnp.where(seq_index > 0, ids_before, -1)
     key_ids = jnp.concatenate([ids_before, ids_own])[:, None]
     query_ids = ids_own[None, :]
-    mixed_stream, lse = attend(query_stream, kv_both, kv_turned, key_ids, query_ids)
-    mixed_group = mul(shuffle, mixed_stream, TN, low)
-
-    mixed_parts = head_exchange([mixed_group[i * row_count :][:row_count] for i in range(4)])
-    order = (0, 2, 1, 3)
-    mixed_parts = [mixed_parts[order.index(j)] for j in range(4)]
-    attended = jnp.concatenate(mixed_parts, axis=1)
-    out_all = jnp.concatenate(head_gather(out_rows))
-    resid = tokens_float + mul(attended, out_all, NN)
-    inverse_two = inverse_norm(resid)
-    normed_two = (resid * inverse_two * gain_two).astype(low)
-    normed_group = jnp.concatenate(head_gather(normed_two))
-    grad_group = jnp.concatenate(head_gather(cotangent))
+    stacks = (qkv_stack, out_stack, gateup_stack, down_stack)
+    whole_rows = all(s.shape[0] % u == 0 for s, u in zip(stacks, (8, 8, 16, 8)))
+    if whole_rows:
+        layouts = (to_columns, to_columns, to_units, to_columns)
+        shards = [turn(s.astype(low)) for s, turn in zip(stacks, layouts)]
+        shards = (shards[0][0], shards[1][0], shards[2].reshape(-1, D), shards[3])
+        section = forward_section(
+            tokens,
+            cotangent,
+            jnp.concatenate([gain_one, gain_two]),
+            shards,
+            token_order[:, None],
+            key_ids,
+            query_ids,
+            seq_count,
+        )
+    else:
+        section = forward_steps(
+            tokens, cotangent, gain_one, gain_two, stacks, token_order, key_ids, query_ids
+        )
+    (
+        resid,
+        normed_group,
+        grad_group,
+        gateup,
+        down,
+        features,
+        qkv_rows,
+        out_rows,
+        stream,
+        kv_both,
+        kv_turned,
+        lse,
+        mixed_group,
+        shuffle,
+    ) = section
+    gateup = gateup.reshape(-1, D)
+    down = joined_halves(down.reshape(-1, BLK, D // 2))
+    unit_count = down.shape[0] // BLK
 
     gate_up = mul(gateup, normed_group, NT).reshape(unit_count, 2, BLK, group)
     hidden, act_pull = jax.vjp(
@@ -518,56 +1649,40 @@
         jnp.stack([gate_grad, up_grad], axis=1).astype(low).reshape(2 * unit_count * BLK, group)
     )
     normed_part = mul(gate_up_grad, gateup, TN, low)
-    normed_two_grad = head_sum([normed_part[i * row_count :][:row_count] for i in range(4)])
     gateup_wgrad = mul(gate_up_grad, normed_group, NN, low).reshape(2 * unit_count, BLK, D)
     down_wgrad = split_halves(mul(hidden, grad_group, NN, low), BLK)
-    gateup_grad_own = sum_rows(gateup_wgrad, gateup_stack.shape[0], 16, from_units)
-    down_grad_own = sum_rows(down_wgrad, down_stack.shape[0], 8, from_columns)
     ffn_part = mul(hidden, down, TN, low)
-    ffn_out = head_sum([ffn_part[i * row_count :][:row_count] for i in range(4)])
-    block_out = (resid + ffn_out).astype(low)
-
-    resid_grad = cotangent.astype(full) + norm_back(resid, inverse_two, gain_two, normed_two_grad)
-    gain_two_grad = jnp.sum(normed_two_grad * resid * inverse_two, axis=0)
-    proj_grad = resid_grad.astype(low)
-    attended_grad = mul(proj_grad, out_all, NT, low)
-    grad_parts = head_exchange(
-        [attended_grad[:, i * local_width : (i + 1) * local_width] for i in range(4)]
-    )
-    mixed_grad_group = jnp.concatenate([grad_parts[order.index(j)] for j in range(4)])
-    mixed_grad_stream = mul(shuffle, mixed_grad_group, NN, low)
-    proj_grad_group = jnp.concatenate(head_gather(proj_grad))
-    out_wgrad = split_halves(mul(mixed_group, proj_grad_group, TN, low), BLK)
-    out_grad_own = sum_rows(out_wgrad, out_stack.shape[0], 8, from_columns)
-
-    query_grad, kv_grad = attend_back(
-        query_stream, mixed_grad_stream, kv_both, kv_turned, key_ids, query_ids, lse
-    )
-    kv_later = lax.ppermute(
-        kv_grad[:group].astype(low), "seq", [(i, i - 1) for i in range(1, seq_count)]
-    )
-    kv_grad = (kv_grad[group:] + kv_later.astype(full)).astype(low)
-    grad_local = mul(shuffle, jnp.concatenate([query_grad, kv_grad], axis=1), TN, low)
-    gathered = head_gather(grad_local)
-
-    def own_order(value, j):
-        quarters = [value[i * row_count :][:row_count] for i in range(4)]
-        return jnp.concatenate([quarters[i ^ j] for i in range(4)])
-
-    gathered = [own_order(value, j) for j, value in enumerate(gathered)]
-    kv_total = sum(value[:, local_width:].astype(full) for value in gathered).astype(low)
-    qkv_grad = jnp.concatenate(
-        [in_order([value[:, :local_width] for value in gathered], 1), kv_total], axis=1
-    )
-    feature_start = head_index * local_width
-    features = lax.dynamic_slice_in_dim(normed_one_group, feature_start, local_width, 1)
-    qkv_wgrad = split_halves(mul(features, qkv_grad, TN, low), BLK)
-    qkv_grad_own = sum_rows(qkv_wgrad, qkv_stack.shape[0], 8, from_columns)
-    feature_grad = mul(qkv_grad, qkv_rows, NT, low)
-    feature_parts = head_exchange([feature_grad[i * row_count :][:row_count] for i in range(4)])
-    normed_one_grad = in_order([feature_parts[order.index(j)] for j in range(4)], 1).astype(full)
-    input_grad = resid_grad + norm_back(tokens_float, inverse_one, gain_one, normed_one_grad)
-    gain_one_grad = jnp.sum(normed_one_grad * tokens_float * inverse_one, axis=0)
+    gains_both = jnp.concatenate([gain_one, gain_two])
+    kept = (features, qkv_rows, out_rows, stream, kv_both, kv_turned, lse, mixed_group, shuffle)
+    counts = [s.shape[0] for s in stacks]
+    if whole_rows:
+        (block_out, input_grad, gain_grads, gateup_own, down_own, qkv_own, out_own, *_) = (
+            backward_section(
+                seq_count,
+                tokens,
+                cotangent,
+                gains_both,
+                resid,
+                normed_part,
+                ffn_part,
+                gateup_wgrad.reshape(seq_count, -1, D),
+                down_wgrad.reshape(seq_count, -1, D // 2),
+                *kept,
+                key_ids,
+                query_ids,
+            )
+        )
+        gateup_grad_own = from_units(gateup_own.reshape(-1, BLK, D))
+        down_grad_own = from_columns(down_own.reshape(-1, BLK, D // 2))
+        qkv_grad_own = from_columns(qkv_own[None])
+        out_grad_own = from_columns(out_own[None])
+    else:
+        section = backward_steps(
+            tokens, cotangent, gains_both, resid, normed_part, ffn_part, gateup_wgrad, down_wgrad, *kept,
+            key_ids, query_ids, counts,
+        )
+        (block_out, input_grad, gain_grads, gateup_grad_own, down_grad_own, qkv_grad_own, out_grad_own) = section
+    gain_one_grad, gain_two_grad = gain_grads[0], gain_grads[1]
     gain_grads = jnp.concatenate(
         [gain_one_grad.reshape(device_count, -1), gain_two_grad.reshape(device_count, -1)], axis=1
     )

time: 642 us -> 559 us (0.87)
  Pallas kernels: 52.1 us -> 394 us
  waiting for transfers between devices: 182 us -> 0.01 us
  starting transfers between devices: 115 us -> 11.3 us
  local copies, waits for them, and re-layouts: 141 us -> 82 us
  other arithmetic: 60.8 us -> 11.4 us
  matrix products: 77.6 us -> 51.6 us
    pallas_call x2, Pallas kernels: 31.3 us -> 373 us  [the longest x1 203 us: forward_section(): pl.pallas_call(functools.partial(forward_kernel, count), in_specs=[vmem,...]
    ppermute x102 -> x0, waiting for transfers between devices: 182 us -> none  [the longest x12 51.2 us: seq_sum(): ahead = lax.ppermute(local, 'seq', up)]
    ppermute x102 -> x0, starting transfers between devices: 105 us -> none  [the longest x36 19.7 us: to_partner(): return lax.ppermute(value, 'head', [(i, i ^ which) for i in range(count)])]
    dynamic_update_slice x36 -> x0, local copies, waits for them, and re-layouts: 34.6 us -> none  [the longest x12 14 us: seq_gather(): lax.dynamic_update_slice(out, behind[None], (ring_index((place + step) %...]
    dot_general x15 -> x6, matrix products: 77.6 us -> 51.6 us  [mul(): return lax.dot_general(a, b, dims, preferred_element_type=kind)]
    convert_element_type x24 -> x2, other arithmetic: 24.2 us -> 1.26 us  [on_device(): shards = [turn(s.astype(low)) for s, turn in zip(stacks, layouts)]]
    unnamed x176 -> x69, local copies, waits for them, and re-layouts: 34.2 us -> 20.8 us
    slice x27 -> x2, local copies, waits for them, and re-layouts: 12.9 us -> 2.1 us  [the longest x1 1.42 us: on_device(): gain_one_grad, gain_two_grad = (gain_grads[0], gain_grads[1])]
  transfers between devices with their start and end apart: 104 -> 2, of which waited for: 43 -> 0; matrix products, arithmetic and copies ran while one was open for 34% -> 7% of each run, Pallas kernels for 8% -> 4%
where the time goes in v2:
time: 559 us; the launch traced here: 551 us
  Pallas kernels  394 us (70%)
  local copies, waits for them, and re-layouts  82 us (15%)
  matrix products  51.6 us (9%)
  other arithmetic  11.4 us (2%)
  starting transfers between devices  11.3 us (2%)
    pallas_call x1, Pallas kernels, forward_section(): pl.pallas_call(functools.partial(forward_kernel, count), in_specs=[vmem,...  203 us
    pallas_call x1, Pallas kernels, backward_section(): pl.pallas_call(functools.partial(backward_kernel, count), in_specs=[vmem]...  170 us
    dot_general x6, matrix products, mul(): return lax.dot_general(a, b, dims, preferred_element_type=kind)  51.6 us
    pallas_call x4, Pallas kernels, update(): pl.pallas_call(functools.partial(update_kernel, rate), grid=(count // bat...  20.9 us
    unnamed x69, local copies, waits for them, and re-layouts  20.8 us
    dot_general x2, local copies, waits for them, and re-layouts, mul(): return lax.dot_general(a, b, dims, preferred_element_type=kind)  13.5 us
    another operation x6, local copies, waits for them, and re-layouts, from_columns(): rows.reshape(n, i, 8, j // 8).transpose(0, 2, 1, 3)  11.8 us
  transfers between devices with their start and end apart: 2, of which 0 were waited for; matrix products, arithmetic and copies ran while one was open for 7% of the time, Pallas kernels for 4%

profile of v2, /device:TPU:0, one launch (start us, length us, event | category | flops | bytes accessed | tf_op | source)
XLA Modules:
  0.0 551.3 jit_solution(15234734616551695785)
XLA Ops:
  0.7 0.8 convert.7
  1.5 0.7 convert.6
  2.2 0.6 broadcast_in_dim.19
  2.8 7.3 %all-to-all-start = ((f32[32,1,96]{2,1,0:T(1,128)}), f32[32,1,96]{2,1,0:T(1,128)S(1)}, u32[]{:S(2)}, u32[]{:S(2)}) async-start(f32[32,1,96]{2,1,0:T(1,128)} %broadcast_in_dim.19), calls=%async_computation | async-start | bytes 32768 | tf_op jit(solution)/shard_map/all_to_all | solution.py:1583
  10.1 1.0 convert_bitcast_fusion.1
  11.2 1.0 convert_bitcast_fusion
  12.2 0.8 dynamic-slice_select_fusion
  14.2 0.9 squeeze_reshape.6.qkv_shard
  15.2 0.8 squeeze_reshape.7.out_shard
  16.0 1.2 convert_element_type.55
  17.2 2.5 copy.71
  19.7 3.1 reshape_reshape.16.gateup_shard
  22.9 1.0 copy.98
  23.9 2.3 reshape.129.down_shard
  26.3 1.7 copy.73.order
  28.0 2.0 copy.74.key_ids
  30.0 0.7 fusion.30
  30.7 0.8 reshape.124
  31.5 0.8 reshape.123
  32.3 0.6 pad_maximum_fusion.1.gains
  32.9 202.6 %forward_section.1 = (f32[256,1536]{1,0:T(8,128)}, bf16[1024,1536]{1,0:T(8,128)(2,1)}, bf16[1024,1536]{1,0:T(8,128)(2,1)}, bf16[8,288,1536]{2,1,0:T(8,128)(2,1)}...) custom-call(bf16[256,1536]{1,0:T(8,128)(2,1)} %tokens.3, ...), custom_call_target="tpu_custom_call" | custom-call | tf_op jit(solution)/shard_map/forward_section/pallas_call | solution.py:741
  235.5 7.4 %copy.101 = bf16[12,2,96,768]{3,1,2,0:T(2,128)(2,1)} copy(bf16[12,2,96,768]{3,2,1,0:T(8,128)(2,1)} %bitcast.122) | data formatting | bytes 7077888 | tf_op jit(solution)/shard_map/reshape;reshape | solution.py:155
  243.0 8.8 %dot_general.26 = bf16[12,96,1536]{2,1,0:T(8,128)(2,1)} reshape(bf16[12,96,2,768]{3,2,1,0:T(2,128)(2,1)} %bitcast.116) | data formatting | bytes 7077888 | tf_op jit(solution)/shard_map/dot_general | solution.py:38
  251.8 10.9 %fusion = f32[12,2,96,1024]{3,2,0,1:T(8,128)S(1)} fusion(bf16[12,2,96,1536]{3,2,1,0:T(8,128)(2,1)} %bitcast.135, bf16[1024,1536]{1,0:T(8,128)(2,1)} %get-tuple-element.53), kind=kOutput, calls=%fused_computation.1 | convolution fusion | flops 7247757312 | bytes 19660800 | tf_op jit(solution)/shard_map/dot_general | solution.py:38
  262.7 2.7 fusion.17
  265.4 1.1 copy-done.27
  266.5 7.2 %fusion.8 = (bf16[12,1,96,1024]{3,2,0,1:T(8,128)(2,1)S(1)}, bf16[12,1,96,1024]{3,2,0,1:T(8,128)(2,1)S(1)}) fusion(f32[12,2,96,1024]{3,2,0,1:T(8,128)S(1)} %fusion, bf16[12,96,1536]{2,1,0:T(8,128)(2,1)S(1)} %copy-done.26, bf16[1024,1536]{1,0:T(8,128)(2,1)S(1)} %copy-done.27), kind=kOutput, calls=%fused_computation.12 | convolution fusion | flops 3652190208 | bytes 20840448 | tf_op jit(solution)/shard_map/dot_general | solution.py:38
  274.2 0.8 copy.78
  275.0 1.8 copy-done.23
  276.9 2.5 copy.90
  279.5 9.3 %fusion.22.gateup_parts = bf16[8,288,1536]{2,1,0:T(8,128)(2,1)} fusion(bf16[8,288,1024]{2,1,0:T(8,128)(2,1)S(1)} %bitcast.119, bf16[1024,1536]{1,0:T(8,128)(2,1)S(1)} %copy-done.32), kind=kOutput, calls=%fused_computation.29 | convolution fusion | flops 7247757312 | bytes 14942208 | tf_op jit(solution)/shard_map/dot_general | solution.py:38
  288.8 4.6 copy.89
  293.4 12.9 %fusion.34.normed_part = bf16[1024,1536]{1,0:T(8,128)(2,1)} fusion(bf16[2304,1024]{1,0:T(8,128)(2,1)} %bitcast.120, bf16[2304,1536]{1,0:T(8,128)(2,1)} %bitcast.136), kind=kOutput, calls=%fused_computation.52 | convolution fusion | flops 7247757312 | bytes 14942208 | tf_op jit(solution)/shard_map/dot_general | solution.py:38
  306.3 5.3 fusion.27
  311.6 5.9 %fusion.35.ffn_part = bf16[1024,1536]{1,0:T(8,128)(2,1)} fusion(bf16[1152,1024]{1,0:T(8,128)(2,1)S(1)} %bitcast.129, bf16[1152,1536]{1,0:T(8,128)(2,1)S(1)} %bitcast.123), kind=kOutput, calls=%fused_computation.53 | convolution fusion | flops 3623878656 | bytes 9043968 | tf_op jit(solution)/shard_map/dot_general | solution.py:38
  317.5 170.2 %backward_section.1 = (bf16[256,1536]{1,0:T(8,128)(2,1)}, f32[256,1536]{1,0:T(8,128)}, f32[2,1536]{1,0:T(2,128)}, f32[288,1536]{1,0:T(8,128)}, f32[288,768]{1,0:...) custom-call(bf16[256,1536]{1,0:T(8,128)(2,1)} %tokens.3, ...), custom_call_target="tpu_custom_call" | custom-call | tf_op jit(solution)/shard_map/backward_section/pallas_call | solution.py:1302
  487.7 1.4 slice_reduce_fusion.1
  489.1 0.8 reshape_squeeze.7
  489.9 1.4 reshape_squeeze.6
  491.3 1.4 pad_maximum_fusion
  492.7 4.0 all-to-all-start.1
  496.7 1.9 reshape_broadcast_in_dim.6
  498.6 1.8 copy.100
  500.4 1.9 reshape_broadcast_in_dim.7
  502.3 1.8 copy.99
  504.2 3.0 reshape_reshape.19
  507.2 3.0 copy.84
  510.2 2.7 reshape_reshape.20
  512.9 1.6 copy.85
  514.6 1.0 copy-done.3
  515.6 1.0 copy-done.6
  516.6 1.0 copy-done.15
  517.6 1.0 copy-done.16
  518.6 1.0 copy-done.17
  519.6 1.0 copy-done.18
  520.6 2.5 update.4
  523.1 1.7 copy-done.8
  524.8 1.7 copy-done.9
  526.4 1.7 copy-done.10
  528.1 10.3 %update.6 = (f32[48,96,96]{2,1,0:T(8,128)}, f32[48,96,96]{2,1,0:T(8,128)}, f32[48,96,96]{2,1,0:T(8,128)}) custom-call(f32[48,96,96]{2,1,0:T(8,128)S(1)} %copy-done, f32[48,96,96]{2,1,0:T(8,128)S(1)} %bitcast.112, f32[48,96,96]{2,1,0:T(8,128)S(1)} %copy-done.7, f32[48,96,96]{2,1,0:T(8,128)S(1)} %copy-done.8, f32[48,96,96]{2,1,0:T(8,128)S(1)} %copy-done.9, ...), custom_call_target="tpu_custom_call" | custom-call | flops 6442450944 | bytes 21233664 | tf_op jit(solution)/shard_map/update/pallas_call | solution.py:1369
  538.5 5.7 %update.7 = (f32[24,96,96]{2,1,0:T(8,128)}, f32[24,96,96]{2,1,0:T(8,128)}, f32[24,96,96]{2,1,0:T(8,128)}) custom-call(f32[24,96,96]{2,1,0:T(8,128)S(1)} %copy-done.2, f32[24,96,96]{2,1,0:T(8,128)S(1)} %bitcast.113, f32[24,96,96]{2,1,0:T(8,128)S(1)} %copy-done.11, f32[24,96,96]{2,1,0:T(8,128)S(1)} %copy-done.12, f32[24,96,96]{2,1,0:T(8,128)S(1)} %copy-done.13, ...), custom_call_target="tpu_custom_call" | custom-call | flops 3221225472 | bytes 10616832 | tf_op jit(solution)/shard_map/update/pallas_call | solution.py:1369
  544.2 2.4 update.5
  547.2 0.9 copy.104
  548.1 2.7 copy.105
  (65 shorter events, 2.7 us)
Async XLA Ops:
  0.6 15.4 %copy-start = (f32[48,96,96]{2,1,0:T(8,128)S(1)}, f32[48,96,96]{2,1,0:T(8,128)}, u32[]{:S(2)}) copy-start(f32[48,96,96]{2,1,0:T(8,128)} %w_ref.6) | copy-start | bytes 5308420
  2.8 27.2 %all-to-all-start = ((f32[32,1,96]{2,1,0:T(1,128)}), f32[32,1,96]{2,1,0:T(1,128)S(1)}, u32[]{:S(2)}, u32[]{:S(2)}) async-start(f32[32,1,96]{2,1,0:T(1,128)} %broadcast_in_dim.19), calls=%async_computation | async-start | bytes 32768 | tf_op jit(solution)/shard_map/all_to_all | solution.py:1583
  13.0 0.6 copy-start.31
  16.0 6.8 %copy-start.2 = (f32[24,96,96]{2,1,0:T(8,128)S(1)}, f32[24,96,96]{2,1,0:T(8,128)}, u32[]{:S(2)}) copy-start(f32[24,96,96]{2,1,0:T(8,128)} %w_ref.7) | copy-start | bytes 2654212
  262.7 2.7 copy-start.26
  262.7 3.8 copy-start.27
  274.2 2.6 copy-start.23
  275.0 4.4 copy-start.24
  276.9 2.6 copy-start.32
  293.4 12.9 %copy-start.28 = (bf16[1536,1024]{1,0:T(8,128)(2,1)S(1)}, bf16[1536,1024]{1,0:T(8,128)(2,1)}, u32[]{:S(2)}) copy-start(bf16[1536,1024]{1,0:T(8,128)(2,1)} %copy.89) | copy-start | bytes 9437188
  293.4 12.9 %copy-start.29 = (bf16[12,1,96,1024]{3,2,0,1:T(8,128)(2,1)S(1)}, bf16[12,1,96,1024]{3,2,0,1:T(8,128)(2,1)}, u32[]{:S(2)}) copy-start(bf16[12,1,96,1024]{3,2,0,1:T(8,128)(2,1)} %fusion.17) | copy-start | bytes 7077892
  306.3 5.3 copy-start.25
  492.7 53.9 %all-to-all-start.1 = ((f32[32,1,96]{2,1,0:T(1,128)}), f32[32,1,96]{2,1,0:T(1,128)S(1)}, u32[]{:S(2)}, u32[]{:S(2)}) async-start(f32[32,1,96]{2,1,0:T(1,128)} %bitcast.34), calls=%async_computation.1 | async-start | bytes 32768 | tf_op jit(solution)/shard_map/all_to_all | solution.py:1689
  512.9 10.2 %copy-start.1 = (f32[3,96,16,96]{1,3,2,0:T(8,128)S(1)}, f32[3,96,16,96]{1,3,2,0:T(8,128)}, u32[]{:S(2)}) copy-start(f32[3,96,16,96]{1,3,2,0:T(8,128)} %copy.84) | copy-start | bytes 5308420
  514.6 1.0 copy-start.3
  515.6 1.0 copy-start.6
  516.6 1.0 copy-start.15
  517.6 1.0 copy-start.16
  518.6 1.0 copy-start.17
  519.6 1.0 copy-start.18
  520.6 2.5 copy-start.7
  523.1 1.7 copy-start.8
  524.8 1.7 copy-start.9
  526.4 1.7 copy-start.10
  528.1 10.3 %copy-start.11 = (f32[24,96,96]{2,1,0:T(8,128)S(1)}, f32[24,96,96]{2,1,0:T(8,128)}, u32[]{:S(2)}) copy-start(f32[24,96,96]{2,1,0:T(8,128)} %l_ref.7) | copy-start | bytes 2654212
  528.1 10.3 %copy-start.12 = (f32[24,96,96]{2,1,0:T(8,128)S(1)}, f32[24,96,96]{2,1,0:T(8,128)}, u32[]{:S(2)}) copy-start(f32[24,96,96]{2,1,0:T(8,128)} %r_ref.7) | copy-start | bytes 2654212
  528.1 10.3 %copy-start.13 = (f32[24,96,96]{2,1,0:T(8,128)S(1)}, f32[24,96,96]{2,1,0:T(8,128)}, u32[]{:S(2)}) copy-start(f32[24,96,96]{2,1,0:T(8,128)} %lr_ref.7) | copy-start | bytes 2654212
  528.1 10.3 %copy-start.14 = (f32[24,96,96]{2,1,0:T(8,128)S(1)}, f32[24,96,96]{2,1,0:T(8,128)}, u32[]{:S(2)}) copy-start(f32[24,96,96]{2,1,0:T(8,128)} %rr_ref.7) | copy-start | bytes 2654212
  538.4 5.7 %copy-start.4 = (f32[8,96,96]{2,1,0:T(8,128)S(1)}, f32[8,96,96]{2,1,0:T(8,128)}, u32[]{:S(2)}) copy-start(f32[8,96,96]{2,1,0:T(8,128)} %w_ref.5) | copy-start | bytes 884740
  538.4 5.7 %copy-start.5 = (f32[1,96,8,96]{3,1,2,0:T(8,128)S(1)}, f32[1,96,8,96]{3,1,2,0:T(8,128)}, u32[]{:S(2)}) copy-start(f32[1,96,8,96]{3,1,2,0:T(8,128)} %copy.99) | copy-start | bytes 884740
  538.4 5.7 %copy-start.19 = (f32[8,96,96]{2,1,0:T(8,128)S(1)}, f32[8,96,96]{2,1,0:T(8,128)}, u32[]{:S(2)}) copy-start(f32[8,96,96]{2,1,0:T(8,128)} %l_ref.5) | copy-start | bytes 884740
  538.5 5.7 %copy-start.20 = (f32[8,96,96]{2,1,0:T(8,128)S(1)}, f32[8,96,96]{2,1,0:T(8,128)}, u32[]{:S(2)}) copy-start(f32[8,96,96]{2,1,0:T(8,128)} %r_ref.5) | copy-start | bytes 884740
  538.5 5.7 %copy-start.21 = (f32[8,96,96]{2,1,0:T(8,128)S(1)}, f32[8,96,96]{2,1,0:T(8,128)}, u32[]{:S(2)}) copy-start(f32[8,96,96]{2,1,0:T(8,128)} %lr_ref.5) | copy-start | bytes 884740
  538.5 5.7 %copy-start.22 = (f32[8,96,96]{2,1,0:T(8,128)S(1)}, f32[8,96,96]{2,1,0:T(8,128)}, u32[]{:S(2)}) copy-start(f32[8,96,96]{2,1,0:T(8,128)} %rr_ref.5) | copy-start | bytes 884740
  544.2 3.1 copy-start.30

commit v3 on v2

--- a/solution.py
+++ b/solution.py
@@ -330,8 +330,9 @@
 
 
 class Ring:
-    def __init__(self, count, view, send, recv):
+    def __init__(self, count, view, send, recv, split=True):
         me = lax.axis_index("seq")
+        self.split = split
         odd = lax.rem(me, 2)
         self.count = count
         self.view = view
@@ -349,10 +350,13 @@
 
     def pair(self, offset, step):
         last = step == self.count // 2
+        halved = last and self.split
         views = [
-            self.view(self.shard(-offset), 0 if last else None),
-            self.view(self.shard(offset), 1 if last else None),
+            self.view(self.shard(-offset), 0 if halved else None),
+            self.view(self.shard(offset), 1 if halved else None),
         ]
+        if last and not self.split:
+            views = views[:1]
         return [
             remote(view, view, self.send.at[i, step - 1], self.recv.at[i, step - 1], where)
             for i, (view, where) in enumerate(zip(views, (self.ahead, self.behind)))
@@ -372,40 +376,48 @@
             copy.wait_send()
 
 
+def turned_row(row):
+    size = row.shape[1]
+    return jnp.broadcast_to(row.astype(full), (128, size)).T[:, :1]
+
+
 def forward_kernel(
     count,
     tokens,
-    cotangent,
+    own_gains,
+    qkv_stack,
+    out_stack,
+    gateup_stack,
+    down_stack,
+    order,
+    ids,
     gains,
-    qkv_shard,
-    out_shard,
-    gateup_shard,
-    down_shard,
-    order,
-    key_ids,
-    query_ids,
     resid,
     normed_group,
-    grad_group,
     gateup,
     down,
     features,
     qkv_rows,
-    out_rows,
+    out_all,
     stream,
     kv_both,
     kv_turned,
     lse,
     mixed_group,
     shuffle,
+    key_ids,
+    query_ids,
     tokens_group,
     normed,
     weights,
     projected,
     mixed,
+    mixed_all,
     bias,
-    part_out,
-    part_in,
+    wide,
+    gateup_own,
+    down_own,
+    gain_tiles,
     own_sem,
     ring_send,
     ring_recv,
@@ -420,9 +432,16 @@
     heads = width // HEAD_DIM
     head = lax.axis_index("head")
     me = lax.axis_index("seq")
-    mate = {"head": head + 1 - 2 * lax.rem(head, 2)}
-    across = {"head": lax.rem(head + 2, 4)}
-    band = pl.multiple_of(head * width, 128)
+    mate_head = head + 1 - 2 * lax.rem(head, 2)
+    across_head = lax.rem(head + 2, 4)
+    mate = {"head": mate_head}
+    across = {"head": across_head}
+
+    def band(of):
+        return pl.ds(pl.multiple_of(of * width, 128), width)
+
+    def chip_columns(of):
+        return pl.ds(pl.multiple_of((of // 2) * 2 * width, 128), 2 * width)
 
     def quarter(ref, i):
         return ref.at[pl.ds(i * rows, rows)]
@@ -437,19 +456,15 @@
     def arrived(index, target, where):
         remote(target, target, head_send.at[index], head_recv.at[index], where).wait_recv()
 
-    def qkv_view(shard, part):
-        first = pl.multiple_of(band + (shard // 2) * BLK, 32)
-        columns = pl.ds(pl.multiple_of(lax.rem(shard, 2) * (QKV // 2), 128), QKV // 2)
-        if part is None:
-            return weights.at[pl.ds(first, BLK), columns]
-        return weights.at[pl.ds(pl.multiple_of(first + part * (BLK // 2), 16), BLK // 2), columns]
-
-    def out_view(shard, part):
-        first = pl.multiple_of((shard // 2) * BLK, 32)
-        columns = pl.ds(pl.multiple_of(lax.rem(shard, 2) * (D // 2), 128), D // 2)
-        if part is None:
-            return out_rows.at[pl.ds(first, BLK), columns]
-        return out_rows.at[pl.ds(pl.multiple_of(first + part * (BLK // 2), 16), BLK // 2), columns]
+    def stack_view(ref, columns):
+        def view(shard, part):
+            first = pl.multiple_of(head * width + (shard // 2) * BLK, 32)
+            at = pl.ds(pl.multiple_of(lax.rem(shard, 2) * columns, 128), columns)
+            if part is None:
+                return ref.at[pl.ds(first, BLK), at]
+            return ref.at[pl.ds(pl.multiple_of(first + part * (BLK // 2), 16), BLK // 2), at]
+
+        return view
 
     def gateup_view(shard, part):
         size = gateup.shape[1]
@@ -462,11 +477,13 @@
             return down.at[shard]
         return down.at[shard, :, pl.ds(part * (BLK // 2), BLK // 2)]
 
-    rings = [
-        Ring(count, view, ring_send.at[i], ring_recv.at[i])
-        for i, view in enumerate((qkv_view, out_view, gateup_view, down_view))
+    qkv_view = stack_view(weights, QKV // 2)
+    out_view = stack_view(out_all, D // 2)
+    gain_view = lambda shard, part: gain_tiles.at[head, shard]
+    qkv_ring, out_ring, gateup_ring, down_ring, gain_ring = rings = [
+        Ring(count, view, ring_send.at[i], ring_recv.at[i], view is not gain_view)
+        for i, view in enumerate((qkv_view, out_view, gateup_view, down_view, gain_view))
     ]
-    qkv_ring, out_ring, gateup_ring, down_ring = rings
 
     barrier = pltpu.get_barrier_semaphore()
     for where in (qkv_ring.ahead, qkv_ring.behind, mate, across):
@@ -478,106 +495,124 @@
             barrier, inc=1, device_id={"seq": me - 1}, device_id_type=pl.DeviceIdType.MESH
         )
 
+    def side_by_side(stack, first):
+        size = stack.shape[2]
+        blocks = 8
+        for c in range(blocks):
+            wide[:, c * size : (c + 1) * size] = stack[first + c]
+        return wide[:, : blocks * size].astype(low)
+
+    qkv_view(me, None)[...] = side_by_side(qkv_stack, 0)
+    gain_tiles[head, me] = own_gains[...]
     pl.semaphore_wait(barrier, 5 - me // (count - 1))
-
+    send(0, tokens, quarter(tokens_group, 2), across)
+    send(1, tokens, quarter(tokens_group, 1), mate)
+    qkv_ring.start(1)
+    gain_ring.start(1)
+    for q in range(gateup_own.shape[0] // BLK):
+        for r in range(GRID):
+            wide[:, r * BLK : (r + 1) * BLK] = gateup_stack[q * GRID + r].T
+        gateup_own[q * BLK : (q + 1) * BLK, :] = wide[:, :D].astype(low)
+    for m in range(down_own.shape[0]):
+        down_own[m] = side_by_side(down_stack, 8 * m)
     own = [
-        pltpu.make_async_copy(gateup_shard, gateup.at[me], own_sem.at[0]),
-        pltpu.make_async_copy(down_shard, down.at[me], own_sem.at[1]),
-        pltpu.make_async_copy(cotangent, quarter(grad_group, 0), own_sem.at[2]),
-        pltpu.make_async_copy(qkv_shard, qkv_view(me, None), own_sem.at[3]),
-        pltpu.make_async_copy(out_shard, out_view(me, None), own_sem.at[4]),
+        pltpu.make_async_copy(gateup_own, gateup.at[me], own_sem.at[0]),
+        pltpu.make_async_copy(down_own, down.at[me], own_sem.at[1]),
     ]
     for copy in own:
         copy.start()
-    own[3].wait()
-    qkv_ring.start(1)
-    own[0].wait()
-    own[1].wait()
-    gateup_ring.start(1)
-    down_ring.start(1)
-
-    def band_view(which, offset):
-        shard = qkv_ring.shard(offset)
-        first = pl.multiple_of(which * width + (shard // 2) * BLK, 32)
-        columns = pl.ds(pl.multiple_of(lax.rem(shard, 2) * (QKV // 2), 128), QKV // 2)
-        return weights.at[pl.ds(first, BLK), columns]
-
-    across_head = lax.rem(head + 2, 4)
-    offsets = [[0]] + [[-i, i] for i in range(1, count // 2)] + [[count // 2]]
-
-    def pass_across(step):
-        for offset in offsets[step]:
-            part = band_view(head, offset)
-            send(17 + offset % count, part, part, across)
-
-    def pass_on(step):
-        for offset in offsets[step]:
-            part = band_view(across_head, offset)
-            arrived(17 + offset % count, part, across)
-            send(17 + count + offset % count, part, part, mate)
-
-    pass_across(0)
-    send(0, tokens, quarter(tokens_group, 2), across)
-    send(1, tokens, quarter(tokens_group, 1), mate)
-
-    def norm_rows(source, i):
-        values = source[...].astype(full)
-        normed[pl.ds(i * rows, rows), :] = (
-            values * inverse_norm(values) * gains[0:1, :]
-        ).astype(low)
-
-    norm_rows(tokens, 0)
+    out_view(me, None)[...] = side_by_side(out_stack, 0)
+    for copy in own:
+        copy.wait()
+
+    def pump(step):
+        if step > 1:
+            gateup_ring.arrive(step - 1)
+            down_ring.arrive(step - 1)
+        if step <= count // 2:
+            gateup_ring.start(step)
+            down_ring.start(step)
+
+    pump(1)
+    tokens_group[:rows, :] = tokens[...]
     qkv_ring.arrive(1)
     qkv_ring.start(2)
-    pass_across(1)
-    at = order[...]
-    owner = at // rows
-    flip = head - 2 * (owner // 2) * (head // 2) * 2 - 2 * lax.rem(owner, 2) * lax.rem(head, 2)
-    place = (owner + flip) * rows + lax.rem(at, rows)
+    gain_ring.arrive(1)
+    gain_ring.start(2)
+
     for i in range(4):
-        shuffle[pl.ds(i * rows, rows), :] = jnp.where(
-            place[i * rows : (i + 1) * rows]
-            == lax.broadcasted_iota(jnp.int32, (rows, group), 1),
-            1.0,
-            0.0,
+        at = turned_row(order[:, i * rows : (i + 1) * rows]).astype(jnp.int32)
+        owner = at // rows
+        flip = head - 4 * (owner // 2) * (head // 2) - 2 * lax.rem(owner, 2) * lax.rem(head, 2)
+        place = (owner + flip) * rows + lax.rem(at, rows)
+        shuffle[i * rows : (i + 1) * rows, :] = jnp.where(
+            place == lax.broadcasted_iota(jnp.int32, (rows, group), 1), 1.0, 0.0
         ).astype(low)
-    arrived(1, quarter(tokens_group, 1), mate)
-    norm_rows(quarter(tokens_group, 1), 1)
+    query_ids[...] = ids[:, pl.ds(pl.multiple_of(me * group, 128), group)].astype(full)
+    before = (me - (me + count - 1) // count) * group
+    for i in range(4):
+        here = slice(i * rows, (i + 1) * rows)
+        at = pl.multiple_of(before + i * rows, 128)
+        key_ids[here, :] = jnp.where(me > 0, turned_row(ids[:, pl.ds(at, rows)]), -1.0)
+        there = slice(group + i * rows, group + (i + 1) * rows)
+        key_ids[there, :] = turned_row(query_ids[:, here])
     for step in range(2, count // 2):
         qkv_ring.arrive(step)
         qkv_ring.start(step + 1)
-        pass_across(step)
-        pass_on(step - 2)
+        gain_ring.arrive(step)
+        gain_ring.start(step + 1)
+    qkv_ring.arrive(count // 2)
+
+    key_columns = pl.ds(QW, 2 * HEAD_DIM)
+
+    def weight_parts(of, chip_of):
+        return [weights.at[band(of), columns] for columns in (chip_columns(chip_of), key_columns)]
+
+    for i, part in enumerate(weight_parts(head, across_head)):
+        send(3 + i, part, part, across)
+    for i, part in enumerate(weight_parts(head, head)):
+        send(7 + i, part, part, mate)
+    gain_ring.arrive(count // 2)
+    send(9, gain_tiles.at[head], gain_tiles.at[head], across)
+    send(10, gain_tiles.at[head], gain_tiles.at[head], mate)
+    out_ring.start(1)
     arrived(0, quarter(tokens_group, 2), across)
     send(2, quarter(tokens_group, 2), quarter(tokens_group, 3), mate)
-    norm_rows(quarter(tokens_group, 2), 2)
-    qkv_ring.arrive(count // 2)
-    pass_across(count // 2)
-    part = weights.at[pl.ds(band, width)]
-    send(5, part, part, mate)
-    own[4].wait()
-    out_ring.start(1)
-    own[2].wait()
-    send(8, quarter(grad_group, 0), quarter(grad_group, 2), across)
-    send(9, quarter(grad_group, 0), quarter(grad_group, 1), mate)
-    pass_on(count // 2 - 2)
-    arrived(2, quarter(tokens_group, 3), mate)
-    norm_rows(quarter(tokens_group, 3), 3)
-    features[...] = normed[:, pl.ds(band, width)]
-    qkv_rows[...] = weights[pl.ds(band, width), :]
-    pass_on(count // 2 - 1)
-    gateup_ring.arrive(1)
-    gateup_ring.start(2)
-    down_ring.arrive(1)
-    down_ring.start(2)
+    qkv_rows[...] = weights[band(head), :]
+    arrived(9, gain_tiles.at[across_head], across)
+    send(11, gain_tiles.at[across_head], gain_tiles.at[across_head], mate)
+    arrived(10, gain_tiles.at[mate_head], mate)
+    arrived(11, gain_tiles.at[3 - head], mate)
+    size = D // (4 * count)
+    for h in range(4):
+        for i in range(count):
+            at = (h * count + i) * size
+            wide[:8, at : at + size] = gain_tiles[h, i][:, :size]
+    gains[...] = wide[:2, :D].astype(low).astype(full)
+
+    def norm_rows(i):
+        here = pl.ds(i * rows, rows)
+        values = tokens_group[here, :].astype(full)
+        normed[here, :] = (values * inverse_norm(values) * gains[0:1, :]).astype(low)
+
+    norm_rows(0)
+    arrived(1, quarter(tokens_group, 1), mate)
+    norm_rows(1)
     out_ring.arrive(1)
     out_ring.start(2)
-    pass_on(count // 2)
-    mate_head = head + 1 - 2 * lax.rem(head, 2)
-    mate_band = pl.multiple_of(mate_head * width, 128)
-    arrived(5, weights.at[pl.ds(mate_band, width)], mate)
-    for offset in range(count):
-        arrived(17 + count + offset, band_view(3 - head, offset), mate)
+    norm_rows(2)
+    arrived(2, quarter(tokens_group, 3), mate)
+    norm_rows(3)
+    features[...] = normed[:, band(head)]
+    for i, part in enumerate(weight_parts(across_head, head)):
+        arrived(3 + i, part, across)
+        send(5 + i, part, part, mate)
+    out_ring.arrive(2)
+    out_ring.start(3)
+    for i, part in enumerate(weight_parts(mate_head, head)):
+        arrived(7 + i, part, mate)
+    for i, part in enumerate(weight_parts(3 - head, head)):
+        arrived(5 + i, part, mate)
 
     key_values = pl.ds(width, 2 * HEAD_DIM)
 
@@ -596,7 +631,7 @@
 
         lax.fori_loop(0, 4, turn, 0)
 
-    project(pl.ds(QW, 2 * HEAD_DIM), key_values)
+    project(key_columns, key_values)
     kv_both[pl.ds(group, group), :] = stream[:, key_values]
     kv_copy = remote(
         kv_both.at[pl.ds(group, group)],
@@ -614,11 +649,21 @@
     def _():
         kv_both[pl.ds(0, group), :] = jnp.zeros((group, 2 * HEAD_DIM), low)
 
-    out_ring.arrive(2)
-    out_ring.start(3)
-    project(pl.ds(band, width), pl.ds(0, width))
+    out_ring.arrive(3)
+    out_ring.start(4)
+    pump(2)
+    project(band(head), pl.ds(0, width))
     for i in range(4, 8):
         kv_turned[:, i * rows : (i + 1) * rows] = kv_both[i * rows : (i + 1) * rows, :].T
+    out_ring.arrive(4)
+    half = width // 2
+
+    def out_part(of, i):
+        return out_all.at[pl.ds(pl.multiple_of(of * width + i * half, 64), half)]
+
+    for i in range(2):
+        send(12 + i, out_part(head, i), out_part(head, i), across)
+    send(16, out_all.at[band(head)], out_all.at[band(head)], mate)
 
     @pl.when(me > 0)
     def _():
@@ -626,8 +671,6 @@
 
     for i in range(4):
         kv_turned[:, i * rows : (i + 1) * rows] = kv_both[i * rows : (i + 1) * rows, :].T
-    out_ring.arrive(3)
-    out_ring.start(4)
 
     def attend_tile(tile, carry):
         start = pl.multiple_of(tile * QUERY_TILE, QUERY_TILE)
@@ -656,53 +699,49 @@
 
     lax.fori_loop(0, group // QUERY_TILE, attend_tile, 0)
 
-    gateup_ring.arrive(2)
-    gateup_ring.start(3)
-    down_ring.arrive(2)
-    down_ring.start(3)
-
     def turn_back(i, carry):
         here = pl.ds(pl.multiple_of(i * rows, rows), rows)
         mixed_group[here, :] = mul(shuffle[:, here], mixed[...], TN).astype(low)
         return carry
 
     lax.fori_loop(0, 4, turn_back, 0)
-    out_ring.arrive(4)
-
-    def projection(i):
-        return mul(mixed_group[i * rows : (i + 1) * rows, :], out_rows[...], NN)
-
-    part_out[0] = projection(3).astype(low)
-    send(10, part_out.at[0], part_in.at[0], mate)
-    part_out[1] = projection(1).astype(low)
-    send(11, part_out.at[1], part_in.at[1], mate)
-    resid[...] = projection(2)
-    arrived(10, part_in.at[0], mate)
-    part_out[2] = (resid[...] + part_in[0].astype(full)).astype(low)
-    send(12, part_out.at[2], part_in.at[2], across)
-    resid[...] = projection(0) + tokens[...].astype(full)
-    arrived(11, part_in.at[1], mate)
-    resid[...] += part_in[1].astype(full)
-    arrived(8, quarter(grad_group, 2), across)
-    send(13, quarter(grad_group, 2), quarter(grad_group, 3), mate)
-    arrived(12, part_in.at[2], across)
-    resid[...] += part_in[2].astype(full)
-    values = resid[...]
-    normed_group[pl.ds(0, rows), :] = (values * inverse_norm(values) * gains[1:2, :]).astype(low)
-    send(14, quarter(normed_group, 0), quarter(normed_group, 2), across)
-    send(15, quarter(normed_group, 0), quarter(normed_group, 1), mate)
-    gateup_ring.arrive(3)
-    gateup_ring.start(4)
-    down_ring.arrive(3)
-    down_ring.start(4)
-    arrived(14, quarter(normed_group, 2), across)
-    send(16, quarter(normed_group, 2), quarter(normed_group, 3), mate)
-    arrived(9, quarter(grad_group, 1), mate)
-    arrived(13, quarter(grad_group, 3), mate)
-    arrived(15, quarter(normed_group, 1), mate)
-    arrived(16, quarter(normed_group, 3), mate)
-    gateup_ring.arrive(4)
-    down_ring.arrive(4)
+
+    def mixed_part(of, i, size):
+        return mixed_all.at[pl.ds(i * size, size), band(of)]
+
+    for i in range(2):
+        source = mixed_group.at[pl.ds(i * 2 * rows, 2 * rows)]
+        send(17 + i, source, mixed_part(head, 1 - i, 2 * rows), across)
+    for i in range(4):
+        send(19 + i, quarter(mixed_group, i), mixed_part(head, i ^ 1, rows), mate)
+    mixed_all[:, band(head)] = mixed_group[...]
+    for i in range(2):
+        arrived(12 + i, out_part(across_head, i), across)
+        send(14 + i, out_part(across_head, i), out_part(across_head, i), mate)
+    pump(3)
+    arrived(16, out_all.at[band(mate_head)], mate)
+    for i in range(2):
+        arrived(14 + i, out_part(3 - head, i), mate)
+    for i in range(4):
+        arrived(19 + i, mixed_part(mate_head, i ^ 1, rows), mate)
+    for i in range(2):
+        arrived(17 + i, mixed_part(across_head, 1 - i, 2 * rows), across)
+        for j in (2 - 2 * i, 3 - 2 * i):
+            part = mixed_part(across_head, j, rows)
+            send(23 + j, part, mixed_part(across_head, j ^ 1, rows), mate)
+    for j in range(4):
+        arrived(23 + j, mixed_part(3 - head, j ^ 1, rows), mate)
+
+    def second(i, carry):
+        here = pl.ds(pl.multiple_of((3 - i) * rows, rows), rows)
+        resid[...] = tokens_group[here, :].astype(full) + mul(mixed_all[here, :], out_all[...], NN)
+        values = resid[...]
+        normed_group[here, :] = (values * inverse_norm(values) * gains[1:2, :]).astype(low)
+        return carry
+
+    lax.fori_loop(0, 4, second, 0)
+    pump(4)
+    pump(5)
     for ring in rings:
         ring.finish()
     for copy in copies:
@@ -713,34 +752,37 @@
         kv_copy.wait_send()
 
 
-def forward_section(tokens, cotangent, gains, shards, order, key_ids, query_ids, count):
+def forward_section(tokens, gains, stacks, order, ids, count):
     rows = tokens.shape[0]
     group = 4 * rows
     width = QW // 4
     steps = count // 2
-    qkv_shard, out_shard, gateup_shard, down_shard = shards
+    gateup_rows = stacks[2].shape[0] // GRID * BLK
+    down_parts = stacks[3].shape[0] // 8
     vmem = pl.BlockSpec(memory_space=pltpu.VMEM)
     hbm = pl.BlockSpec(memory_space=pl.ANY)
     outs = [
+        ((2, D), full, vmem),
         ((rows, D), full, vmem),
         ((group, D), low, vmem),
-        ((group, D), low, hbm),
-        ((count,) + gateup_shard.shape, low, hbm),
-        ((count,) + down_shard.shape, low, hbm),
+        ((count, gateup_rows, D), low, hbm),
+        ((count, down_parts, BLK, D // 2), low, hbm),
         ((group, width), low, vmem),
         ((width, QKV), low, vmem),
-        ((width, D), low, vmem),
+        ((D, D), low, vmem),
         ((group, width + 2 * HEAD_DIM), low, vmem),
         ((2 * group, 2 * HEAD_DIM), low, vmem),
         ((2 * HEAD_DIM, 2 * group), low, vmem),
         ((width // HEAD_DIM, 1, group), full, vmem),
         ((group, width), low, vmem),
         ((group, group), low, vmem),
+        ((2 * group, 1), full, vmem),
+        ((1, group), full, vmem),
     ]
     dma = pltpu.SemaphoreType.DMA
     return pl.pallas_call(
         functools.partial(forward_kernel, count),
-        in_specs=[vmem, hbm, vmem, hbm, hbm, hbm, hbm, vmem, vmem, vmem],
+        in_specs=[vmem] * 8,
         out_specs=[spec for _, _, spec in outs],
         out_shape=[jax.ShapeDtypeStruct(shape, kind) for shape, kind, _ in outs],
         scratch_shapes=[
@@ -749,14 +791,17 @@
             pltpu.VMEM((D, QKV), low),
             pltpu.VMEM((group, width + 2 * HEAD_DIM), low),
             pltpu.VMEM((group, width), low),
+            pltpu.VMEM((group, D), low),
             pltpu.VMEM((SPAN, QUERY_TILE), full),
-            pltpu.VMEM((3, rows, D), low),
-            pltpu.VMEM((3, rows, D), low),
-            dma((5,)),
-            dma((4, 2, steps)),
-            dma((4, 2, steps)),
-            dma((17 + 2 * count,)),
-            dma((17 + 2 * count,)),
+            pltpu.VMEM((BLK, D), full),
+            pltpu.VMEM((gateup_rows, D), low),
+            pltpu.VMEM((down_parts, BLK, D // 2), low),
+            pltpu.VMEM((4, count, 8, 128), full),
+            dma((2,)),
+            dma((5, 2, steps)),
+            dma((5, 2, steps)),
+            dma((27,)),
+            dma((27,)),
             dma,
             dma,
         ],
@@ -764,18 +809,7 @@
             collective_id=0, has_side_effects=True, vmem_limit_bytes=58 * 1024 * 1024
         ),
         name="forward_section",
-    )(
-        tokens,
-        cotangent,
-        gains,
-        qkv_shard,
-        out_shard,
-        gateup_shard,
-        down_shard,
-        order,
-        key_ids,
-        query_ids,
-    )
+    )(tokens, gains, *stacks, order, ids)
 
 
 class SumRing:
@@ -1343,35 +1377,40 @@
     )(*values)
 
 
-def update_kernel(rate, w_ref, g_ref, l_ref, r_ref, lr_ref, rr_ref, ln_ref, rn_ref, wn_ref):
-    count, rows, columns = g_ref.shape
-
-    def block(b, carry):
-        grad = g_ref[b]
+def update_kernel(
+    rate, turned, w_ref, g_ref, l_ref, r_ref, lr_ref, rr_ref, ln_ref, rn_ref, wn_ref
+):
+    count, rows, columns = w_ref.shape
+    size = g_ref.shape[1] // count
+    for b in range(count):
+        grad = g_ref[:, b * size : (b + 1) * size]
+        other = grad.T
+        if turned:
+            grad, other = other, grad
         square = jnp.sum(jnp.sum(grad * grad, axis=1, keepdims=True), axis=0, keepdims=True)
         square = square * (1.0 / (rows * columns)) + stat_eps
-        short = grad.astype(low)
-        turned = grad.T.astype(low)
-        ln_ref[b] = 0.5 * l_ref[b] + mul(short, turned, NN) * (0.5 / (columns * square))
-        rn_ref[b] = 0.5 * r_ref[b] + mul(turned, short, NN) * (0.5 / (rows * square))
-        step = mul(lr_ref[b].astype(low), short, NN).astype(low)
+        grad = grad.astype(low)
+        other = other.astype(low)
+        ln_ref[b] = 0.5 * l_ref[b] + mul(grad, other, NN) * (0.5 / (columns * square))
+        rn_ref[b] = 0.5 * r_ref[b] + mul(other, grad, NN) * (0.5 / (rows * square))
+        step = mul(lr_ref[b].astype(low), grad, NN).astype(low)
         step = mul(step, rr_ref[b].astype(low), NN)
         wn_ref[b] = w_ref[b] - step * (rate * lax.rsqrt(square))
-        return carry
-
-    lax.fori_loop(0, count, block, 0, unroll=2 if count % 2 == 0 else 1)
-
-
-def update(weight, grad, left, right, left_root, right_root, rate):
+
+
+def update(weight, grad, left, right, left_root, right_root, rate, turned=False):
     count, rows, columns = weight.shape
-    batch = next(b for b in (8, 6, 4, 3, 2, 1) if count % b == 0)
+    if grad.ndim == 3:
+        grad = grad.transpose(1, 0, 2).reshape(rows, count * columns)
+    height = columns if turned else rows
+    batch = count // (grad.shape[0] // height)
     spec = lambda i, j: pl.BlockSpec((batch, i, j), lambda b: (b, 0, 0))
     return pl.pallas_call(
-        functools.partial(update_kernel, rate),
+        functools.partial(update_kernel, rate, turned),
         grid=(count // batch,),
         in_specs=[
             spec(rows, columns),
-            spec(rows, columns),
+            pl.BlockSpec((height, grad.shape[1]), lambda b: (b, 0)),
             spec(rows, rows),
             spec(columns, columns),
             spec(rows, rows),
@@ -1383,7 +1422,7 @@
             jax.ShapeDtypeStruct(right.shape, full),
             jax.ShapeDtypeStruct(weight.shape, full),
         ],
-        compiler_params=pltpu.CompilerParams(vmem_limit_bytes=24 * 1024 * 1024),
+        compiler_params=pltpu.CompilerParams(vmem_limit_bytes=58 * 1024 * 1024),
         cost_estimate=pl.CostEstimate(
             flops=16 * count * 256 * 256 * 128,
             bytes_accessed=36 * count * rows * 128,
@@ -1403,7 +1442,7 @@
     return lax.rsqrt(jnp.mean(values * values, axis=-1, keepdims=True) + norm_eps)
 
 
-def forward_steps(tokens, cotangent, gain_one, gain_two, stacks, token_order, key_ids, query_ids):
+def forward_steps(tokens, cotangent, attn_gain, ffn_gain, stacks, token_order, sequence_ids):
     qkv_stack, out_stack, gateup_stack, down_stack = stacks
     row_count = tokens.shape[0]
     head_count = lax.axis_size("head")
@@ -1411,6 +1450,27 @@
     group = row_count * head_count
     head_index = lax.axis_index("head")
     local_width = QW // head_count
+    seq_index = lax.axis_index("seq")
+    gains = jnp.concatenate([attn_gain, ffn_gain]).astype(low).astype(full)[None]
+    gains = lax.all_to_all(
+        jnp.broadcast_to(gains, (head_count * seq_count, gains.shape[1])),
+        ("head", "seq"),
+        split_axis=0,
+        concat_axis=0,
+        tiled=True,
+    )
+    own_gains = attn_gain.shape[0]
+    gain_one = gains[:, :own_gains].reshape(1, D)
+    gain_two = gains[:, own_gains:].reshape(1, D)
+
+
+    ids_own = lax.dynamic_slice_in_dim(sequence_ids, seq_index * group, group, 0)
+    ids_before = lax.dynamic_slice_in_dim(
+        sequence_ids, jnp.maximum(seq_index - 1, 0) * group, group, 0
+    )
+    ids_before = jnp.where(seq_index > 0, ids_before, -1)
+    key_ids = jnp.concatenate([ids_before, ids_own])[:, None]
+    query_ids = ids_own[None, :]
     qkv_rows = joined_halves(gather_rows(qkv_stack, 8, to_columns))
     out_rows = joined_halves(gather_rows(out_stack, 8, to_columns))
     gateup = gather_rows(gateup_stack, 16, to_units)
@@ -1441,10 +1501,10 @@
     normed_two = (resid * inverse_norm(resid) * gain_two).astype(low)
     normed_group = jnp.concatenate(head_gather(normed_two))
     grad_group = jnp.concatenate(head_gather(cotangent))
-    return (
+    section = (
+        jnp.concatenate([gain_one, gain_two]),
         resid,
         normed_group,
-        grad_group,
         gateup,
         down,
         features,
@@ -1456,7 +1516,10 @@
         lse,
         mixed_group,
         shuffle,
-    )
+        key_ids,
+        query_ids,
+    )
+    return grad_group, section
 
 
 def backward_steps(
@@ -1579,60 +1642,42 @@
     seq_index = lax.axis_index("seq")
     local_width = QW // head_count
 
-    gains = jnp.concatenate([attn_gain, ffn_gain]).astype(low).astype(full)[None]
-    gains = lax.all_to_all(
-        jnp.broadcast_to(gains, (device_count, gains.shape[1])),
-        ("head", "seq"),
-        split_axis=0,
-        concat_axis=0,
-        tiled=True,
-    )
     own_gains = attn_gain.shape[0]
-    gain_one = gains[:, :own_gains].reshape(1, D)
-    gain_two = gains[:, own_gains:].reshape(1, D)
-
-    ids_own = lax.dynamic_slice_in_dim(sequence_ids, seq_index * group, group, 0)
-    ids_before = lax.dynamic_slice_in_dim(
-        sequence_ids, jnp.maximum(seq_index - 1, 0) * group, group, 0
-    )
-    ids_before = jnp.where(seq_index > 0, ids_before, -1)
-    key_ids = jnp.concatenate([ids_before, ids_own])[:, None]
-    query_ids = ids_own[None, :]
     stacks = (qkv_stack, out_stack, gateup_stack, down_stack)
     whole_rows = all(s.shape[0] % u == 0 for s, u in zip(stacks, (8, 8, 16, 8)))
     if whole_rows:
-        layouts = (to_columns, to_columns, to_units, to_columns)
-        shards = [turn(s.astype(low)) for s, turn in zip(stacks, layouts)]
-        shards = (shards[0][0], shards[1][0], shards[2].reshape(-1, D), shards[3])
+        tile = jnp.concatenate([attn_gain[None], ffn_gain[None]])
         section = forward_section(
             tokens,
-            cotangent,
-            jnp.concatenate([gain_one, gain_two]),
-            shards,
-            token_order[:, None],
-            key_ids,
-            query_ids,
+            jnp.pad(tile, ((0, 6), (0, 128 - own_gains))),
+            stacks,
+            token_order[None, :],
+            sequence_ids[None, :],
             seq_count,
         )
+        cotangent_late, section = lax.optimization_barrier((cotangent, section))
+        grad_group = jnp.concatenate(head_gather(cotangent_late))
     else:
-        section = forward_steps(
-            tokens, cotangent, gain_one, gain_two, stacks, token_order, key_ids, query_ids
+        grad_group, section = forward_steps(
+            tokens, cotangent, attn_gain, ffn_gain, stacks, token_order, sequence_ids
         )
     (
+        gains_both,
         resid,
         normed_group,
-        grad_group,
         gateup,
         down,
         features,
         qkv_rows,
-        out_rows,
+        out_all,
         stream,
         kv_both,
         kv_turned,
         lse,
         mixed_group,
         shuffle,
+        key_ids,
+        query_ids,
     ) = section
     gateup = gateup.reshape(-1, D)
     down = joined_halves(down.reshape(-1, BLK, D // 2))
@@ -1652,7 +1697,10 @@
     gateup_wgrad = mul(gate_up_grad, normed_group, NN, low).reshape(2 * unit_count, BLK, D)
     down_wgrad = split_halves(mul(hidden, grad_group, NN, low), BLK)
     ffn_part = mul(hidden, down, TN, low)
-    gains_both = jnp.concatenate([gain_one, gain_two])
+    out_rows = out_all
+    if whole_rows:
+        start = lax.axis_index("head") * local_width
+        out_rows = lax.dynamic_slice_in_dim(out_all, start, local_width, 0)
     kept = (features, qkv_rows, out_rows, stream, kv_both, kv_turned, lse, mixed_group, shuffle)
     counts = [s.shape[0] for s in stacks]
     if whole_rows:
@@ -1672,10 +1720,8 @@
                 query_ids,
             )
         )
-        gateup_grad_own = from_units(gateup_own.reshape(-1, BLK, D))
-        down_grad_own = from_columns(down_own.reshape(-1, BLK, D // 2))
-        qkv_grad_own = from_columns(qkv_own[None])
-        out_grad_own = from_columns(out_own[None])
+        gateup_grad_own, down_grad_own = gateup_own, down_own
+        qkv_grad_own, out_grad_own = qkv_own, out_own
     else:
         section = backward_steps(
             tokens, cotangent, gains_both, resid, normed_part, ffn_part, gateup_wgrad, down_wgrad, *kept,
@@ -1699,6 +1745,7 @@
         gateup_left_root,
         gateup_right_root,
         0.5 * D ** (-0.5),
+        whole_rows,
     )
     down_new = update(
         down_stack,

time: 559 us -> 471 us (0.84)
  local copies, waits for them, and re-layouts: 82 us -> 36.2 us
  Pallas kernels: 394 us -> 369 us
  starting transfers between devices: 11.3 us -> 4.02 us
  other arithmetic: 11.4 us -> 4.29 us
    another operation x11 -> x0, local copies, waits for them, and re-layouts: 22.7 us -> none  [the longest x6 11.8 us: from_columns(): rows.reshape(n, i, 8, j // 8).transpose(0, 2, 1, 3)]
    pallas_call x5, Pallas kernels: 223 us -> 202 us  [the longest x1 177 us: forward_section(): pl.pallas_call(functools.partial(forward_kernel, count), in_specs=[vmem]...]
    reshape x5 -> x0, local copies, waits for them, and re-layouts: 7.47 us -> none  [the longest x2 3.38 us: to_columns(): stack.reshape(n // 8, 8, i, j).transpose(0, 2, 1, 3)]
    all_to_all x1 -> x0, starting transfers between devices: 7.3 us -> none  [on_device(): lax.all_to_all(jnp.broadcast_to(gains, (device_count, gains.shape[1])), (...]
    unnamed x69 -> x30, local copies, waits for them, and re-layouts: 20.8 us -> 14.9 us
  transfers between devices with their start and end apart: 2 -> 4, of which waited for: 0 -> 0; matrix products, arithmetic and copies ran while one was open for 7% -> 7% of each run, Pallas kernels for 4% -> 5%
where the time goes in v3:
time: 471 us; the launch traced here: 463 us
  Pallas kernels  369 us (78%)
  matrix products  48.2 us (10%)
  local copies, waits for them, and re-layouts  36.2 us (8%)
    pallas_call x1, Pallas kernels, forward_section(): pl.pallas_call(functools.partial(forward_kernel, count), in_specs=[vmem]...  177 us
    pallas_call x1, Pallas kernels, backward_section(): pl.pallas_call(functools.partial(backward_kernel, count), in_specs=[vmem]...  167 us
    dot_general x6, matrix products, mul(): return lax.dot_general(a, b, dims, preferred_element_type=kind)  48.2 us
    pallas_call x4, Pallas kernels, update(): pl.pallas_call(functools.partial(update_kernel, rate, turned), grid=(coun...  25.3 us
    unnamed x30, local copies, waits for them, and re-layouts  14.9 us
  transfers between devices with their start and end apart: 4, of which 0 were waited for; matrix products, arithmetic and copies ran while one was open for 7% of the time, Pallas kernels for 5%

profile of v3, /device:TPU:0, one launch (start us, length us, event | category | flops | bytes accessed | tf_op | source)
XLA Modules:
  0.0 463.2 jit_solution(11847723629711490680)
XLA Ops:
  0.6 1.3 select_maximum_fusion.own_gains
  1.9 176.5 %forward_section.1 = (f32[2,1536]{1,0:T(2,128)}, f32[256,1536]{1,0:T(8,128)}, bf16[1024,1536]{1,0:T(8,128)(2,1)}, bf16[8,288,1536]{2,1,0:T(8,128)(2,1)}, bf16[8,...) custom-call(bf16[256,1536]{1,0:T(8,128)(2,1)} %tokens.3, ...), custom_call_target="tpu_custom_call" | custom-call | tf_op jit(solution)/shard_map/forward_section/pallas_call | solution.py:783
  178.5 0.8 collective-permute-start.1
  179.2 0.0 collective-permute-start
  179.3 0.0 copy-start.8
  179.3 5.8 %copy.67 = bf16[12,2,96,768]{3,1,2,0:T(2,128)(2,1)S(1)} copy(bf16[12,2,96,768]{3,2,1,0:T(8,128)(2,1)} %bitcast.79) | data formatting | bytes 7077888 | tf_op jit(solution)/shard_map/reshape;reshape | solution.py:155
  185.0 0.0 copy-start.7
  185.1 0.7 copy.62
  185.8 0.0 copy-done.8
  185.8 2.3 copy-done.7
  188.1 7.5 %fusion = f32[12,2,96,1024]{3,2,0,1:T(8,128)S(1)} fusion(bf16[12,2,96,1536]{3,2,1,0:T(8,128)(2,1)S(1)} %bitcast.88, bf16[1024,1536]{1,0:T(8,128)(2,1)S(1)} %copy-done.8), kind=kOutput, calls=%fused_computation.1 | convolution fusion | flops 7247757312 | bytes 19660800 | tf_op jit(solution)/shard_map/dot_general | solution.py:38
  195.6 0.0 copy-start
  195.6 1.8 fusion.17
  197.5 1.8 copy-done
  199.3 0.0 copy-start.3
  199.3 5.8 %fusion.34.ffn_part = bf16[1024,1536]{1,0:T(8,128)(2,1)} fusion(bf16[1152,1024]{1,0:T(8,128)(2,1)S(1)} %bitcast.83, bf16[1152,1536]{1,0:T(8,128)(2,1)S(1)} %bitcast.80), kind=kOutput, calls=%fused_computation.51 | convolution fusion | flops 3623878656 | bytes 9043968 | tf_op jit(solution)/shard_map/dot_general | solution.py:38
  205.1 0.0 copy-done.3
  205.1 0.0 collective-permute-done.1
  205.1 0.5 collective-permute-start.2
  205.6 2.1 constant_dynamic-update-slice_fusion.3
  207.6 4.0 dot_general.26
  211.6 2.4 constant_dynamic-slice_fusion.out_rows
  214.0 0.0 collective-permute-done
  214.0 2.1 constant_dynamic-update-slice_fusion.2
  216.1 2.1 constant_dynamic-update-slice_fusion.1
  218.1 0.0 collective-permute-done.2
  218.1 2.1 constant_dynamic-update-slice_fusion
  220.2 0.0 copy-start.1
  220.2 4.8 %copy.61 = bf16[1536,1024]{1,0:T(8,128)(2,1)} copy(bf16[1536,1024]{0,1:T(8,128)(2,1)} %bitcast.76) | data formatting | bytes 6291456 | tf_op jit(solution)/shard_map/dot_general | solution.py:38
  225.0 0.0 copy-done.1
  225.0 10.7 %fusion.8 = (bf16[12,1,96,1024]{3,2,0,1:T(8,128)(2,1)S(1)}, bf16[12,1,96,1024]{3,2,0,1:T(8,128)(2,1)S(1)}) fusion(f32[12,2,96,1024]{3,2,0,1:T(8,128)} %copy-done, bf16[12,96,1536]{2,1,0:T(8,128)(2,1)} %dot_general.26, bf16[1024,1536]{1,0:T(8,128)(2,1)S(1)} %copy-done.1), kind=kOutput, calls=%fused_computation.12 | convolution fusion | flops 3652190208 | bytes 20840448 | tf_op jit(solution)/shard_map/dot_general | solution.py:38
  235.7 0.4 maximum_convert_fusion
  236.2 0.0 copy-start.2
  236.2 0.0 copy-start.4
  236.2 0.8 copy.55
  237.0 1.1 copy-done.2
  238.1 0.7 copy-done.4
  238.8 0.0 copy-start.9
  238.8 0.0 slice-start
  238.8 5.3 %fusion.27 = bf16[12,96,2,768]{3,1,2,0:T(8,128)(2,1)} fusion(bf16[2,768,1024,1]{2,1,0,3:T(8,128)(2,1)S(1)} %bitcast.82, bf16[12,1,96,1024]{3,2,0,1:T(8,128)(2,1)S(1)} %copy-done.4), kind=kOutput, calls=%fused_computation.34 | convolution fusion | flops 3623878656 | bytes 9043968 | tf_op jit(solution)/shard_map/dot_general | solution.py:38
  244.1 0.0 copy-done.9
  244.1 9.2 %fusion.22.gateup_parts = bf16[8,288,1536]{2,1,0:T(8,128)(2,1)} fusion(bf16[8,288,1024]{2,1,0:T(8,128)(2,1)S(1)} %bitcast.77, bf16[1024,1536]{1,0:T(8,128)(2,1)S(1)} %copy-done.9), kind=kOutput, calls=%fused_computation.29 | convolution fusion | flops 7247757312 | bytes 14942208 | tf_op jit(solution)/shard_map/dot_general | solution.py:38
  253.4 0.0 slice-done
  253.4 0.0 slice-done.1
  253.4 9.7 %fusion.33.normed_part = bf16[1024,1536]{1,0:T(8,128)(2,1)} fusion(bf16[2304,1024]{1,0:T(8,128)(2,1)S(1)} %bitcast.78, bf16[2304,1536]{1,0:T(8,128)(2,1)S(1)} %bitcast.91), kind=kOutput, calls=%fused_computation.50 | convolution fusion | flops 7247757312 | bytes 14942208 | tf_op jit(solution)/shard_map/dot_general | solution.py:38
  263.0 167.4 %backward_section.1 = (bf16[256,1536]{1,0:T(8,128)(2,1)}, f32[256,1536]{1,0:T(8,128)}, f32[2,1536]{1,0:T(2,128)}, f32[288,1536]{1,0:T(8,128)}, f32[288,768]{1,0:...) custom-call(bf16[256,1536]{1,0:T(8,128)(2,1)} %tokens.3, ...), custom_call_target="tpu_custom_call" | custom-call | tf_op jit(solution)/shard_map/backward_section/pallas_call | solution.py:1336
  430.4 0.8 slice_reduce_fusion.1
  431.3 0.1 reshape_squeeze.6
  431.3 0.1 reshape_squeeze.7
  431.4 0.7 pad_maximum_fusion
  432.1 2.7 all-to-all-start
  434.8 3.6 update.5
  438.4 6.7 %update.7 = (f32[24,96,96]{2,1,0:T(8,128)}, f32[24,96,96]{2,1,0:T(8,128)}, f32[24,96,96]{2,1,0:T(8,128)}) custom-call(f32[24,96,96]{2,1,0:T(8,128)} %w_ref.7, f32[288,768]{1,0:T(8,128)} %get-tuple-element.116.g_ref, f32[24,96,96]{2,1,0:T(8,128)} %l_ref.7, f32[24,96,96]{2,1,0:T(8,128)} %r_ref.7, f32[24,96,96]{2,1,0:T(8,128)} %lr_ref.7, f32[24,96,96]{2,1,0:T(8,128)} %rr_ref.7), custom_call_target="tpu_custom_call" | custom-call | flops 3221225472 | bytes 10616832 | tf_op jit(solution)/shard_map/update/pallas_call | solution.py:1408
  445.1 11.1 %update.6 = (f32[48,96,96]{2,1,0:T(8,128)}, f32[48,96,96]{2,1,0:T(8,128)}, f32[48,96,96]{2,1,0:T(8,128)}) custom-call(f32[48,96,96]{2,1,0:T(8,128)} %w_ref.6, f32[288,1536]{1,0:T(8,128)} %get-tuple-element.112.g_ref, f32[48,96,96]{2,1,0:T(8,128)} %l_ref.6, f32[48,96,96]{2,1,0:T(8,128)} %r_ref.6, f32[48,96,96]{2,1,0:T(8,128)} %lr_ref.6, f32[48,96,96]{2,1,0:T(8,128)} %rr_ref.6), custom_call_target="tpu_custom_call" | custom-call | flops 6442450944 | bytes 21233664 | tf_op jit(solution)/shard_map/update/pallas_call | solution.py:1408
  456.1 0.0 copy-start.6
  456.1 0.0 copy-start.5
  456.1 3.9 update.4
  460.1 0.0 all-to-all-done
  460.1 0.1 reduce_sum.9
  460.2 0.6 fusion.30
  460.7 0.0 copy-done.6
  460.7 0.9 copy.73
  461.6 0.0 copy-done.5
  461.6 1.1 copy.74
  (2 shorter events, 0.0 us)
Async XLA Ops:
  178.5 26.6 %collective-permute-start.1 = (bf16[256,1536]{1,0:T(8,128)(2,1)}, bf16[256,1536]{1,0:T(8,128)(2,1)}, u32[]{:S(2)}, u32[]{:S(2)}) collective-permute-start(bf16[256,1536]{1,0:T(8,128)(2,1)} %cotangent.1), channel_id=1, source_target_pairs={{0,16},{8,24},{16,0},{24,8},{1,17},{9,25},{17,1},{25,9},{2,18},{10... | collective-permute-start | bytes 2359304 | tf_op jit(solution)/shard_map/ppermute | solution.py:168
  179.2 34.7 %collective-permute-start = (bf16[256,1536]{1,0:T(8,128)(2,1)}, bf16[256,1536]{1,0:T(8,128)(2,1)}, u32[]{:S(2)}, u32[]{:S(2)}) collective-permute-start(bf16[256,1536]{1,0:T(8,128)(2,1)} %cotangent.1), channel_id=1, source_target_pairs={{0,8},{8,0},{16,24},{24,16},{1,9},{9,1},{17,25},{25,17},{2,10},{10... | collective-permute-start | bytes 2359304 | tf_op jit(solution)/shard_map/ppermute | solution.py:168
  179.3 6.5 %copy-start.8 = (bf16[1024,1536]{1,0:T(8,128)(2,1)S(1)}, bf16[1024,1536]{1,0:T(8,128)(2,1)}, u32[]{:S(2)}) copy-start(bf16[1024,1536]{1,0:T(8,128)(2,1)} %get-tuple-element.89) | copy-start | bytes 9437188
  185.0 3.0 copy-start.7
  195.6 3.7 copy-start
  199.3 5.8 %copy-start.3 = (bf16[12,1,96,1024]{3,2,0,1:T(8,128)(2,1)}, bf16[12,1,96,1024]{3,2,0,1:T(8,128)(2,1)S(1)}, u32[]{:S(2)}) copy-start(bf16[12,1,96,1024]{3,2,0,1:T(8,128)(2,1)S(1)} %fusion.17) | copy-start | bytes 7077892
  205.1 13.1 %collective-permute-start.2 = (bf16[256,1536]{1,0:T(8,128)(2,1)}, bf16[256,1536]{1,0:T(8,128)(2,1)}, u32[]{:S(2)}, u32[]{:S(2)}) collective-permute-start(bf16[256,1536]{1,0:T(8,128)(2,1)} %collective-permute-done.1), channel_id=1, source_target_pairs={{0,8},{8,0},{16,24},{24,16},{1,9},{9,1},{17,25},{25,17},{2,10},{10... | collective-permute-start | bytes 2359304 | tf_op jit(solution)/shard_map/ppermute | solution.py:168
  220.2 4.8 %copy-start.1 = (bf16[1024,1536]{1,0:T(8,128)(2,1)S(1)}, bf16[1024,1536]{1,0:T(8,128)(2,1)}, u32[]{:S(2)}) copy-start(bf16[1024,1536]{1,0:T(8,128)(2,1)} %constant_dynamic-update-slice_fusion) | copy-start | bytes 9437188
  236.2 1.9 copy-start.2
  236.2 2.6 copy-start.4
  238.8 5.3 %copy-start.9 = (bf16[1024,1536]{1,0:T(8,128)(2,1)S(1)}, bf16[1024,1536]{1,0:T(8,128)(2,1)}, u32[]{:S(2)}) copy-start(bf16[1024,1536]{1,0:T(8,128)(2,1)} %get-tuple-element.89) | copy-start | bytes 9437188
  238.8 14.6 %slice-start = ((s8[7077888]{0:T(1024)(128)(4,1)}), s8[4194304]{0:T(1024)(128)(4,1)S(1)}, s32[]{:S(2)}) async-start(s8[7077888]{0:T(1024)(128)(4,1)} %bitcast.89), calls=%async_computation.1 | async-start | bytes 8388608
  244.1 9.2 %slice-start.1 = ((s8[7077888]{0:T(1024)(128)(4,1)}), s8[2883584]{0:T(1024)(128)(4,1)S(1)}, s32[]{:S(2)}) async-start(s8[7077888]{0:T(1024)(128)(4,1)} %bitcast.89), calls=%async_computation.2 | async-start | bytes 5767168
  432.1 28.0 %all-to-all-start = ((f32[32,1,96]{2,1,0:T(1,128)}), f32[32,1,96]{2,1,0:T(1,128)S(1)}, u32[]{:S(2)}, u32[]{:S(2)}) async-start(f32[32,1,96]{2,1,0:T(1,128)} %bitcast.26), calls=%async_computation | async-start | bytes 32768 | tf_op jit(solution)/shard_map/all_to_all | solution.py:1735
  456.1 4.6 copy-start.6
  456.1 5.5 %copy-start.5 = (f32[256,1536]{1,0:T(8,128)S(1)}, f32[256,1536]{1,0:T(8,128)}, u32[]{:S(2)}) copy-start(f32[256,1536]{1,0:T(8,128)} %get-tuple-element.145) | copy-start | bytes 4718596

commit v4 on v3

--- a/solution.py
+++ b/solution.py
@@ -157,10 +157,9 @@
 
 def split_halves(matrix, i):
     rows, columns = matrix.shape
-    m = rows // i
-    return (
-        matrix.reshape(m, i, 2, columns // 2).transpose(0, 2, 1, 3).reshape(2 * m, i, columns // 2)
-    )
+    half = columns // 2
+    parts = [matrix[:, at : at + half].reshape(rows // i, i, half) for at in (0, half)]
+    return jnp.stack(parts, axis=1).reshape(2 * rows // i, i, half)
 
 
 def to_partner(value, which):
@@ -384,6 +383,7 @@
 def forward_kernel(
     count,
     tokens,
+    cotangent,
     own_gains,
     qkv_stack,
     out_stack,
@@ -394,6 +394,7 @@
     gains,
     resid,
     normed_group,
+    grad_group,
     gateup,
     down,
     features,
@@ -415,6 +416,7 @@
     mixed_all,
     bias,
     wide,
+    tall,
     gateup_own,
     down_own,
     gain_tiles,
@@ -499,8 +501,8 @@
         size = stack.shape[2]
         blocks = 8
         for c in range(blocks):
-            wide[:, c * size : (c + 1) * size] = stack[first + c]
-        return wide[:, : blocks * size].astype(low)
+            tall[c * size : (c + 1) * size, :] = stack[first + c].T
+        return tall[: blocks * size, :].T.astype(low)
 
     qkv_view(me, None)[...] = side_by_side(qkv_stack, 0)
     gain_tiles[head, me] = own_gains[...]
@@ -510,19 +512,19 @@
     qkv_ring.start(1)
     gain_ring.start(1)
     for q in range(gateup_own.shape[0] // BLK):
-        for r in range(GRID):
-            wide[:, r * BLK : (r + 1) * BLK] = gateup_stack[q * GRID + r].T
-        gateup_own[q * BLK : (q + 1) * BLK, :] = wide[:, :D].astype(low)
+        column = gateup_stack[q * GRID : (q + 1) * GRID].reshape(D, BLK)
+        gateup_own[q * BLK : (q + 1) * BLK, :] = column.T.astype(low)
     for m in range(down_own.shape[0]):
         down_own[m] = side_by_side(down_stack, 8 * m)
     own = [
         pltpu.make_async_copy(gateup_own, gateup.at[me], own_sem.at[0]),
         pltpu.make_async_copy(down_own, down.at[me], own_sem.at[1]),
+        pltpu.make_async_copy(cotangent, quarter(grad_group, 0), own_sem.at[2]),
     ]
     for copy in own:
         copy.start()
     out_view(me, None)[...] = side_by_side(out_stack, 0)
-    for copy in own:
+    for copy in own[:2]:
         copy.wait()
 
     def pump(step):
@@ -568,14 +570,15 @@
     def weight_parts(of, chip_of):
         return [weights.at[band(of), columns] for columns in (chip_columns(chip_of), key_columns)]
 
+    gain_ring.arrive(count // 2)
+    send(9, gain_tiles.at[head], gain_tiles.at[head], across)
+    send(10, gain_tiles.at[head], gain_tiles.at[head], mate)
     for i, part in enumerate(weight_parts(head, across_head)):
         send(3 + i, part, part, across)
     for i, part in enumerate(weight_parts(head, head)):
         send(7 + i, part, part, mate)
-    gain_ring.arrive(count // 2)
-    send(9, gain_tiles.at[head], gain_tiles.at[head], across)
-    send(10, gain_tiles.at[head], gain_tiles.at[head], mate)
     out_ring.start(1)
+    pump(2)
     arrived(0, quarter(tokens_group, 2), across)
     send(2, quarter(tokens_group, 2), quarter(tokens_group, 3), mate)
     qkv_rows[...] = weights[band(head), :]
@@ -611,6 +614,8 @@
     out_ring.start(3)
     for i, part in enumerate(weight_parts(mate_head, head)):
         arrived(7 + i, part, mate)
+    send(27, cotangent, quarter(grad_group, 2), across)
+    send(28, cotangent, quarter(grad_group, 1), mate)
     for i, part in enumerate(weight_parts(3 - head, head)):
         arrived(5 + i, part, mate)
 
@@ -651,8 +656,8 @@
 
     out_ring.arrive(3)
     out_ring.start(4)
-    pump(2)
     project(band(head), pl.ds(0, width))
+    pump(3)
     for i in range(4, 8):
         kv_turned[:, i * rows : (i + 1) * rows] = kv_both[i * rows : (i + 1) * rows, :].T
     out_ring.arrive(4)
@@ -671,6 +676,8 @@
 
     for i in range(4):
         kv_turned[:, i * rows : (i + 1) * rows] = kv_both[i * rows : (i + 1) * rows, :].T
+    arrived(27, quarter(grad_group, 2), across)
+    send(29, quarter(grad_group, 2), quarter(grad_group, 3), mate)
 
     def attend_tile(tile, carry):
         start = pl.multiple_of(tile * QUERY_TILE, QUERY_TILE)
@@ -718,7 +725,7 @@
     for i in range(2):
         arrived(12 + i, out_part(across_head, i), across)
         send(14 + i, out_part(across_head, i), out_part(across_head, i), mate)
-    pump(3)
+    pump(4)
     arrived(16, out_all.at[band(mate_head)], mate)
     for i in range(2):
         arrived(14 + i, out_part(3 - head, i), mate)
@@ -740,8 +747,10 @@
         return carry
 
     lax.fori_loop(0, 4, second, 0)
-    pump(4)
+    arrived(28, quarter(grad_group, 1), mate)
+    arrived(29, quarter(grad_group, 3), mate)
     pump(5)
+    own[2].wait()
     for ring in rings:
         ring.finish()
     for copy in copies:
@@ -752,7 +761,7 @@
         kv_copy.wait_send()
 
 
-def forward_section(tokens, gains, stacks, order, ids, count):
+def forward_section(tokens, cotangent, gains, stacks, order, ids, count):
     rows = tokens.shape[0]
     group = 4 * rows
     width = QW // 4
@@ -765,6 +774,7 @@
         ((2, D), full, vmem),
         ((rows, D), full, vmem),
         ((group, D), low, vmem),
+        ((group, D), low, hbm),
         ((count, gateup_rows, D), low, hbm),
         ((count, down_parts, BLK, D // 2), low, hbm),
         ((group, width), low, vmem),
@@ -782,7 +792,7 @@
     dma = pltpu.SemaphoreType.DMA
     return pl.pallas_call(
         functools.partial(forward_kernel, count),
-        in_specs=[vmem] * 8,
+        in_specs=[vmem] * 9,
         out_specs=[spec for _, _, spec in outs],
         out_shape=[jax.ShapeDtypeStruct(shape, kind) for shape, kind, _ in outs],
         scratch_shapes=[
@@ -793,15 +803,16 @@
             pltpu.VMEM((group, width), low),
             pltpu.VMEM((group, D), low),
             pltpu.VMEM((SPAN, QUERY_TILE), full),
-            pltpu.VMEM((BLK, D), full),
+            pltpu.VMEM((8, D), full),
+            pltpu.VMEM((QKV // 2, BLK), full),
             pltpu.VMEM((gateup_rows, D), low),
             pltpu.VMEM((down_parts, BLK, D // 2), low),
             pltpu.VMEM((4, count, 8, 128), full),
-            dma((2,)),
+            dma((3,)),
             dma((5, 2, steps)),
             dma((5, 2, steps)),
-            dma((27,)),
-            dma((27,)),
+            dma((30,)),
+            dma((30,)),
             dma,
             dma,
         ],
@@ -809,7 +820,7 @@
             collective_id=0, has_side_effects=True, vmem_limit_bytes=58 * 1024 * 1024
         ),
         name="forward_section",
-    )(tokens, gains, *stacks, order, ids)
+    )(tokens, cotangent, gains, *stacks, order, ids)
 
 
 class SumRing:
@@ -1377,15 +1388,105 @@
     )(*values)
 
 
+def ffn_kernel(
+    normed, cotangent, gateup, down, hidden, gate_up_grad, normed_part, ffn_part, normed_sum, ffn_sum
+):
+    units = down.shape[0]
+    tile = next(u for u in (4, 3, 2, 1) if units % u == 0)
+    size = normed.shape[0]
+    half = D // 2
+    root = (2.0 / 3.141592653589793) ** 0.5
+
+    def step(c, carry):
+        here = pl.ds(pl.multiple_of(c * tile * BLK, 32), tile * BLK)
+        pair = pl.ds(pl.multiple_of(c * tile * 2 * BLK, 64), 2 * tile * BLK)
+        weights = gateup[pair, :]
+        parts = [down[pl.ds(c * tile, tile), i].reshape(tile * BLK, half) for i in range(2)]
+        both = mul(weights, normed[...], NT).reshape(tile, 2, BLK, size)
+        gate = both[:, 0].reshape(tile * BLK, size)
+        upper = both[:, 1].reshape(tile * BLK, size)
+        grad = mul(parts[0], cotangent[:, :half], NT) + mul(parts[1], cotangent[:, half:], NT)
+        square = gate * gate
+        bent = jnp.tanh(root * gate * (1.0 + 0.044715 * square))
+        share = 0.5 * (1.0 + bent)
+        active = gate * share
+        slope = share + 0.5 * gate * (1.0 - bent * bent) * (root * (1.0 + 0.134145 * square))
+        units_out = (active * upper).astype(low)
+        grads = [(grad * upper * slope).astype(low), (grad * active).astype(low)]
+        grads = [g.reshape(tile, 1, BLK, size) for g in grads]
+        grads = jnp.concatenate(grads, axis=1).reshape(2 * tile * BLK, size)
+        hidden[here, :] = units_out
+        gate_up_grad[pair, :] = grads
+        first = c == 0
+        term = mul(grads, weights, TN)
+        terms = [mul(units_out, part, TN) for part in parts]
+
+        @pl.when(first)
+        def _():
+            normed_sum[...] = term
+            ffn_sum[:, :half] = terms[0]
+            ffn_sum[:, half:] = terms[1]
+
+        @pl.when(jnp.logical_not(first))
+        def _():
+            normed_sum[...] += term
+            ffn_sum[:, :half] += terms[0]
+            ffn_sum[:, half:] += terms[1]
+
+        return carry
+
+    lax.fori_loop(0, units // tile, step, 0)
+    normed_part[...] = normed_sum[...].astype(low)
+    ffn_part[...] = ffn_sum[...].astype(low)
+
+
+def feed_forward(normed, cotangent, gateup, down):
+    group = normed.shape[0]
+    units = down.shape[0]
+    size = min(512, group)
+    rows = pl.BlockSpec((size, D), lambda t: (t, 0))
+    once = pl.Buffered(1)
+    return pl.pallas_call(
+        ffn_kernel,
+        grid=(group // size,),
+        in_specs=[
+            rows,
+            rows,
+            pl.BlockSpec(gateup.shape, lambda t: (0, 0), pipeline_mode=once),
+            pl.BlockSpec(down.shape, lambda t: (0, 0, 0, 0), pipeline_mode=once),
+        ],
+        out_specs=[
+            pl.BlockSpec((units * BLK, size), lambda t: (0, t)),
+            pl.BlockSpec((2 * units * BLK, size), lambda t: (0, t)),
+            rows,
+            rows,
+        ],
+        out_shape=[
+            jax.ShapeDtypeStruct((units * BLK, group), low),
+            jax.ShapeDtypeStruct((2 * units * BLK, group), low),
+            jax.ShapeDtypeStruct((group, D), low),
+            jax.ShapeDtypeStruct((group, D), low),
+        ],
+        scratch_shapes=[pltpu.VMEM((size, D), full), pltpu.VMEM((size, D), full)],
+        compiler_params=pltpu.CompilerParams(vmem_limit_bytes=58 * 1024 * 1024),
+        cost_estimate=pl.CostEstimate(
+            flops=12 * units * BLK * group * D,
+            bytes_accessed=40 << 20,
+            transcendentals=units * BLK * group,
+        ),
+        name="feed_forward",
+    )(normed, cotangent, gateup, down)
+
+
 def update_kernel(
     rate, turned, w_ref, g_ref, l_ref, r_ref, lr_ref, rr_ref, ln_ref, rn_ref, wn_ref
 ):
     count, rows, columns = w_ref.shape
-    size = g_ref.shape[1] // count
+    blocks = g_ref[...].T.reshape(count, g_ref.shape[1] // count, g_ref.shape[0])
     for b in range(count):
-        grad = g_ref[:, b * size : (b + 1) * size]
+        grad = blocks[b]
         other = grad.T
-        if turned:
+        if not turned:
             grad, other = other, grad
         square = jnp.sum(jnp.sum(grad * grad, axis=1, keepdims=True), axis=0, keepdims=True)
         square = square * (1.0 / (rows * columns)) + stat_eps
@@ -1505,6 +1606,7 @@
         jnp.concatenate([gain_one, gain_two]),
         resid,
         normed_group,
+        grad_group,
         gateup,
         down,
         features,
@@ -1519,7 +1621,7 @@
         key_ids,
         query_ids,
     )
-    return grad_group, section
+    return section
 
 
 def backward_steps(
@@ -1649,22 +1751,22 @@
         tile = jnp.concatenate([attn_gain[None], ffn_gain[None]])
         section = forward_section(
             tokens,
+            cotangent,
             jnp.pad(tile, ((0, 6), (0, 128 - own_gains))),
             stacks,
             token_order[None, :],
             sequence_ids[None, :],
             seq_count,
         )
-        cotangent_late, section = lax.optimization_barrier((cotangent, section))
-        grad_group = jnp.concatenate(head_gather(cotangent_late))
     else:
-        grad_group, section = forward_steps(
+        section = forward_steps(
             tokens, cotangent, attn_gain, ffn_gain, stacks, token_order, sequence_ids
         )
     (
         gains_both,
         resid,
         normed_group,
+        grad_group,
         gateup,
         down,
         features,
@@ -1680,29 +1782,21 @@
         query_ids,
     ) = section
     gateup = gateup.reshape(-1, D)
-    down = joined_halves(down.reshape(-1, BLK, D // 2))
-    unit_count = down.shape[0] // BLK
-
-    gate_up = mul(gateup, normed_group, NT).reshape(unit_count, 2, BLK, group)
-    hidden, act_pull = jax.vjp(
-        lambda g, u: jax.nn.gelu(g, approximate=True) * u, gate_up[:, 0], gate_up[:, 1]
-    )
-    hidden = hidden.astype(low).reshape(unit_count * BLK, group)
-    hidden_grad = mul(down, grad_group, NT).reshape(unit_count, BLK, group)
-    gate_grad, up_grad = act_pull(hidden_grad)
-    gate_up_grad = (
-        jnp.stack([gate_grad, up_grad], axis=1).astype(low).reshape(2 * unit_count * BLK, group)
-    )
-    normed_part = mul(gate_up_grad, gateup, TN, low)
-    gateup_wgrad = mul(gate_up_grad, normed_group, NN, low).reshape(2 * unit_count, BLK, D)
+    down = down.reshape(-1, 2, BLK, D // 2)
+    unit_count = down.shape[0]
+    hidden, gate_up_grad, normed_part, ffn_part = feed_forward(
+        normed_group, grad_group, gateup, down
+    )
+    gateup_wgrad = mul(gate_up_grad, normed_group, NN, low)
     down_wgrad = split_halves(mul(hidden, grad_group, NN, low), BLK)
-    ffn_part = mul(hidden, down, TN, low)
     out_rows = out_all
     if whole_rows:
         start = lax.axis_index("head") * local_width
         out_rows = lax.dynamic_slice_in_dim(out_all, start, local_width, 0)
     kept = (features, qkv_rows, out_rows, stream, kv_both, kv_turned, lse, mixed_group, shuffle)
     counts = [s.shape[0] for s in stacks]
+    if not whole_rows:
+        gateup_wgrad = gateup_wgrad.reshape(2 * unit_count, BLK, D)
     if whole_rows:
         (block_out, input_grad, gain_grads, gateup_own, down_own, qkv_own, out_own, *_) = (
             backward_section(

time: 471 us -> 420 us (0.89); the launches traced: 463 us -> 419 us
  matrix products: 48.2 us -> 15.1 us
  local copies, waits for them, and re-layouts: 36.2 us -> 7.81 us
  Pallas kernels: 369 us -> 389 us
    pallas_call x0 -> x1, Pallas kernels: none -> 37.7 us  [feed_forward(): pl.pallas_call(ffn_kernel, grid=(group // size,), in_specs=[rows, rows, p...]
    dot_general x6 -> x2, matrix products: 48.2 us -> 15.1 us  [mul(): return lax.dot_general(a, b, dims, preferred_element_type=kind)]
    pallas_call x1, Pallas kernels: 177 us -> 159 us  [forward_section(): pl.pallas_call(functools.partial(forward_kernel, count), in_specs=[vmem]...]
    unnamed x30 -> x12, local copies, waits for them, and re-layouts: 14.9 us -> 3.67 us
    dot_general x2 -> x0, local copies, waits for them, and re-layouts: 8.78 us -> none  [mul(): return lax.dot_general(a, b, dims, preferred_element_type=kind)]
    another operation x1 -> x0, local copies, waits for them, and re-layouts: 5.79 us -> none  [joined_halves(): rows.reshape(n // 2, 2, i, j).transpose(0, 2, 1, 3)]
  transfers between devices with their start and end apart: 4 -> 1, of which waited for: 0 -> 0; matrix products, arithmetic and copies ran while one was open for 7% -> 0% of each run, Pallas kernels for 5% -> 5%
where the time goes in v4:
time: 420 us; the launch traced here: 419 us
  Pallas kernels  389 us (93%)
  matrix products  15.1 us (4%)
  local copies, waits for them, and re-layouts  7.81 us (2%)
    pallas_call x1, Pallas kernels, backward_section(): pl.pallas_call(functools.partial(backward_kernel, count), in_specs=[vmem]...  169 us
    pallas_call x1, Pallas kernels, forward_section(): pl.pallas_call(functools.partial(forward_kernel, count), in_specs=[vmem]...  159 us
    pallas_call x1, Pallas kernels, feed_forward(): pl.pallas_call(ffn_kernel, grid=(group // size,), in_specs=[rows, rows, p...  37.7 us
    pallas_call x4, Pallas kernels, update(): pl.pallas_call(functools.partial(update_kernel, rate, turned), grid=(coun...  22.5 us
    dot_general x2, matrix products, mul(): return lax.dot_general(a, b, dims, preferred_element_type=kind)  15.1 us
  transfers between devices with their start and end apart: 1, of which 0 were waited for; matrix products, arithmetic and copies ran while one was open for 0% of the time, Pallas kernels for 5%

profile of v4, /device:TPU:0, one launch (start us, length us, event | category | flops | bytes accessed | tf_op | source)
XLA Modules:
  0.0 419.4 jit_solution(9876967851882386535)
XLA Ops:
  0.7 1.3 select_maximum_fusion.own_gains
  1.9 159.4 %forward_section.1 = (f32[2,1536]{1,0:T(2,128)}, f32[256,1536]{1,0:T(8,128)}, bf16[1024,1536]{1,0:T(8,128)(2,1)}, bf16[1024,1536]{1,0:T(8,128)(2,1)}, bf16[8,288...) custom-call(bf16[256,1536]{1,0:T(8,128)(2,1)} %tokens.3, ...), custom_call_target="tpu_custom_call" | custom-call | tf_op jit(solution)/shard_map/forward_section/pallas_call | solution.py:793
  161.3 0.0 copy-start.3
  161.3 37.7 %feed_forward.1 = (bf16[1152,1024]{1,0:T(8,128)(2,1)}, bf16[2304,1024]{1,0:T(8,128)(2,1)}, bf16[1024,1536]{1,0:T(8,128)(2,1)}, bf16[1024,1536]{1,0:T(8,128)(2,1)}) custom-call(bf16[1024,1536]{1,0:T(8,128)(2,1)} %get-tuple-element.58.normed, bf16[1024,1536]{1,0:T(8,128)(2,1)} %get-tuple-element.59.cotangent, bf16[2304,1536]{1,0:T(8,128)(2,1)} %bitcast.27, ...), custom_call_target="tpu_custom_call" | custom-call | flops 21743271936 | bytes 41943040 | tf_op jit(solution)/shard_map/feed_forward/pallas_call | solution.py:1449
  199.0 0.0 copy-done.3
  199.0 0.0 copy-start.4
  199.0 5.9 %fusion.3 = bf16[1152,1536]{1,0:T(8,128)(2,1)S(1)} fusion(bf16[1152,1024]{1,0:T(8,128)(2,1)} %get-tuple-element.65, bf16[1024,1536]{1,0:T(8,128)(2,1)S(1)} %copy-done.3), kind=kOutput, calls=%fused_computation.11 | convolution fusion | flops 3623878656 | bytes 9043968 | tf_op jit(solution)/shard_map/dot_general | solution.py:38
  204.9 0.0 copy-start.2
  204.9 0.2 fusion
  205.2 0.0 copy-done.4
  205.2 1.6 copy-done.2
  206.8 9.2 %fusion.2 = bf16[2304,1536]{1,0:T(8,128)(2,1)} fusion(bf16[2304,1024]{1,0:T(8,128)(2,1)S(1)} %copy-done.4, bf16[1024,1536]{1,0:T(8,128)(2,1)S(1)} %copy-done.2), kind=kOutput, calls=%fused_computation.10 | convolution fusion | flops 7247757312 | bytes 14942208 | tf_op jit(solution)/shard_map/dot_general | solution.py:38
  216.0 2.4 constant_dynamic-slice_fusion.out_rows
  218.4 2.1 pad_maximum_fusion
  220.5 169.0 %backward_section.1 = (bf16[256,1536]{1,0:T(8,128)(2,1)}, f32[256,1536]{1,0:T(8,128)}, f32[2,1536]{1,0:T(2,128)}, f32[288,1536]{1,0:T(8,128)}, f32[288,768]{1,0:...) custom-call(bf16[256,1536]{1,0:T(8,128)(2,1)} %tokens.3, ...), custom_call_target="tpu_custom_call" | custom-call | tf_op jit(solution)/shard_map/backward_section/pallas_call | solution.py:1347
  389.5 0.8 slice_reduce_fusion.1
  390.3 0.1 reshape_squeeze.6
  390.4 0.1 reshape_squeeze.7
  390.4 0.7 pad_maximum_fusion.1
  391.1 3.1 all-to-all-start
  394.2 3.2 update.5
  397.4 6.2 %update.7 = (f32[24,96,96]{2,1,0:T(8,128)}, f32[24,96,96]{2,1,0:T(8,128)}, f32[24,96,96]{2,1,0:T(8,128)}) custom-call(f32[24,96,96]{2,1,0:T(8,128)} %w_ref.7, f32[288,768]{1,0:T(8,128)} %get-tuple-element.92.g_ref, f32[24,96,96]{2,1,0:T(8,128)} %l_ref.7, f32[24,96,96]{2,1,0:T(8,128)} %r_ref.7, f32[24,96,96]{2,1,0:T(8,128)} %lr_ref.7, f32[24,96,96]{2,1,0:T(8,128)} %rr_ref.7), custom_call_target="tpu_custom_call" | custom-call | flops 3221225472 | bytes 10616832 | tf_op jit(solution)/shard_map/update/pallas_call | solution.py:1509
  403.6 9.4 %update.6 = (f32[48,96,96]{2,1,0:T(8,128)}, f32[48,96,96]{2,1,0:T(8,128)}, f32[48,96,96]{2,1,0:T(8,128)}) custom-call(f32[48,96,96]{2,1,0:T(8,128)} %w_ref.6, f32[288,1536]{1,0:T(8,128)} %get-tuple-element.88.g_ref, f32[48,96,96]{2,1,0:T(8,128)} %l_ref.6, f32[48,96,96]{2,1,0:T(8,128)} %r_ref.6, f32[48,96,96]{2,1,0:T(8,128)} %lr_ref.6, f32[48,96,96]{2,1,0:T(8,128)} %rr_ref.6), custom_call_target="tpu_custom_call" | custom-call | flops 6442450944 | bytes 21233664 | tf_op jit(solution)/shard_map/update/pallas_call | solution.py:1509
  413.1 0.0 copy-start.1
  413.1 0.0 copy-start
  413.1 3.7 update.4
  416.8 0.0 all-to-all-done
  416.8 0.1 reduce_sum.9
  416.8 0.6 fusion.1
  417.4 0.0 copy-done.1
  417.4 0.9 copy.48
  418.3 0.0 copy-done
  418.3 1.1 copy.49
Async XLA Ops:
  161.3 37.7 %copy-start.3 = (bf16[1024,1536]{1,0:T(8,128)(2,1)S(1)}, bf16[1024,1536]{1,0:T(8,128)(2,1)}, u32[]{:S(2)}) copy-start(bf16[1024,1536]{1,0:T(8,128)(2,1)} %get-tuple-element.59.cotangent) | copy-start | bytes 9437188
  199.0 6.1 %copy-start.4 = (bf16[2304,1024]{1,0:T(8,128)(2,1)S(1)}, bf16[2304,1024]{1,0:T(8,128)(2,1)}, u32[]{:S(2)}) copy-start(bf16[2304,1024]{1,0:T(8,128)(2,1)} %get-tuple-element.64) | copy-start | bytes 14155780
  204.9 1.9 copy-start.2
  391.1 25.6 %all-to-all-start = ((f32[32,1,96]{2,1,0:T(1,128)}), f32[32,1,96]{2,1,0:T(1,128)S(1)}, u32[]{:S(2)}, u32[]{:S(2)}) async-start(f32[32,1,96]{2,1,0:T(1,128)} %bitcast.12), calls=%async_computation | async-start | bytes 32768 | tf_op jit(solution)/shard_map/all_to_all | solution.py:1829
  413.1 4.3 %copy-start.1 = (bf16[256,1536]{1,0:T(8,128)(2,1)S(1)}, bf16[256,1536]{1,0:T(8,128)(2,1)}, u32[]{:S(2)}) copy-start(bf16[256,1536]{1,0:T(8,128)(2,1)} %get-tuple-element.118) | copy-start | bytes 2359300
  413.1 5.2 %copy-start = (f32[256,1536]{1,0:T(8,128)S(1)}, f32[256,1536]{1,0:T(8,128)}, u32[]{:S(2)}) copy-start(f32[256,1536]{1,0:T(8,128)} %get-tuple-element.119) | copy-start | bytes 4718596

commit v5 on v4

--- a/solution.py
+++ b/solution.py
@@ -1001,7 +1001,7 @@
     down_parts,
     features,
     qkv_rows,
-    out_rows,
+    out_all,
     stream,
     kv_both,
     kv_turned,
@@ -1031,6 +1031,7 @@
     sum_out,
     sum_in,
     proj_group,
+    turned_out,
     turned_grad,
     grad_stream,
     kv_total,
@@ -1165,23 +1166,21 @@
         values, inverse, gains[1:2, :], normed_two_grad
     )
     proj_group[quarter(0), :] = input_grad[...].astype(low)
+
+    def back_projection(of):
+        weights = out_all[pl.ds(pl.multiple_of(of * width, 128), width), :]
+        return mul(proj_group[quarter(0), :], weights, NT).astype(low)
+
+    for j, of, where in ((2, across_head, across), (3, 3 - head, corner), (1, mate_head, mate)):
+        turned_out[j - 1] = back_projection(of)
+        send(31 + j, turned_out.at[j - 1], turned_grad.at[quarter(j)], where)
     send(6, proj_group.at[quarter(0)], proj_group.at[quarter(2)], across)
     send(7, proj_group.at[quarter(0)], proj_group.at[quarter(1)], mate)
+    turned_grad[quarter(0), :] = back_projection(head)
     gateup_ring.step(1)
     down_ring.step(1)
-    sum_across(3, 3, ffn_part)
-
-    def back_projection(i):
-        turned_grad[quarter(i), :] = mul(proj_group[quarter(i), :], out_rows[...], NT).astype(low)
-
-    back_projection(0)
-    arrived(7, proj_group.at[quarter(1)], mate)
-    back_projection(1)
-    arrived(6, proj_group.at[quarter(2)], across)
-    send(8, proj_group.at[quarter(2)], proj_group.at[quarter(3)], mate)
-    back_projection(2)
-    arrived(8, proj_group.at[quarter(3)], mate)
-    back_projection(3)
+    for j, where in ((1, mate), (2, across), (3, corner)):
+        arrived(31 + j, turned_grad.at[quarter(j)], where)
 
     def turn(i, carry):
         here = pl.ds(pl.multiple_of(i * rows, rows), rows)
@@ -1189,12 +1188,6 @@
         return carry
 
     lax.fori_loop(0, 4, turn, 0)
-    for i in range(3):
-        at = slice(i * (D // 3), (i + 1) * (D // 3))
-        out_local[:, at] = mul(mixed_group[...], proj_group[:, at], TN).astype(low)
-    out_ring.start()
-    gateup_ring.step(2)
-    down_ring.step(2)
 
     kv_total[...] = jnp.zeros_like(kv_total)
 
@@ -1226,7 +1219,14 @@
 
         return lax.fori_loop(0, heads, back_head, carry)
 
-    lax.fori_loop(0, group // QUERY_TILE, back_tile, 0)
+    tiles = group // QUERY_TILE
+    lax.fori_loop(0, tiles // 2, back_tile, 0)
+    arrived(6, proj_group.at[quarter(2)], across)
+    send(8, proj_group.at[quarter(2)], proj_group.at[quarter(3)], mate)
+    sum_across(3, 3, ffn_part)
+    gateup_ring.step(2)
+    down_ring.step(2)
+    lax.fori_loop(tiles // 2, tiles, back_tile, 0)
     kv_out[...] = kv_total[:group, :].astype(low)
     kv_copy = remote(kv_out, kv_in, kv_send, kv_recv, {"seq": lax.rem(me + count - 1, count)})
 
@@ -1258,7 +1258,12 @@
     swapped(13, all_grad, lanes(head), 1, mate)
     gateup_ring.step(3)
     down_ring.step(3)
-    out_ring.step(1)
+    arrived(7, proj_group.at[quarter(1)], mate)
+    arrived(8, proj_group.at[quarter(3)], mate)
+    for i in range(3):
+        at = slice(i * (D // 3), (i + 1) * (D // 3))
+        out_local[:, at] = mul(mixed_group[...], proj_group[:, at], TN).astype(low)
+    out_ring.start()
 
     @pl.when(me < count - 1)
     def _():
@@ -1279,15 +1284,23 @@
         arrived(17 + i, kv_mate.at[1, quarter(i ^ 1)], mate)
     kv_total[pl.ds(0, group), :] = kv_mate[0].astype(full) + kv_mate[1].astype(full)
     kv_mate[2] = kv_total[pl.ds(0, group), :].astype(low)
+    mine = pl.ds(pl.multiple_of(lax.rem(head, 2) * HEAD_DIM, HEAD_DIM), HEAD_DIM)
+    of_mine = pl.ds(pl.multiple_of(QW + lax.rem(head, 2) * HEAD_DIM, HEAD_DIM), HEAD_DIM)
+    of_mate = pl.ds(pl.multiple_of(QW + lax.rem(mate_head, 2) * HEAD_DIM, HEAD_DIM), HEAD_DIM)
     for i in range(4):
-        send(21 + i, kv_mate.at[2, quarter(i)], kv_mate.at[3, quarter(i ^ 2)], across)
+        send(21 + i, kv_mate.at[2, quarter(i), mine], kv_mate.at[3, quarter(i ^ 2), mine], across)
+    out_ring.step(1)
     swapped_arrived(9, all_grad, lanes(across_head), 2, across)
     swapped(25, all_grad, lanes(across_head), 1, mate)
     out_ring.step(2)
     swapped_arrived(13, all_grad, lanes(mate_head), 1, mate)
     for i in range(4):
-        arrived(21 + i, kv_mate.at[3, quarter(i ^ 2)], across)
-    all_grad[:, QW:] = (kv_total[pl.ds(0, group), :] + kv_mate[3].astype(full)).astype(low)
+        arrived(21 + i, kv_mate.at[3, quarter(i ^ 2), mine], across)
+    all_grad[:, of_mine] = (
+        kv_total[pl.ds(0, group), mine] + kv_mate[3, :, mine].astype(full)
+    ).astype(low)
+    swapped(35, all_grad, of_mine, 1, mate)
+    swapped_arrived(35, all_grad, of_mate, 1, mate)
     swapped_arrived(25, all_grad, lanes(3 - head), 1, mate)
 
     for i in range(2):
@@ -1299,10 +1312,8 @@
         feature_grad[quarter(i), :] = mul(all_grad[quarter(i), :], qkv_rows[...], NT).astype(low)
         send(28 + i, feature_grad.at[quarter(i)], normed_grad.at[:, lanes(head)], where)
     normed_grad[:, lanes(head)] = mul(all_grad[quarter(0), :], qkv_rows[...], NT).astype(low)
+    qkv_ring.step(1)
     block_out[...] = (resid[...] + sum_last(3, 3, ffn_part)).astype(low)
-    gateup_ring.finish(gateup_grad)
-    down_ring.finish(down_grad)
-    qkv_ring.step(1)
     for i, where, of in ((2, across, across_head), (3, corner, 3 - head), (1, mate, mate_head)):
         arrived(28 + i, normed_grad.at[:, lanes(of)], where)
     qkv_ring.step(2)
@@ -1312,6 +1323,8 @@
     gain_grads[0:1, :] = jnp.sum(normed_one_grad * values * inverse, axis=0, keepdims=True)
     input_grad[...] += norm_back(values, inverse, gains[0:1, :], normed_one_grad)
     qkv_ring.step(3)
+    gateup_ring.finish(gateup_grad)
+    down_ring.finish(down_grad)
     out_ring.finish(out_grad)
     qkv_ring.finish(qkv_grad)
     for copy in copies:
@@ -1362,6 +1375,7 @@
             pltpu.VMEM((2, rows, D), low),
             pltpu.VMEM((6, rows, D), low),
             pltpu.VMEM((group, D), low),
+            pltpu.VMEM((3, rows, width), low),
             pltpu.VMEM((group, width), low),
             pltpu.VMEM((group, width), low),
             pltpu.VMEM((2 * group, 2 * HEAD_DIM), full),
@@ -1376,13 +1390,13 @@
             dma,
             dma((4, 2, steps)),
             dma((4, 2, steps)),
-            dma((32,)),
-            dma((32,)),
+            dma((39,)),
+            dma((39,)),
             dma,
             dma,
         ],
         compiler_params=pltpu.CompilerParams(
-            collective_id=1, has_side_effects=True, vmem_limit_bytes=60 * 1024 * 1024
+            collective_id=1, has_side_effects=True, vmem_limit_bytes=63 * 1024 * 1024
         ),
         name="backward_section",
     )(*values)
@@ -1392,7 +1406,7 @@
     normed, cotangent, gateup, down, hidden, gate_up_grad, normed_part, ffn_part, normed_sum, ffn_sum
 ):
     units = down.shape[0]
-    tile = next(u for u in (4, 3, 2, 1) if units % u == 0)
+    tile = next(u for u in (6, 4, 3, 2, 1) if units % u == 0)
     size = normed.shape[0]
     half = D // 2
     root = (2.0 / 3.141592653589793) ** 0.5
@@ -1789,11 +1803,7 @@
     )
     gateup_wgrad = mul(gate_up_grad, normed_group, NN, low)
     down_wgrad = split_halves(mul(hidden, grad_group, NN, low), BLK)
-    out_rows = out_all
-    if whole_rows:
-        start = lax.axis_index("head") * local_width
-        out_rows = lax.dynamic_slice_in_dim(out_all, start, local_width, 0)
-    kept = (features, qkv_rows, out_rows, stream, kv_both, kv_turned, lse, mixed_group, shuffle)
+    kept = (features, qkv_rows, out_all, stream, kv_both, kv_turned, lse, mixed_group, shuffle)
     counts = [s.shape[0] for s in stacks]
     if not whole_rows:
         gateup_wgrad = gateup_wgrad.reshape(2 * unit_count, BLK, D)

time: 420 us -> 424 us (level)
  no operation moved by 1% of the time
where the time goes in v5:
time: 424 us; the launch traced here: 419 us
  Pallas kernels  391 us (92%)
  matrix products  15.3 us (4%)
  local copies, waits for them, and re-layouts  5.46 us (1%)
    pallas_call x1, Pallas kernels, backward_section(): pl.pallas_call(functools.partial(backward_kernel, count), in_specs=[vmem]...  172 us
    pallas_call x1, Pallas kernels, forward_section(): pl.pallas_call(functools.partial(forward_kernel, count), in_specs=[vmem]...  159 us
    pallas_call x1, Pallas kernels, feed_forward(): pl.pallas_call(ffn_kernel, grid=(group // size,), in_specs=[rows, rows, p...  36.7 us
    pallas_call x4, Pallas kernels, update(): pl.pallas_call(functools.partial(update_kernel, rate, turned), grid=(coun...  22.5 us
    dot_general x2, matrix products, mul(): return lax.dot_general(a, b, dims, preferred_element_type=kind)  15.3 us
  transfers between devices with their start and end apart: 1, of which 0 were waited for; matrix products, arithmetic and copies ran while one was open for 0% of the time, Pallas kernels for 5%

profile of v5, /device:TPU:0, one launch (start us, length us, event | category | flops | bytes accessed | tf_op | source)
XLA Modules:
  0.0 419.3 jit_solution(11650365303689357002)
XLA Ops:
  0.6 1.3 select_maximum_fusion.own_gains
  1.9 159.4 %forward_section.1 = (f32[2,1536]{1,0:T(2,128)}, f32[256,1536]{1,0:T(8,128)}, bf16[1024,1536]{1,0:T(8,128)(2,1)}, bf16[1024,1536]{1,0:T(8,128)(2,1)}, bf16[8,288...) custom-call(bf16[256,1536]{1,0:T(8,128)(2,1)} %tokens.3, ...), custom_call_target="tpu_custom_call" | custom-call | tf_op jit(solution)/shard_map/forward_section/pallas_call | solution.py:793
  161.3 0.0 copy-start.3
  161.3 36.7 %feed_forward.1 = (bf16[1152,1024]{1,0:T(8,128)(2,1)}, bf16[2304,1024]{1,0:T(8,128)(2,1)}, bf16[1024,1536]{1,0:T(8,128)(2,1)}, bf16[1024,1536]{1,0:T(8,128)(2,1)}) custom-call(bf16[1024,1536]{1,0:T(8,128)(2,1)} %get-tuple-element.58.normed, bf16[1024,1536]{1,0:T(8,128)(2,1)} %get-tuple-element.59.cotangent, bf16[2304,1536]{1,0:T(8,128)(2,1)} %bitcast.27, ...), custom_call_target="tpu_custom_call" | custom-call | flops 21743271936 | bytes 41943040 | tf_op jit(solution)/shard_map/feed_forward/pallas_call | solution.py:1463
  198.0 0.0 copy-done.3
  198.0 0.0 copy-start.4
  198.1 6.1 %fusion.3 = bf16[1152,1536]{1,0:T(8,128)(2,1)S(1)} fusion(bf16[1152,1024]{1,0:T(8,128)(2,1)} %get-tuple-element.65, bf16[1024,1536]{1,0:T(8,128)(2,1)S(1)} %copy-done.3), kind=kOutput, calls=%fused_computation.10 | convolution fusion | flops 3623878656 | bytes 9043968 | tf_op jit(solution)/shard_map/dot_general | solution.py:38
  204.1 0.0 copy-start.2
  204.2 0.2 fusion
  204.4 0.0 copy-done.4
  204.4 1.6 copy-done.2
  206.0 9.2 %fusion.2 = bf16[2304,1536]{1,0:T(8,128)(2,1)} fusion(bf16[2304,1024]{1,0:T(8,128)(2,1)S(1)} %copy-done.4, bf16[1024,1536]{1,0:T(8,128)(2,1)S(1)} %copy-done.2), kind=kOutput, calls=%fused_computation.9 | convolution fusion | flops 7247757312 | bytes 14942208 | tf_op jit(solution)/shard_map/dot_general | solution.py:38
  215.2 2.1 pad_maximum_fusion
  217.3 171.9 %backward_section.1 = (bf16[256,1536]{1,0:T(8,128)(2,1)}, f32[256,1536]{1,0:T(8,128)}, f32[2,1536]{1,0:T(2,128)}, f32[288,1536]{1,0:T(8,128)}, f32[288,768]{1,0:...) custom-call(bf16[256,1536]{1,0:T(8,128)(2,1)} %tokens.3, ...), custom_call_target="tpu_custom_call" | custom-call | tf_op jit(solution)/shard_map/backward_section/pallas_call | solution.py:1360
  389.2 0.8 slice_reduce_fusion.1
  390.0 0.1 reshape_squeeze.6
  390.1 0.1 reshape_squeeze.7
  390.2 0.7 pad_maximum_fusion.1
  390.9 2.8 all-to-all-start
  393.6 3.2 update.5
  396.8 6.2 %update.7 = (f32[24,96,96]{2,1,0:T(8,128)}, f32[24,96,96]{2,1,0:T(8,128)}, f32[24,96,96]{2,1,0:T(8,128)}) custom-call(f32[24,96,96]{2,1,0:T(8,128)} %w_ref.7, f32[288,768]{1,0:T(8,128)} %get-tuple-element.92.g_ref, f32[24,96,96]{2,1,0:T(8,128)} %l_ref.7, f32[24,96,96]{2,1,0:T(8,128)} %r_ref.7, f32[24,96,96]{2,1,0:T(8,128)} %lr_ref.7, f32[24,96,96]{2,1,0:T(8,128)} %rr_ref.7), custom_call_target="tpu_custom_call" | custom-call | flops 3221225472 | bytes 10616832 | tf_op jit(solution)/shard_map/update/pallas_call | solution.py:1523
  403.0 9.4 %update.6 = (f32[48,96,96]{2,1,0:T(8,128)}, f32[48,96,96]{2,1,0:T(8,128)}, f32[48,96,96]{2,1,0:T(8,128)}) custom-call(f32[48,96,96]{2,1,0:T(8,128)} %w_ref.6, f32[288,1536]{1,0:T(8,128)} %get-tuple-element.88.g_ref, f32[48,96,96]{2,1,0:T(8,128)} %l_ref.6, f32[48,96,96]{2,1,0:T(8,128)} %r_ref.6, f32[48,96,96]{2,1,0:T(8,128)} %lr_ref.6, f32[48,96,96]{2,1,0:T(8,128)} %rr_ref.6), custom_call_target="tpu_custom_call" | custom-call | flops 6442450944 | bytes 21233664 | tf_op jit(solution)/shard_map/update/pallas_call | solution.py:1523
  412.5 0.0 copy-start.1
  412.5 0.0 copy-start
  412.5 3.7 update.4
  416.2 0.0 all-to-all-done
  416.2 0.1 reduce_sum.9
  416.2 0.6 fusion.1
  416.8 0.0 copy-done.1
  416.8 0.9 copy.48
  417.7 0.0 copy-done
  417.7 1.1 copy.49
Async XLA Ops:
  161.3 36.8 %copy-start.3 = (bf16[1024,1536]{1,0:T(8,128)(2,1)S(1)}, bf16[1024,1536]{1,0:T(8,128)(2,1)}, u32[]{:S(2)}) copy-start(bf16[1024,1536]{1,0:T(8,128)(2,1)} %get-tuple-element.59.cotangent) | copy-start | bytes 9437188
  198.0 6.3 %copy-start.4 = (bf16[2304,1024]{1,0:T(8,128)(2,1)S(1)}, bf16[2304,1024]{1,0:T(8,128)(2,1)}, u32[]{:S(2)}) copy-start(bf16[2304,1024]{1,0:T(8,128)(2,1)} %get-tuple-element.64) | copy-start | bytes 14155780
  204.1 1.9 copy-start.2
  390.9 25.3 %all-to-all-start = ((f32[32,1,96]{2,1,0:T(1,128)}), f32[32,1,96]{2,1,0:T(1,128)S(1)}, u32[]{:S(2)}, u32[]{:S(2)}) async-start(f32[32,1,96]{2,1,0:T(1,128)} %bitcast.12), calls=%async_computation | async-start | bytes 32768 | tf_op jit(solution)/shard_map/all_to_all | solution.py:1839
  412.5 4.3 %copy-start.1 = (bf16[256,1536]{1,0:T(8,128)(2,1)S(1)}, bf16[256,1536]{1,0:T(8,128)(2,1)}, u32[]{:S(2)}) copy-start(bf16[256,1536]{1,0:T(8,128)(2,1)} %get-tuple-element.118) | copy-start | bytes 2359300
  412.5 5.2 %copy-start = (f32[256,1536]{1,0:T(8,128)S(1)}, f32[256,1536]{1,0:T(8,128)}, u32[]{:S(2)}) copy-start(f32[256,1536]{1,0:T(8,128)} %get-tuple-element.119) | copy-start | bytes 4718596

commit v6 on v5

--- a/solution.py
+++ b/solution.py
@@ -397,15 +397,15 @@
     grad_group,
     gateup,
     down,
-    features,
-    qkv_rows,
-    out_all,
-    stream,
-    kv_both,
-    kv_turned,
+    features_out,
+    qkv_rows_out,
+    out_all_out,
+    stream_out,
+    kv_both_out,
+    kv_turned_out,
     lse,
-    mixed_group,
-    shuffle,
+    mixed_group_out,
+    shuffle_out,
     key_ids,
     query_ids,
     tokens_group,
@@ -427,6 +427,15 @@
     head_recv,
     kv_send,
     kv_recv,
+    features,
+    qkv_rows,
+    out_all,
+    stream,
+    kv_both,
+    kv_turned,
+    mixed_group,
+    shuffle,
+    store_sem,
 ):
     rows = tokens.shape[0]
     group = 4 * rows
@@ -739,6 +748,24 @@
     for j in range(4):
         arrived(23 + j, mixed_part(3 - head, j ^ 1, rows), mate)
 
+    stores = [
+        pltpu.make_async_copy(source, target, store_sem.at[i])
+        for i, (source, target) in enumerate(
+            (
+                (features, features_out),
+                (qkv_rows, qkv_rows_out),
+                (out_all, out_all_out),
+                (stream, stream_out),
+                (kv_both, kv_both_out),
+                (kv_turned, kv_turned_out),
+                (mixed_group, mixed_group_out),
+                (shuffle, shuffle_out),
+            )
+        )
+    ]
+    for copy in stores:
+        copy.start()
+
     def second(i, carry):
         here = pl.ds(pl.multiple_of((3 - i) * rows, rows), rows)
         resid[...] = tokens_group[here, :].astype(full) + mul(mixed_all[here, :], out_all[...], NN)
@@ -751,6 +778,8 @@
     arrived(29, quarter(grad_group, 3), mate)
     pump(5)
     own[2].wait()
+    for copy in stores:
+        copy.wait()
     for ring in rings:
         ring.finish()
     for copy in copies:
@@ -777,15 +806,15 @@
         ((group, D), low, hbm),
         ((count, gateup_rows, D), low, hbm),
         ((count, down_parts, BLK, D // 2), low, hbm),
-        ((group, width), low, vmem),
-        ((width, QKV), low, vmem),
-        ((D, D), low, vmem),
-        ((group, width + 2 * HEAD_DIM), low, vmem),
-        ((2 * group, 2 * HEAD_DIM), low, vmem),
-        ((2 * HEAD_DIM, 2 * group), low, vmem),
+        ((group, width), low, hbm),
+        ((width, QKV), low, hbm),
+        ((D, D), low, hbm),
+        ((group, width + 2 * HEAD_DIM), low, hbm),
+        ((2 * group, 2 * HEAD_DIM), low, hbm),
+        ((2 * HEAD_DIM, 2 * group), low, hbm),
         ((width // HEAD_DIM, 1, group), full, vmem),
-        ((group, width), low, vmem),
-        ((group, group), low, vmem),
+        ((group, width), low, hbm),
+        ((group, group), low, hbm),
         ((2 * group, 1), full, vmem),
         ((1, group), full, vmem),
     ]
@@ -815,6 +844,8 @@
             dma((30,)),
             dma,
             dma,
+            *[pltpu.VMEM(outs[i][0], low) for i in (6, 7, 8, 9, 10, 11, 13, 14)],
+            dma((8,)),
         ],
         compiler_params=pltpu.CompilerParams(
             collective_id=0, has_side_effects=True, vmem_limit_bytes=58 * 1024 * 1024
@@ -999,15 +1030,15 @@
     ffn_part,
     gateup_parts,
     down_parts,
-    features,
-    qkv_rows,
-    out_all,
-    stream,
-    kv_both,
-    kv_turned,
+    features_in,
+    qkv_rows_in,
+    out_all_in,
+    stream_in,
+    kv_both_in,
+    kv_turned_in,
     lse,
-    mixed_group,
-    shuffle,
+    mixed_group_in,
+    shuffle_in,
     key_ids,
     query_ids,
     block_out,
@@ -1050,6 +1081,15 @@
     head_recv,
     kv_send,
     kv_recv,
+    features,
+    qkv_rows,
+    out_all,
+    stream,
+    kv_both,
+    kv_turned,
+    mixed_group,
+    shuffle,
+    take_sem,
 ):
     rows = tokens.shape[0]
     group = 4 * rows
@@ -1152,7 +1192,24 @@
         arrived(base + 2, sum_in.at[slot + 2], across)
         return own + sum_in[slot + 2].astype(full)
 
+    takes = [
+        pltpu.make_async_copy(source, target, take_sem.at[i])
+        for i, (source, target) in enumerate(
+            (
+                (features_in, features),
+                (qkv_rows_in, qkv_rows),
+                (out_all_in, out_all),
+                (stream_in, stream),
+                (kv_both_in, kv_both),
+                (kv_turned_in, kv_turned),
+                (mixed_group_in, mixed_group),
+                (shuffle_in, shuffle),
+            )
+        )
+    ]
     sum_first(0, 0, normed_part)
+    for copy in takes:
+        copy.start()
     gateup_ring.start()
     down_ring.start()
     sum_across(0, 0, normed_part)
@@ -1166,6 +1223,9 @@
         values, inverse, gains[1:2, :], normed_two_grad
     )
     proj_group[quarter(0), :] = input_grad[...].astype(low)
+
+    for copy in takes:
+        copy.wait()
 
     def back_projection(of):
         weights = out_all[pl.ds(pl.multiple_of(of * width, 128), width), :]
@@ -1219,14 +1279,7 @@
 
         return lax.fori_loop(0, heads, back_head, carry)
 
-    tiles = group // QUERY_TILE
-    lax.fori_loop(0, tiles // 2, back_tile, 0)
-    arrived(6, proj_group.at[quarter(2)], across)
-    send(8, proj_group.at[quarter(2)], proj_group.at[quarter(3)], mate)
-    sum_across(3, 3, ffn_part)
-    gateup_ring.step(2)
-    down_ring.step(2)
-    lax.fori_loop(tiles // 2, tiles, back_tile, 0)
+    lax.fori_loop(0, group // QUERY_TILE, back_tile, 0)
     kv_out[...] = kv_total[:group, :].astype(low)
     kv_copy = remote(kv_out, kv_in, kv_send, kv_recv, {"seq": lax.rem(me + count - 1, count)})
 
@@ -1256,8 +1309,11 @@
 
     swapped(9, all_grad, lanes(head), 2, across)
     swapped(13, all_grad, lanes(head), 1, mate)
-    gateup_ring.step(3)
-    down_ring.step(3)
+    arrived(6, proj_group.at[quarter(2)], across)
+    send(8, proj_group.at[quarter(2)], proj_group.at[quarter(3)], mate)
+    gateup_ring.step(2)
+    down_ring.step(2)
+    sum_across(3, 3, ffn_part)
     arrived(7, proj_group.at[quarter(1)], mate)
     arrived(8, proj_group.at[quarter(3)], mate)
     for i in range(3):
@@ -1290,9 +1346,10 @@
     for i in range(4):
         send(21 + i, kv_mate.at[2, quarter(i), mine], kv_mate.at[3, quarter(i ^ 2), mine], across)
     out_ring.step(1)
+    gateup_ring.step(3)
+    down_ring.step(3)
     swapped_arrived(9, all_grad, lanes(across_head), 2, across)
     swapped(25, all_grad, lanes(across_head), 1, mate)
-    out_ring.step(2)
     swapped_arrived(13, all_grad, lanes(mate_head), 1, mate)
     for i in range(4):
         arrived(21 + i, kv_mate.at[3, quarter(i ^ 2), mine], across)
@@ -1307,12 +1364,12 @@
         at = slice(i * (QKV // 2), (i + 1) * (QKV // 2))
         qkv_local[:, at] = mul(features[...], all_grad[:, at], TN).astype(low)
     qkv_ring.start()
-    out_ring.step(3)
     for i, where in ((2, across), (3, corner), (1, mate)):
         feature_grad[quarter(i), :] = mul(all_grad[quarter(i), :], qkv_rows[...], NT).astype(low)
         send(28 + i, feature_grad.at[quarter(i)], normed_grad.at[:, lanes(head)], where)
     normed_grad[:, lanes(head)] = mul(all_grad[quarter(0), :], qkv_rows[...], NT).astype(low)
     qkv_ring.step(1)
+    out_ring.step(2)
     block_out[...] = (resid[...] + sum_last(3, 3, ffn_part)).astype(low)
     for i, where, of in ((2, across, across_head), (3, corner, 3 - head), (1, mate, mate_head)):
         arrived(28 + i, normed_grad.at[:, lanes(of)], where)
@@ -1323,6 +1380,7 @@
     gain_grads[0:1, :] = jnp.sum(normed_one_grad * values * inverse, axis=0, keepdims=True)
     input_grad[...] += norm_back(values, inverse, gains[0:1, :], normed_one_grad)
     qkv_ring.step(3)
+    out_ring.step(3)
     gateup_ring.finish(gateup_grad)
     down_ring.finish(down_grad)
     out_ring.finish(out_grad)
@@ -1359,7 +1417,7 @@
     dma = pltpu.SemaphoreType.DMA
     return pl.pallas_call(
         functools.partial(backward_kernel, count),
-        in_specs=[vmem] * 4 + [hbm] * 4 + [vmem] * 11,
+        in_specs=[vmem] * 4 + [hbm] * 10 + [vmem] + [hbm] * 2 + [vmem] * 2,
         out_specs=[vmem] * 7 + [hbm] * 2,
         out_shape=[jax.ShapeDtypeStruct(shape, kind) for shape, kind in outs],
         scratch_shapes=[
@@ -1394,6 +1452,8 @@
             dma((39,)),
             dma,
             dma,
+            *[pltpu.VMEM(values[i].shape, low) for i in (8, 9, 10, 11, 12, 13, 15, 16)],
+            dma((8,)),
         ],
         compiler_params=pltpu.CompilerParams(
             collective_id=1, has_side_effects=True, vmem_limit_bytes=63 * 1024 * 1024

time: 424 us -> 416 us (0.981)
  Pallas kernels: 391 us -> 380 us
    pallas_call x1, Pallas kernels: 172 us -> 165 us  [backward_section(): pl.pallas_call(functools.partial(backward_kernel, count), in_specs=[vmem]...]
where the time goes in v6:
time: 416 us; the launch traced here: 411 us
  Pallas kernels  380 us (91%)
  matrix products  15.3 us (4%)
  starting transfers between devices  5.54 us (1%)
  local copies, waits for them, and re-layouts  5.46 us (1%)
    pallas_call x1, Pallas kernels, backward_section(): pl.pallas_call(functools.partial(backward_kernel, count), in_specs=[vmem]...  165 us
    pallas_call x1, Pallas kernels, forward_section(): pl.pallas_call(functools.partial(forward_kernel, count), in_specs=[vmem]...  155 us
    pallas_call x1, Pallas kernels, feed_forward(): pl.pallas_call(ffn_kernel, grid=(group // size,), in_specs=[rows, rows, p...  36.7 us
    pallas_call x4, Pallas kernels, update(): pl.pallas_call(functools.partial(update_kernel, rate, turned), grid=(coun...  22.5 us
    dot_general x2, matrix products, mul(): return lax.dot_general(a, b, dims, preferred_element_type=kind)  15.3 us
  transfers between devices with their start and end apart: 1, of which 0 were waited for; matrix products, arithmetic and copies ran while one was open for 0% of the time, Pallas kernels for 5%

profile of v6, /device:TPU:0, one launch (start us, length us, event | category | flops | bytes accessed | tf_op | source)
XLA Modules:
  0.0 411.4 jit_solution(10665865727335001073)
XLA Ops:
  0.6 1.3 select_maximum_fusion.own_gains
  1.9 155.5 %forward_section.1 = (f32[2,1536]{1,0:T(2,128)}, f32[256,1536]{1,0:T(8,128)}, bf16[1024,1536]{1,0:T(8,128)(2,1)}, bf16[1024,1536]{1,0:T(8,128)(2,1)}, bf16[8,288...) custom-call(bf16[256,1536]{1,0:T(8,128)(2,1)} %tokens.3, ...), custom_call_target="tpu_custom_call" | custom-call | tf_op jit(solution)/shard_map/forward_section/pallas_call | solution.py:822
  157.4 0.0 copy-start.3
  157.4 36.7 %feed_forward.1 = (bf16[1152,1024]{1,0:T(8,128)(2,1)}, bf16[2304,1024]{1,0:T(8,128)(2,1)}, bf16[1024,1536]{1,0:T(8,128)(2,1)}, bf16[1024,1536]{1,0:T(8,128)(2,1)}) custom-call(bf16[1024,1536]{1,0:T(8,128)(2,1)} %get-tuple-element.58.normed, bf16[1024,1536]{1,0:T(8,128)(2,1)} %get-tuple-element.59.cotangent, bf16[2304,1536]{1,0:T(8,128)(2,1)} %bitcast.27, ...), custom_call_target="tpu_custom_call" | custom-call | flops 21743271936 | bytes 41943040 | tf_op jit(solution)/shard_map/feed_forward/pallas_call | solution.py:1523
  194.1 0.0 copy-done.3
  194.1 0.0 copy-start.4
  194.2 6.1 %fusion.3 = bf16[1152,1536]{1,0:T(8,128)(2,1)S(1)} fusion(bf16[1152,1024]{1,0:T(8,128)(2,1)} %get-tuple-element.65, bf16[1024,1536]{1,0:T(8,128)(2,1)S(1)} %copy-done.3), kind=kOutput, calls=%fused_computation.10 | convolution fusion | flops 3623878656 | bytes 9043968 | tf_op jit(solution)/shard_map/dot_general | solution.py:38
  200.2 0.0 copy-start.2
  200.3 0.2 fusion
  200.5 0.0 copy-done.4
  200.5 1.6 copy-done.2
  202.1 9.2 %fusion.2 = bf16[2304,1536]{1,0:T(8,128)(2,1)} fusion(bf16[2304,1024]{1,0:T(8,128)(2,1)S(1)} %copy-done.4, bf16[1024,1536]{1,0:T(8,128)(2,1)S(1)} %copy-done.2), kind=kOutput, calls=%fused_computation.9 | convolution fusion | flops 7247757312 | bytes 14942208 | tf_op jit(solution)/shard_map/dot_general | solution.py:38
  211.3 2.1 pad_maximum_fusion
  213.4 165.2 %backward_section.1 = (bf16[256,1536]{1,0:T(8,128)(2,1)}, f32[256,1536]{1,0:T(8,128)}, f32[2,1536]{1,0:T(2,128)}, f32[288,1536]{1,0:T(8,128)}, f32[288,768]{1,0:...) custom-call(bf16[256,1536]{1,0:T(8,128)(2,1)} %tokens.3, ...), custom_call_target="tpu_custom_call" | custom-call | tf_op jit(solution)/shard_map/backward_section/pallas_call | solution.py:1418
  378.6 0.8 slice_reduce_fusion.1
  379.4 0.1 reshape_squeeze.6
  379.4 0.1 reshape_squeeze.7
  379.5 0.7 pad_maximum_fusion.1
  380.2 5.5 %all-to-all-start = ((f32[32,1,96]{2,1,0:T(1,128)}), f32[32,1,96]{2,1,0:T(1,128)S(1)}, u32[]{:S(2)}, u32[]{:S(2)}) async-start(f32[32,1,96]{2,1,0:T(1,128)} %bitcast.12), calls=%async_computation | async-start | bytes 32768 | tf_op jit(solution)/shard_map/all_to_all | solution.py:1899
  385.8 3.2 update.5
  388.9 6.2 %update.7 = (f32[24,96,96]{2,1,0:T(8,128)}, f32[24,96,96]{2,1,0:T(8,128)}, f32[24,96,96]{2,1,0:T(8,128)}) custom-call(f32[24,96,96]{2,1,0:T(8,128)} %w_ref.7, f32[288,768]{1,0:T(8,128)} %get-tuple-element.92.g_ref, f32[24,96,96]{2,1,0:T(8,128)} %l_ref.7, f32[24,96,96]{2,1,0:T(8,128)} %r_ref.7, f32[24,96,96]{2,1,0:T(8,128)} %lr_ref.7, f32[24,96,96]{2,1,0:T(8,128)} %rr_ref.7), custom_call_target="tpu_custom_call" | custom-call | flops 3221225472 | bytes 10616832 | tf_op jit(solution)/shard_map/update/pallas_call | solution.py:1583
  395.2 9.4 %update.6 = (f32[48,96,96]{2,1,0:T(8,128)}, f32[48,96,96]{2,1,0:T(8,128)}, f32[48,96,96]{2,1,0:T(8,128)}) custom-call(f32[48,96,96]{2,1,0:T(8,128)} %w_ref.6, f32[288,1536]{1,0:T(8,128)} %get-tuple-element.88.g_ref, f32[48,96,96]{2,1,0:T(8,128)} %l_ref.6, f32[48,96,96]{2,1,0:T(8,128)} %r_ref.6, f32[48,96,96]{2,1,0:T(8,128)} %lr_ref.6, f32[48,96,96]{2,1,0:T(8,128)} %rr_ref.6), custom_call_target="tpu_custom_call" | custom-call | flops 6442450944 | bytes 21233664 | tf_op jit(solution)/shard_map/update/pallas_call | solution.py:1583
  404.6 0.0 copy-start.1
  404.6 0.0 copy-start
  404.6 3.7 update.4
  408.3 0.0 all-to-all-done
  408.3 0.1 reduce_sum.9
  408.4 0.6 fusion.1
  408.9 0.0 copy-done.1
  408.9 0.9 copy.48
  409.8 0.0 copy-done
  409.8 1.1 copy.49
Async XLA Ops:
  157.4 36.7 %copy-start.3 = (bf16[1024,1536]{1,0:T(8,128)(2,1)S(1)}, bf16[1024,1536]{1,0:T(8,128)(2,1)}, u32[]{:S(2)}) copy-start(bf16[1024,1536]{1,0:T(8,128)(2,1)} %get-tuple-element.59.cotangent) | copy-start | bytes 9437188
  194.1 6.3 %copy-start.4 = (bf16[2304,1024]{1,0:T(8,128)(2,1)S(1)}, bf16[2304,1024]{1,0:T(8,128)(2,1)}, u32[]{:S(2)}) copy-start(bf16[2304,1024]{1,0:T(8,128)(2,1)} %get-tuple-element.64) | copy-start | bytes 14155780
  200.2 1.9 copy-start.2
  380.2 28.1 %all-to-all-start = ((f32[32,1,96]{2,1,0:T(1,128)}), f32[32,1,96]{2,1,0:T(1,128)S(1)}, u32[]{:S(2)}, u32[]{:S(2)}) async-start(f32[32,1,96]{2,1,0:T(1,128)} %bitcast.12), calls=%async_computation | async-start | bytes 32768 | tf_op jit(solution)/shard_map/all_to_all | solution.py:1899
  404.6 4.3 %copy-start.1 = (bf16[256,1536]{1,0:T(8,128)(2,1)S(1)}, bf16[256,1536]{1,0:T(8,128)(2,1)}, u32[]{:S(2)}) copy-start(bf16[256,1536]{1,0:T(8,128)(2,1)} %get-tuple-element.118) | copy-start | bytes 2359300
  404.6 5.2 %copy-start = (f32[256,1536]{1,0:T(8,128)S(1)}, f32[256,1536]{1,0:T(8,128)}, u32[]{:S(2)}) copy-start(f32[256,1536]{1,0:T(8,128)} %get-tuple-element.119) | copy-start | bytes 4718596

commit v7 on v6

--- a/solution.py
+++ b/solution.py
@@ -1509,7 +1509,7 @@
 
         return carry
 
-    lax.fori_loop(0, units // tile, step, 0)
+    lax.fori_loop(0, units // tile, step, 0, unroll=True)
     normed_part[...] = normed_sum[...].astype(low)
     ffn_part[...] = ffn_sum[...].astype(low)
 

time: 416 us -> 415 us (level)
  Pallas kernels: 380 us -> 375 us
    pallas_call x1, Pallas kernels: 36.7 us -> 32.2 us  [feed_forward(): pl.pallas_call(ffn_kernel, grid=(group // size,), in_specs=[rows, rows, p...]
  transfers between devices with their start and end apart: 1 -> 1, of which waited for: 0 -> 0; matrix products, arithmetic and copies ran while one was open for 0% -> 0% of each run, Pallas kernels for 5% -> 6%
where the time goes in v7:
time: 415 us; the launch traced here: 407 us
  Pallas kernels  375 us (90%)
  matrix products  15.3 us (4%)
  starting transfers between devices  5.54 us (1%)
  local copies, waits for them, and re-layouts  5.46 us (1%)
    pallas_call x1, Pallas kernels, backward_section(): pl.pallas_call(functools.partial(backward_kernel, count), in_specs=[vmem]...  165 us
    pallas_call x1, Pallas kernels, forward_section(): pl.pallas_call(functools.partial(forward_kernel, count), in_specs=[vmem]...  155 us
    pallas_call x1, Pallas kernels, feed_forward(): pl.pallas_call(ffn_kernel, grid=(group // size,), in_specs=[rows, rows, p...  32.2 us
    pallas_call x4, Pallas kernels, update(): pl.pallas_call(functools.partial(update_kernel, rate, turned), grid=(coun...  22.5 us
    dot_general x2, matrix products, mul(): return lax.dot_general(a, b, dims, preferred_element_type=kind)  15.3 us
  transfers between devices with their start and end apart: 1, of which 0 were waited for; matrix products, arithmetic and copies ran while one was open for 0% of the time, Pallas kernels for 6%

profile of v7, /device:TPU:0, one launch (start us, length us, event | category | flops | bytes accessed | tf_op | source)
XLA Modules:
  0.0 406.9 jit_solution(16249218125695217543)
XLA Ops:
  0.6 1.3 select_maximum_fusion.own_gains
  1.9 155.5 %forward_section.1 = (f32[2,1536]{1,0:T(2,128)}, f32[256,1536]{1,0:T(8,128)}, bf16[1024,1536]{1,0:T(8,128)(2,1)}, bf16[1024,1536]{1,0:T(8,128)(2,1)}, bf16[8,288...) custom-call(bf16[256,1536]{1,0:T(8,128)(2,1)} %tokens.3, ...), custom_call_target="tpu_custom_call" | custom-call | tf_op jit(solution)/shard_map/forward_section/pallas_call | solution.py:822
  157.4 0.0 copy-start.3
  157.4 32.2 %feed_forward.1 = (bf16[1152,1024]{1,0:T(8,128)(2,1)}, bf16[2304,1024]{1,0:T(8,128)(2,1)}, bf16[1024,1536]{1,0:T(8,128)(2,1)}, bf16[1024,1536]{1,0:T(8,128)(2,1)}) custom-call(bf16[1024,1536]{1,0:T(8,128)(2,1)} %get-tuple-element.58.normed, bf16[1024,1536]{1,0:T(8,128)(2,1)} %get-tuple-element.59.cotangent, bf16[2304,1536]{1,0:T(8,128)(2,1)} %bitcast.27, ...), custom_call_target="tpu_custom_call" | custom-call | flops 21743271936 | bytes 41943040 | tf_op jit(solution)/shard_map/feed_forward/pallas_call | solution.py:1523
  189.6 0.0 copy-done.3
  189.6 0.0 copy-start.4
  189.7 5.9 %fusion.3 = bf16[1152,1536]{1,0:T(8,128)(2,1)S(1)} fusion(bf16[1152,1024]{1,0:T(8,128)(2,1)} %get-tuple-element.65, bf16[1024,1536]{1,0:T(8,128)(2,1)S(1)} %copy-done.3), kind=kOutput, calls=%fused_computation.10 | convolution fusion | flops 3623878656 | bytes 9043968 | tf_op jit(solution)/shard_map/dot_general | solution.py:38
  195.5 0.0 copy-start.2
  195.5 0.2 fusion
  195.8 0.0 copy-done.4
  195.8 1.6 copy-done.2
  197.4 9.4 %fusion.2 = bf16[2304,1536]{1,0:T(8,128)(2,1)} fusion(bf16[2304,1024]{1,0:T(8,128)(2,1)S(1)} %copy-done.4, bf16[1024,1536]{1,0:T(8,128)(2,1)S(1)} %copy-done.2), kind=kOutput, calls=%fused_computation.9 | convolution fusion | flops 7247757312 | bytes 14942208 | tf_op jit(solution)/shard_map/dot_general | solution.py:38
  206.8 2.1 pad_maximum_fusion
  208.9 165.2 %backward_section.1 = (bf16[256,1536]{1,0:T(8,128)(2,1)}, f32[256,1536]{1,0:T(8,128)}, f32[2,1536]{1,0:T(2,128)}, f32[288,1536]{1,0:T(8,128)}, f32[288,768]{1,0:...) custom-call(bf16[256,1536]{1,0:T(8,128)(2,1)} %tokens.3, ...), custom_call_target="tpu_custom_call" | custom-call | tf_op jit(solution)/shard_map/backward_section/pallas_call | solution.py:1418
  374.0 0.8 slice_reduce_fusion.1
  374.9 0.1 reshape_squeeze.6
  374.9 0.1 reshape_squeeze.7
  375.0 0.7 pad_maximum_fusion.1
  375.7 5.5 %all-to-all-start = ((f32[32,1,96]{2,1,0:T(1,128)}), f32[32,1,96]{2,1,0:T(1,128)S(1)}, u32[]{:S(2)}, u32[]{:S(2)}) async-start(f32[32,1,96]{2,1,0:T(1,128)} %bitcast.12), calls=%async_computation | async-start | bytes 32768 | tf_op jit(solution)/shard_map/all_to_all | solution.py:1899
  381.3 3.2 update.5
  384.4 6.2 %update.7 = (f32[24,96,96]{2,1,0:T(8,128)}, f32[24,96,96]{2,1,0:T(8,128)}, f32[24,96,96]{2,1,0:T(8,128)}) custom-call(f32[24,96,96]{2,1,0:T(8,128)} %w_ref.7, f32[288,768]{1,0:T(8,128)} %get-tuple-element.92.g_ref, f32[24,96,96]{2,1,0:T(8,128)} %l_ref.7, f32[24,96,96]{2,1,0:T(8,128)} %r_ref.7, f32[24,96,96]{2,1,0:T(8,128)} %lr_ref.7, f32[24,96,96]{2,1,0:T(8,128)} %rr_ref.7), custom_call_target="tpu_custom_call" | custom-call | flops 3221225472 | bytes 10616832 | tf_op jit(solution)/shard_map/update/pallas_call | solution.py:1583
  390.7 9.4 %update.6 = (f32[48,96,96]{2,1,0:T(8,128)}, f32[48,96,96]{2,1,0:T(8,128)}, f32[48,96,96]{2,1,0:T(8,128)}) custom-call(f32[48,96,96]{2,1,0:T(8,128)} %w_ref.6, f32[288,1536]{1,0:T(8,128)} %get-tuple-element.88.g_ref, f32[48,96,96]{2,1,0:T(8,128)} %l_ref.6, f32[48,96,96]{2,1,0:T(8,128)} %r_ref.6, f32[48,96,96]{2,1,0:T(8,128)} %lr_ref.6, f32[48,96,96]{2,1,0:T(8,128)} %rr_ref.6), custom_call_target="tpu_custom_call" | custom-call | flops 6442450944 | bytes 21233664 | tf_op jit(solution)/shard_map/update/pallas_call | solution.py:1583
  400.1 0.0 copy-start.1
  400.1 0.0 copy-start
  400.1 3.7 update.4
  403.8 0.0 all-to-all-done
  403.8 0.1 reduce_sum.9
  403.8 0.6 fusion.1
  404.4 0.0 copy-done.1
  404.4 0.9 copy.48
  405.3 0.0 copy-done
  405.3 1.1 copy.49
Async XLA Ops:
  157.4 32.2 %copy-start.3 = (bf16[1024,1536]{1,0:T(8,128)(2,1)S(1)}, bf16[1024,1536]{1,0:T(8,128)(2,1)}, u32[]{:S(2)}) copy-start(bf16[1024,1536]{1,0:T(8,128)(2,1)} %get-tuple-element.59.cotangent) | copy-start | bytes 9437188
  189.6 6.1 %copy-start.4 = (bf16[2304,1024]{1,0:T(8,128)(2,1)S(1)}, bf16[2304,1024]{1,0:T(8,128)(2,1)}, u32[]{:S(2)}) copy-start(bf16[2304,1024]{1,0:T(8,128)(2,1)} %get-tuple-element.64) | copy-start | bytes 14155780
  195.5 1.9 copy-start.2
  375.7 28.1 %all-to-all-start = ((f32[32,1,96]{2,1,0:T(1,128)}), f32[32,1,96]{2,1,0:T(1,128)S(1)}, u32[]{:S(2)}, u32[]{:S(2)}) async-start(f32[32,1,96]{2,1,0:T(1,128)} %bitcast.12), calls=%async_computation | async-start | bytes 32768 | tf_op jit(solution)/shard_map/all_to_all | solution.py:1899
  400.1 4.3 %copy-start.1 = (bf16[256,1536]{1,0:T(8,128)(2,1)S(1)}, bf16[256,1536]{1,0:T(8,128)(2,1)}, u32[]{:S(2)}) copy-start(bf16[256,1536]{1,0:T(8,128)(2,1)} %get-tuple-element.118) | copy-start | bytes 2359300
  400.1 5.2 %copy-start = (f32[256,1536]{1,0:T(8,128)S(1)}, f32[256,1536]{1,0:T(8,128)}, u32[]{:S(2)}) copy-start(f32[256,1536]{1,0:T(8,128)} %get-tuple-element.119) | copy-start | bytes 4718596

commit v8 on v7

--- a/solution.py
+++ b/solution.py
@@ -1347,7 +1347,6 @@
         send(21 + i, kv_mate.at[2, quarter(i), mine], kv_mate.at[3, quarter(i ^ 2), mine], across)
     out_ring.step(1)
     gateup_ring.step(3)
-    down_ring.step(3)
     swapped_arrived(9, all_grad, lanes(across_head), 2, across)
     swapped(25, all_grad, lanes(across_head), 1, mate)
     swapped_arrived(13, all_grad, lanes(mate_head), 1, mate)
@@ -1364,6 +1363,7 @@
         at = slice(i * (QKV // 2), (i + 1) * (QKV // 2))
         qkv_local[:, at] = mul(features[...], all_grad[:, at], TN).astype(low)
     qkv_ring.start()
+    down_ring.step(3)
     for i, where in ((2, across), (3, corner), (1, mate)):
         feature_grad[quarter(i), :] = mul(all_grad[quarter(i), :], qkv_rows[...], NT).astype(low)
         send(28 + i, feature_grad.at[quarter(i)], normed_grad.at[:, lanes(head)], where)

time: 415 us -> 413 us (level)
  no operation moved by 1% of the time
where the time goes in v8:
time: 413 us; the launch traced here: 405 us
  Pallas kernels  374 us (91%)
  matrix products  15.3 us (4%)
  local copies, waits for them, and re-layouts  5.46 us (1%)
  starting transfers between devices  5.25 us (1%)
    pallas_call x1, Pallas kernels, backward_section(): pl.pallas_call(functools.partial(backward_kernel, count), in_specs=[vmem]...  164 us
    pallas_call x1, Pallas kernels, forward_section(): pl.pallas_call(functools.partial(forward_kernel, count), in_specs=[vmem]...  155 us
    pallas_call x1, Pallas kernels, feed_forward(): pl.pallas_call(ffn_kernel, grid=(group // size,), in_specs=[rows, rows, p...  32.2 us
    pallas_call x4, Pallas kernels, update(): pl.pallas_call(functools.partial(update_kernel, rate, turned), grid=(coun...  22.5 us
    dot_general x2, matrix products, mul(): return lax.dot_general(a, b, dims, preferred_element_type=kind)  15.3 us
  transfers between devices with their start and end apart: 1, of which 0 were waited for; matrix products, arithmetic and copies ran while one was open for 0% of the time, Pallas kernels for 6%

profile of v8, /device:TPU:0, one launch (start us, length us, event | category | flops | bytes accessed | tf_op | source)
XLA Modules:
  0.0 405.4 jit_solution(12272190764034828886)
XLA Ops:
  0.6 1.3 select_maximum_fusion.own_gains
  1.9 155.5 %forward_section.1 = (f32[2,1536]{1,0:T(2,128)}, f32[256,1536]{1,0:T(8,128)}, bf16[1024,1536]{1,0:T(8,128)(2,1)}, bf16[1024,1536]{1,0:T(8,128)(2,1)}, bf16[8,288...) custom-call(bf16[256,1536]{1,0:T(8,128)(2,1)} %tokens.3, ...), custom_call_target="tpu_custom_call" | custom-call | tf_op jit(solution)/shard_map/forward_section/pallas_call | solution.py:822
  157.4 0.0 copy-start.3
  157.4 32.2 %feed_forward.1 = (bf16[1152,1024]{1,0:T(8,128)(2,1)}, bf16[2304,1024]{1,0:T(8,128)(2,1)}, bf16[1024,1536]{1,0:T(8,128)(2,1)}, bf16[1024,1536]{1,0:T(8,128)(2,1)}) custom-call(bf16[1024,1536]{1,0:T(8,128)(2,1)} %get-tuple-element.58.normed, bf16[1024,1536]{1,0:T(8,128)(2,1)} %get-tuple-element.59.cotangent, bf16[2304,1536]{1,0:T(8,128)(2,1)} %bitcast.27, ...), custom_call_target="tpu_custom_call" | custom-call | flops 21743271936 | bytes 41943040 | tf_op jit(solution)/shard_map/feed_forward/pallas_call | solution.py:1523
  189.6 0.0 copy-done.3
  189.6 0.0 copy-start.4
  189.7 5.9 %fusion.3 = bf16[1152,1536]{1,0:T(8,128)(2,1)S(1)} fusion(bf16[1152,1024]{1,0:T(8,128)(2,1)} %get-tuple-element.65, bf16[1024,1536]{1,0:T(8,128)(2,1)S(1)} %copy-done.3), kind=kOutput, calls=%fused_computation.10 | convolution fusion | flops 3623878656 | bytes 9043968 | tf_op jit(solution)/shard_map/dot_general | solution.py:38
  195.5 0.0 copy-start.2
  195.5 0.2 fusion
  195.8 0.0 copy-done.4
  195.8 1.6 copy-done.2
  197.4 9.4 %fusion.2 = bf16[2304,1536]{1,0:T(8,128)(2,1)} fusion(bf16[2304,1024]{1,0:T(8,128)(2,1)S(1)} %copy-done.4, bf16[1024,1536]{1,0:T(8,128)(2,1)S(1)} %copy-done.2), kind=kOutput, calls=%fused_computation.9 | convolution fusion | flops 7247757312 | bytes 14942208 | tf_op jit(solution)/shard_map/dot_general | solution.py:38
  206.8 2.1 pad_maximum_fusion
  208.9 164.0 %backward_section.1 = (bf16[256,1536]{1,0:T(8,128)(2,1)}, f32[256,1536]{1,0:T(8,128)}, f32[2,1536]{1,0:T(2,128)}, f32[288,1536]{1,0:T(8,128)}, f32[288,768]{1,0:...) custom-call(bf16[256,1536]{1,0:T(8,128)(2,1)} %tokens.3, ...), custom_call_target="tpu_custom_call" | custom-call | tf_op jit(solution)/shard_map/backward_section/pallas_call | solution.py:1418
  372.9 0.8 slice_reduce_fusion.1
  373.7 0.1 reshape_squeeze.6
  373.8 0.1 reshape_squeeze.7
  373.8 0.7 pad_maximum_fusion.1
  374.5 5.3 %all-to-all-start = ((f32[32,1,96]{2,1,0:T(1,128)}), f32[32,1,96]{2,1,0:T(1,128)S(1)}, u32[]{:S(2)}, u32[]{:S(2)}) async-start(f32[32,1,96]{2,1,0:T(1,128)} %bitcast.12), calls=%async_computation | async-start | bytes 32768 | tf_op jit(solution)/shard_map/all_to_all | solution.py:1899
  379.8 3.2 update.5
  383.0 6.2 %update.7 = (f32[24,96,96]{2,1,0:T(8,128)}, f32[24,96,96]{2,1,0:T(8,128)}, f32[24,96,96]{2,1,0:T(8,128)}) custom-call(f32[24,96,96]{2,1,0:T(8,128)} %w_ref.7, f32[288,768]{1,0:T(8,128)} %get-tuple-element.92.g_ref, f32[24,96,96]{2,1,0:T(8,128)} %l_ref.7, f32[24,96,96]{2,1,0:T(8,128)} %r_ref.7, f32[24,96,96]{2,1,0:T(8,128)} %lr_ref.7, f32[24,96,96]{2,1,0:T(8,128)} %rr_ref.7), custom_call_target="tpu_custom_call" | custom-call | flops 3221225472 | bytes 10616832 | tf_op jit(solution)/shard_map/update/pallas_call | solution.py:1583
  389.2 9.4 %update.6 = (f32[48,96,96]{2,1,0:T(8,128)}, f32[48,96,96]{2,1,0:T(8,128)}, f32[48,96,96]{2,1,0:T(8,128)}) custom-call(f32[48,96,96]{2,1,0:T(8,128)} %w_ref.6, f32[288,1536]{1,0:T(8,128)} %get-tuple-element.88.g_ref, f32[48,96,96]{2,1,0:T(8,128)} %l_ref.6, f32[48,96,96]{2,1,0:T(8,128)} %r_ref.6, f32[48,96,96]{2,1,0:T(8,128)} %lr_ref.6, f32[48,96,96]{2,1,0:T(8,128)} %rr_ref.6), custom_call_target="tpu_custom_call" | custom-call | flops 6442450944 | bytes 21233664 | tf_op jit(solution)/shard_map/update/pallas_call | solution.py:1583
  398.6 0.0 copy-start.1
  398.6 0.0 copy-start
  398.6 3.7 update.4
  402.3 0.0 all-to-all-done
  402.3 0.1 reduce_sum.9
  402.4 0.6 fusion.1
  403.0 0.0 copy-done.1
  403.0 0.9 copy.48
  403.8 0.0 copy-done
  403.8 1.1 copy.49
Async XLA Ops:
  157.4 32.2 %copy-start.3 = (bf16[1024,1536]{1,0:T(8,128)(2,1)S(1)}, bf16[1024,1536]{1,0:T(8,128)(2,1)}, u32[]{:S(2)}) copy-start(bf16[1024,1536]{1,0:T(8,128)(2,1)} %get-tuple-element.59.cotangent) | copy-start | bytes 9437188
  189.6 6.1 %copy-start.4 = (bf16[2304,1024]{1,0:T(8,128)(2,1)S(1)}, bf16[2304,1024]{1,0:T(8,128)(2,1)}, u32[]{:S(2)}) copy-start(bf16[2304,1024]{1,0:T(8,128)(2,1)} %get-tuple-element.64) | copy-start | bytes 14155780
  195.5 1.9 copy-start.2
  374.5 27.8 %all-to-all-start = ((f32[32,1,96]{2,1,0:T(1,128)}), f32[32,1,96]{2,1,0:T(1,128)S(1)}, u32[]{:S(2)}, u32[]{:S(2)}) async-start(f32[32,1,96]{2,1,0:T(1,128)} %bitcast.12), calls=%async_computation | async-start | bytes 32768 | tf_op jit(solution)/shard_map/all_to_all | solution.py:1899
  398.6 4.3 %copy-start.1 = (bf16[256,1536]{1,0:T(8,128)(2,1)S(1)}, bf16[256,1536]{1,0:T(8,128)(2,1)}, u32[]{:S(2)}) copy-start(bf16[256,1536]{1,0:T(8,128)(2,1)} %get-tuple-element.118) | copy-start | bytes 2359300
  398.6 5.2 %copy-start = (f32[256,1536]{1,0:T(8,128)S(1)}, f32[256,1536]{1,0:T(8,128)}, u32[]{:S(2)}) copy-start(f32[256,1536]{1,0:T(8,128)} %get-tuple-element.119) | copy-start | bytes 4718596
